TPU v7x, 32 devices: a whole 2x2x4 slice. The times are simulated.
32 devices in a mesh: scan: 8 (over z, y), mode: 4 (over x, core).
Axes of the slice: x: 2, y: 2, z: 4, core: 2. Of those that a mesh axis runs over, the one named last changes fastest.
Arguments:
- object_field: float32 [2, 512, 1024], P(None, 'scan', 'mode'), may hold values from -6 to 6
- probe: float32 [4, 2, 128, 128], P('mode'), may hold values from -6 to 6
- amplitude: float32 [64, 128, 128], P(('scan', 'mode')), may hold values from 0.5 to 8
- offsets: int32 [64, 2], P(('scan', 'mode')), may hold values from 0 to 1023, as said below
- counts: int32 [32], P(('scan', 'mode')), may hold values from 1 to 2, as said below
Outputs:
- object_out: float32 [2, 512, 1024], P(None, 'scan', 'mode')
- probe_out: float32 [4, 2, 128, 128], P('mode')
Inputs may be any that keep to these rules, and one draw needn't show every extreme that they name: `offsets`: slot i belongs to the device of index i // 2 along scan+mode, with scan index s and mode index m; its top row lies in s * 64 to s * 64 + 63 and its left column in m * 256 to m * 256 + 255. `counts`: entry d is how many of the first slots of device d are used; some device uses all 2.
All inputs are finite; a program needn't handle non-finite values.
Results may differ from a plain program's by a relative error of at most 0.0001.
Values sent between devices are 32-bit elements; how exact they have to be, the bound alone decides.
No kernel may reach another device: no remote copies, remote signals or barrier semaphores. Data moves between devices by JAX's collectives and lax.ppermute only.
A program may use at most 64 MiB of HBM per device.

v0:
```python
import math

import jax
import jax.numpy as jnp
from jax import lax
from jax.sharding import PartitionSpec as P

ITERS = 2


def passed_along(value, axis, steps):
    count = lax.axis_size(axis)
    initial, last = (max(0, -steps), min(count, count - steps))
    return lax.ppermute(value, axis, [(source, source + steps) for source in range(initial, last)])


def fresnel_table(length):
    pixel_ids = jnp.arange(length, dtype=jnp.int32)
    phase_grid = pixel_ids[:, None] * pixel_ids[None, :] % length
    centred = pixel_ids - length // 2
    chirp = centred * centred % (4 * length)
    angle_table = -2.0 * math.pi / length * phase_grid.astype(jnp.float32) + math.pi / (
        2 * length
    ) * chirp[None, :].astype(jnp.float32)
    factor = 1.0 / math.sqrt(length)
    return (jnp.cos(angle_table) * factor, jnp.sin(angle_table) * factor)


def product(form, first, second):
    return jnp.einsum(form, first, second, precision=lax.Precision.HIGHEST)


def wave_terms(object_patch, probes, amplitude_row, kern_re, kern_im):
    probe_re = probes[:, 0]
    probe_im = probes[:, 1]
    object_re = object_patch[0]
    object_im = object_patch[1]
    exit_re = probe_re * object_re - probe_im * object_im
    exit_im = probe_re * object_im + probe_im * object_re
    left_re = product("ux,kxy->kuy", kern_re, exit_re) - product("ux,kxy->kuy", kern_im, exit_im)
    left_im = product("ux,kxy->kuy", kern_re, exit_im) + product("ux,kxy->kuy", kern_im, exit_re)
    far_re = product("kuy,vy->kuv", left_re, kern_re) - product("kuy,vy->kuv", left_im, kern_im)
    far_im = product("kuy,vy->kuv", left_re, kern_im) + product("kuy,vy->kuv", left_im, kern_re)
    intensity = jnp.sum(far_re * far_re + far_im * far_im, axis=0)
    factor = amplitude_row / jnp.sqrt(jnp.maximum(intensity, 1.0))
    fixed_re = far_re * factor
    fixed_im = far_im * factor
    back_re = product("ux,kuy->kxy", kern_re, fixed_re) + product("ux,kuy->kxy", kern_im, fixed_im)
    back_im = product("ux,kuy->kxy", kern_re, fixed_im) - product("ux,kuy->kxy", kern_im, fixed_re)
    near_re = product("kxv,vy->kxy", back_re, kern_re) + product("kxv,vy->kxy", back_im, kern_im)
    near_im = product("kxv,vy->kxy", back_im, kern_re) - product("kxv,vy->kxy", back_re, kern_im)
    change_re = near_re - exit_re
    change_im = near_im - exit_im
    numerator = jnp.stack(
        [
            jnp.sum(probe_re * change_re + probe_im * change_im, axis=0),
            jnp.sum(probe_re * change_im - probe_im * change_re, axis=0),
            jnp.sum(probe_re * probe_re + probe_im * probe_im, axis=0),
        ]
    )
    gradient = jnp.stack(
        [
            object_re * change_re + object_im * change_im,
            object_re * change_im - object_im * change_re,
        ],
        axis=1,
    )
    density = object_re * object_re + object_im * object_im
    return (numerator, gradient, density)


def local(object_field, probe, amplitude, offsets, counts):
    tile_rows = object_field.shape[1]
    band_cols = object_field.shape[2]
    length = probe.shape[2]
    slot_count = amplitude.shape[0]
    reach_tiles = -(-length // tile_rows)
    kern_re, kern_im = fresnel_table(length)
    start_zero = jnp.zeros((), jnp.int32)
    for iteration in range(ITERS):
        probes = lax.all_gather(probe, "mode", axis=0, tiled=True)
        pieces = [object_field]
        for shift_step in range(1, reach_tiles + 1):
            height = min(tile_rows, length - (shift_step - 1) * tile_rows)
            pieces.append(passed_along(object_field, "scan", -shift_step))
        extended_rows = jnp.concatenate(pieces, axis=1)
        beside = passed_along(extended_rows[:, :, :length], "mode", -1)
        extended = jnp.concatenate([extended_rows, beside], axis=2)

        def add_position(slot, state_carry):
            sums, gradient, density = state_carry
            row_start = offsets[slot, 0] % tile_rows
            col_start = offsets[slot, 1] % band_cols
            object_patch = lax.dynamic_slice(
                extended, (start_zero, row_start, col_start), (2, length, length)
            )
            numerator, grad_term, dens_term = wave_terms(
                object_patch, probes, amplitude[slot], kern_re, kern_im
            )
            used = (slot < counts[0]).astype(jnp.float32)
            current = lax.dynamic_slice(
                sums, (start_zero, row_start, col_start), (3, length, length)
            )
            sums = lax.dynamic_update_slice(
                sums, current + used * numerator, (start_zero, row_start, col_start)
            )
            return (sums, gradient + used * grad_term, density + used * dens_term)

        initial = (
            jnp.zeros((3, tile_rows + length, band_cols + length), jnp.float32),
            jnp.zeros(probes.shape, jnp.float32),
            jnp.zeros((length, length), jnp.float32),
        )
        sums, gradient, density = lax.fori_loop(0, slot_count, add_position, initial)
        margin = passed_along(sums[:, :, band_cols:], "mode", 1)
        folded = sums[:, :, :band_cols].at[:, :, :length].add(margin)
        own_block = folded[:, :tile_rows, :]
        for shift_step in range(1, reach_tiles + 1):
            height = min(tile_rows, length - (shift_step - 1) * tile_rows)
            first_row = shift_step * tile_rows
            arrived = passed_along(folded[:, first_row : first_row + height, :], "scan", shift_step)
            own_block = own_block.at[:, :height, :].add(arrived)
        object_new = object_field + own_block[:2] / (own_block[2:3] + 1.0)
        summed_grad, summed_density = lax.psum((gradient, density), ("scan", "mode"))
        own_grad = lax.dynamic_slice_in_dim(summed_grad, lax.axis_index("mode"), 1, 0)
        probe = probe + own_grad / (summed_density + 1.0)
        object_field = object_new
    return (object_field, probe)


def solution(mesh):
    placed = (
        P(None, "scan", "mode"),
        P("mode", None, None, None),
        P(("scan", "mode"), None, None),
        P(("scan", "mode"), None),
        P(("scan", "mode")),
    )
    return jax.shard_map(
        local,
        mesh=mesh,
        in_specs=placed,
        out_specs=(P(None, "scan", "mode"), P("mode", None, None, None)),
        check_vma=False,
    )
```

profile of v0, /device:TPU:0, one launch (start us, length us, event | category | flops | bytes accessed | tf_op | source)
XLA Modules:
  0.0 413.4 jit_solution(16391768953870138634)
XLA Ops:
  7.2 1.3 collective-permute-start
  8.5 1.3 collective-permute-start.1
  9.8 9.0 %all_gather.6 = f32[4,2,128,128]{3,2,0,1:T(8,128)S(1)} all-gather(f32[1,2,128,128]{3,2,0,1:T(8,128)} %bitcast.403), channel_id=1, replica_groups=mesh['scan'=8,'mode'=4] {'mode'}, dimensions={0}, use_global_device_ids=true | all-gather | bytes 655360 | tf_op jit(solution)/shard_map/all_gather | solution.py:81
  18.8 0.9 collective-permute-done.1
  19.8 1.3 collective-permute-start.2
  21.2 2.0 collective-permute-done.2
  24.1 39.4 %while.58 = (s32[]{:T(128)}, f32[3,192,384]{2,1,0:T(8,128)S(1)}, f32[4,2,128,128]{3,2,0,1:T(8,128)S(1)}, f32[128,128]{1,0:T(8,128)S(1)}, s32[2,2]{1,0:T(2,128)S(...) while((s32[]{:T(128)}, f32[3,192,384]{2,1,0:T(8,128)S(1)}, ...), condition=%wide.region_5.6_spmd.clone.clone.clone.clone, body=%wide.region_1.0_spmd.clone.clone.clone.clone.sunk | while | flops 1618100224 | bytes 17244724 | solution.py:114
  41.4 1.7 dynamic_update_slice.32
  60.4 2.8 dynamic_update_slice.32
  64.1 6.5 %collective-permute-start.3 = (f32[3,192,128]{2,1,0:T(8,128)S(1)}, f32[3,192,128]{2,1,0:T(8,128)S(1)}, u32[]{:S(2)}, u32[]{:S(2)}) collective-permute-start(f32[3,192,128]{2,1,0:T(8,128)S(1)} %slice.279), channel_id=1, source_target_pairs={{0,1},{1,2},{2,3},{4,5},{5,6},{6,7},{8,9},{9,10},{10,11},{12,13},{... | collective-permute-start | bytes 884744 | tf_op jit(solution)/shard_map/ppermute | solution.py:14
  71.9 3.9 collective-permute-start.4
  75.8 4.8 %collective-permute-start.5 = (f32[3,64,256]{2,1,0:T(8,128)S(1)}, f32[3,64,256]{2,1,0:T(8,128)S(1)}, u32[]{:S(2)}, u32[]{:S(2)}) collective-permute-start(f32[3,64,256]{2,1,0:T(8,128)S(1)} %get-tuple-element.1219), channel_id=1, source_target_pairs={{0,8},{4,12},{8,16},{12,20},{16,24},{20,28},{1,9},{5,13},{9,17},{1... | collective-permute-start | bytes 589832 | tf_op jit(solution)/shard_map/ppermute | solution.py:14
  80.6 121.1 %all-reduce.7.cloned.1.call-done = (f32[4,2,128,128]{3,2,1,0:T(8,128)}, f32[128,128]{1,0:T(8,128)}) async-done(((f32[4,2,128,128]{3,2,1,0:T(8,128)}, f32[128,128]{1,0:T(8,128)}), (f32[4,2,128,128]{3,2,1,0:T(8,128)}, f32[128,128]{1,0:T(8,128)})) %all-reduce.7.cloned.1.call-update) | async-done | bytes 589840 | tf_op jit(solution)/shard_map/psum | solution.py:124
  201.6 0.8 broadcast_add_fusion.1
  202.6 0.9 copy-done.8
  203.5 1.4 collective-permute-start.6
  204.9 1.3 collective-permute-start.7
  206.2 0.9 divide_add_fusion.1
  207.2 4.1 collective-permute-done.6
  211.2 3.7 collective-permute-done.7
  214.9 1.3 collective-permute-start.8
  216.2 9.0 %all_gather.7 = f32[4,2,128,128]{3,2,1,0:T(8,128)S(1)} all-gather(f32[1,2,128,128]{3,2,1,0:T(8,128)S(1)} %divide_add_fusion.1), channel_id=1, replica_groups=mesh['scan'=8,'mode'=4] {'mode'}, dimensions={0}, use_global_device_ids=true | all-gather | bytes 655360 | tf_op jit(solution)/shard_map/all_gather | solution.py:81
  225.5 39.5 %while.59 = (s32[]{:T(128)}, f32[3,192,384]{2,1,0:T(8,128)S(1)}, f32[4,2,128,128]{3,2,0,1:T(8,128)S(1)}, f32[128,128]{1,0:T(8,128)S(1)}, s32[2,2]{1,0:T(2,128)S(...) while((s32[]{:T(128)}, f32[3,192,384]{2,1,0:T(8,128)S(1)}, ...), condition=%wide.region_13.14_spmd.clone.clone.clone.clone, body=%wide.region_9.13_spmd.clone.clone.clone.clone.sunk | while | flops 1618100224 | bytes 17244724 | solution.py:114
  243.0 1.7 dynamic_update_slice.33
  262.1 2.8 dynamic_update_slice.33
  265.9 3.3 collective-permute-start.9
  269.3 123.4 %all-reduce.5.cloned.1.call-done = (f32[4,2,128,128]{3,2,1,0:T(8,128)}, f32[128,128]{1,0:T(8,128)}) async-done(((f32[4,2,128,128]{3,2,1,0:T(8,128)}, f32[128,128]{1,0:T(8,128)}), (f32[4,2,128,128]{3,2,1,0:T(8,128)}, f32[128,128]{1,0:T(8,128)})) %all-reduce.5.cloned.1.call-update) | async-done | bytes 589840 | tf_op jit(solution)/shard_map/psum | solution.py:124
  393.6 3.5 collective-permute-start.10
  397.1 4.7 %collective-permute-start.11 = (f32[3,64,256]{2,1,0:T(8,128)S(1)}, f32[3,64,256]{2,1,0:T(8,128)S(1)}, u32[]{:S(2)}, u32[]{:S(2)}) collective-permute-start(f32[3,64,256]{2,1,0:T(8,128)S(1)} %get-tuple-element.1217), channel_id=1, source_target_pairs={{0,8},{4,12},{8,16},{12,20},{16,24},{20,28},{1,9},{5,13},{9,17},{1... | collective-permute-start | bytes 589832 | tf_op jit(solution)/shard_map/ppermute | solution.py:14
  401.8 1.6 divide_add_fusion
  403.4 1.6 collective-permute-done.11
  405.0 0.9 copy-done.4
  (153 shorter events, 57.5 us)
Async XLA Ops:
  7.2 194.5 %all-reduce.7.cloned.1.call-start = ((), (), s32[]{:S(2)}) async-start(), calls=%async_computation.1 | async-start | bytes 1179648 | tf_op jit(solution)/shard_map/psum | solution.py:124
  7.2 11.6 %collective-permute-start = (f32[2,64,256]{2,1,0:T(8,128)}, f32[2,64,256]{2,1,0:T(8,128)S(1)}, u32[]{:S(2)}, u32[]{:S(2)}) collective-permute-start(f32[2,64,256]{2,1,0:T(8,128)} %param.29), channel_id=1, source_target_pairs={{4,0},{8,4},{12,8},{16,12},{20,16},{24,20},{28,24},{5,1},{9,5},{13... | collective-permute-start | bytes 393224 | tf_op jit(solution)/shard_map/ppermute | solution.py:14
  8.5 11.3 %collective-permute-start.1 = (f32[2,64,256]{2,1,0:T(8,128)}, f32[2,64,256]{2,1,0:T(8,128)S(1)}, u32[]{:S(2)}, u32[]{:S(2)}) collective-permute-start(f32[2,64,256]{2,1,0:T(8,128)} %param.29), channel_id=1, source_target_pairs={{8,0},{12,4},{16,8},{20,12},{24,16},{28,20},{9,1},{13,5},{17,9},{2... | collective-permute-start | bytes 393224 | tf_op jit(solution)/shard_map/ppermute | solution.py:14
  9.8 9.0 %copy-start.7 = (f32[2,64,256]{2,1,0:T(8,128)S(1)}, f32[2,64,256]{2,1,0:T(8,128)}, u32[]{:S(2)}) copy-start(f32[2,64,256]{2,1,0:T(8,128)} %param.29) | copy-start | bytes 393220
  19.8 3.3 collective-permute-start.2
  23.2 0.9 copy-start
  23.2 0.9 copy-start.10
  63.5 0.6 copy-start.2
  64.1 7.7 %collective-permute-start.3 = (f32[3,192,128]{2,1,0:T(8,128)S(1)}, f32[3,192,128]{2,1,0:T(8,128)S(1)}, u32[]{:S(2)}, u32[]{:S(2)}) collective-permute-start(f32[3,192,128]{2,1,0:T(8,128)S(1)} %slice.279), channel_id=1, source_target_pairs={{0,1},{1,2},{2,3},{4,5},{5,6},{6,7},{8,9},{9,10},{10,11},{12,13},{... | collective-permute-start | bytes 884744 | tf_op jit(solution)/shard_map/ppermute | solution.py:14
  71.6 321.1 %all-reduce.5.cloned.1.call-start = ((), (), s32[]{:S(2)}) async-start(), calls=%async_computation | async-start | bytes 1179648 | tf_op jit(solution)/shard_map/psum | solution.py:124
  71.9 130.6 %collective-permute-start.4 = (f32[3,64,256]{2,1,0:T(8,128)S(1)}, f32[3,64,256]{2,1,0:T(8,128)S(1)}, u32[]{:S(2)}, u32[]{:S(2)}) collective-permute-start(f32[3,64,256]{2,1,0:T(8,128)S(1)} %get-tuple-element.1218), channel_id=1, source_target_pairs={{0,4},{4,8},{8,12},{12,16},{16,20},{20,24},{24,28},{1,5},{5,9},{9,... | collective-permute-start | bytes 589832 | tf_op jit(solution)/shard_map/ppermute | solution.py:14
  75.8 126.7 %collective-permute-start.5 = (f32[3,64,256]{2,1,0:T(8,128)S(1)}, f32[3,64,256]{2,1,0:T(8,128)S(1)}, u32[]{:S(2)}, u32[]{:S(2)}) collective-permute-start(f32[3,64,256]{2,1,0:T(8,128)S(1)} %get-tuple-element.1219), channel_id=1, source_target_pairs={{0,8},{4,12},{8,16},{12,20},{16,24},{20,28},{1,9},{5,13},{9,17},{1... | collective-permute-start | bytes 589832 | tf_op jit(solution)/shard_map/ppermute | solution.py:14
  202.5 0.9 copy-start.8
  203.5 2.8 copy-start.9
  203.5 21.9 %copy-start.3 = (f32[2,64,256]{2,1,0:T(8,128)}, f32[2,64,256]{2,1,0:T(8,128)S(1)}, u32[]{:S(2)}) copy-start(f32[2,64,256]{2,1,0:T(8,128)S(1)} %fusion.283) | copy-start | bytes 393220
  203.5 7.7 %collective-permute-start.6 = (f32[2,64,256]{2,1,0:T(8,128)S(1)}, f32[2,64,256]{2,1,0:T(8,128)S(1)}, u32[]{:S(2)}, u32[]{:S(2)}) collective-permute-start(f32[2,64,256]{2,1,0:T(8,128)S(1)} %fusion.283), channel_id=1, source_target_pairs={{4,0},{8,4},{12,8},{16,12},{20,16},{24,20},{28,24},{5,1},{9,5},{13... | collective-permute-start | bytes 393224 | tf_op jit(solution)/shard_map/ppermute | solution.py:14
  204.9 10.0 %collective-permute-start.7 = (f32[2,64,256]{2,1,0:T(8,128)S(1)}, f32[2,64,256]{2,1,0:T(8,128)S(1)}, u32[]{:S(2)}, u32[]{:S(2)}) collective-permute-start(f32[2,64,256]{2,1,0:T(8,128)S(1)} %fusion.283), channel_id=1, source_target_pairs={{8,0},{12,4},{16,8},{20,12},{24,16},{28,20},{9,1},{13,5},{17,9},{2... | collective-permute-start | bytes 393224 | tf_op jit(solution)/shard_map/ppermute | solution.py:14
  207.2 9.1 %copy-start.5 = (f32[1,2,128,128]{3,2,1,0:T(8,128)}, f32[1,2,128,128]{3,2,1,0:T(8,128)S(1)}, u32[]{:S(2)}) copy-start(f32[1,2,128,128]{3,2,1,0:T(8,128)S(1)} %divide_add_fusion.1) | copy-start | bytes 393220
  214.9 10.4 %collective-permute-start.8 = (f32[2,192,128]{2,1,0:T(8,128)S(1)}, f32[2,192,128]{2,1,0:T(8,128)S(1)}, u32[]{:S(2)}, u32[]{:S(2)}) collective-permute-start(f32[2,192,128]{2,1,0:T(8,128)S(1)} %pad_maximum_fusion.2), channel_id=1, source_target_pairs={{1,0},{2,1},{3,2},{5,4},{6,5},{7,6},{9,8},{10,9},{11,10},{13,12},{... | collective-permute-start | bytes 589832 | tf_op jit(solution)/shard_map/ppermute | solution.py:14
  265.0 0.9 copy-start.1
  265.9 127.6 %collective-permute-start.9 = (f32[3,192,128]{2,1,0:T(8,128)S(1)}, f32[3,192,128]{2,1,0:T(8,128)S(1)}, u32[]{:S(2)}, u32[]{:S(2)}) collective-permute-start(f32[3,192,128]{2,1,0:T(8,128)S(1)} %slice.290), channel_id=1, source_target_pairs={{0,1},{1,2},{2,3},{4,5},{5,6},{6,7},{8,9},{9,10},{10,11},{12,13},{... | collective-permute-start | bytes 884744 | tf_op jit(solution)/shard_map/ppermute | solution.py:14
  393.6 8.2 %copy-start.6 = (f32[1,2,128,128]{3,2,1,0:T(8,128)S(1)}, f32[1,2,128,128]{3,2,1,0:T(8,128)}, u32[]{:S(2)}) copy-start(f32[1,2,128,128]{3,2,1,0:T(8,128)} %copy-done.5) | copy-start | bytes 393220
  393.6 9.8 %collective-permute-start.10 = (f32[3,64,256]{2,1,0:T(8,128)S(1)}, f32[3,64,256]{2,1,0:T(8,128)S(1)}, u32[]{:S(2)}, u32[]{:S(2)}) collective-permute-start(f32[3,64,256]{2,1,0:T(8,128)S(1)} %get-tuple-element.1216), channel_id=1, source_target_pairs={{0,4},{4,8},{8,12},{12,16},{16,20},{20,24},{24,28},{1,5},{5,9},{9,... | collective-permute-start | bytes 589832 | tf_op jit(solution)/shard_map/ppermute | solution.py:14
  397.1 7.8 %collective-permute-start.11 = (f32[3,64,256]{2,1,0:T(8,128)S(1)}, f32[3,64,256]{2,1,0:T(8,128)S(1)}, u32[]{:S(2)}, u32[]{:S(2)}) collective-permute-start(f32[3,64,256]{2,1,0:T(8,128)S(1)} %get-tuple-element.1217), channel_id=1, source_target_pairs={{0,8},{4,12},{8,16},{12,20},{16,24},{20,28},{1,9},{5,13},{9,17},{1... | collective-permute-start | bytes 589832 | tf_op jit(solution)/shard_map/ppermute | solution.py:14
  405.0 0.9 copy-start.4
Sparse Core Ops, SparseCore 0:
  71.7 129.8 all-reduce.6
  266.0 126.6 all-reduce.4
where the time goes:
time: 414 us; the launch traced here: 413 us
  waiting for transfers between devices  257 us (62%)
  matrix products  47.3 us (11%)
  starting transfers between devices  34.7 us (8%)
  loops' own time  18.2 us (4%)
  blocking collectives  18 us (4%)
  local copies, waits for them, and re-layouts  16.6 us (4%)
  between operations  14.5 us (4%)
  other arithmetic  7.29 us (2%)
    psum x2, waiting for transfers between devices, local(): lax.psum((gradient, density), ('scan', 'mode'))  244 us
    dot_general x64, matrix products, product(): return jnp.einsum(form, first, second, precision=lax.Precision.HIGHEST)  47.3 us
    ppermute x12, starting transfers between devices, passed_along(): lax.ppermute(value, axis, [(source, source + steps) for source in range(i...  34.6 us
    another operation x2, loops' own time, local(): lax.fori_loop(0, slot_count, add_position, initial)  18.2 us
    all_gather x2, blocking collectives, local(): probes = lax.all_gather(probe, 'mode', axis=0, tiled=True)  18 us
    ppermute x12, waiting for transfers between devices, passed_along(): lax.ppermute(value, axis, [(source, source + steps) for source in range(i...  12.4 us
    dynamic_update_slice x4, local copies, waits for them, and re-layouts, add_position(): lax.dynamic_update_slice(sums, current + used * numerator, (start_zero, r...  8.97 us
  transfers between devices with their start and end apart: 14, of which 8 were waited for; matrix products, arithmetic and copies ran while one was open for 1% of the time, Pallas kernels for 0%

commit v1 on v0

v1 whole, which is shorter than its diff:
```python
import functools
import math

import jax
import jax.numpy as jnp
import numpy as np
from jax import lax
from jax.experimental import pallas as pl
from jax.experimental.pallas import tpu as pltpu
from jax.sharding import PartitionSpec as P

ITERS = 2
SUBLANES, LANES = 8, 128
F32 = jnp.float32
BF16 = jnp.bfloat16


def shifted(value, axis, steps):
    count = lax.axis_size(axis)
    initial, last = (max(0, -steps), min(count, count - steps))
    return lax.ppermute(value, axis, [(source, source + steps) for source in range(initial, last)])


def swapped(value, axis, bit):
    return lax.ppermute(value, axis, [(i, i ^ bit) for i in range(lax.axis_size(axis))])


def bits_of(axis):
    return [1 << b for b in range(lax.axis_size(axis).bit_length() - 1)]


def gathered(value, axis):
    for bit in reversed(bits_of(axis)):
        value = jnp.concatenate([value, swapped(value, axis, bit)], axis=0)
    return value


def scattered(value, axis):
    for bit in bits_of(axis):
        half = value.shape[0] // 2
        value = value[:half] + swapped(value[half:], axis, bit)
    return value


def summed(value, axis):
    for bit in bits_of(axis):
        value = value + swapped(value, axis, bit)
    return value


@functools.lru_cache
def fresnel_parts(length):
    ids = np.arange(length, dtype=np.int64)
    phase = ids[:, None] * ids[None, :] % length
    centred = ids - length // 2
    chirp = centred * centred % (4 * length)
    angle = -2.0 * math.pi / length * phase + math.pi / (2 * length) * chirp[None, :]
    real, imag = np.cos(angle) / math.sqrt(length), np.sin(angle) / math.sqrt(length)
    whole = np.block([[real, -imag], [imag, real]])
    parts = []
    for matrix in (whole, whole.T):
        high = matrix.astype(jnp.bfloat16)
        low = (matrix - high.astype(np.float64)).astype(jnp.bfloat16)
        parts.append(np.stack([high, low]))
    return np.stack(parts)


def split(value):
    high = value.astype(BF16)
    return high, (value - high.astype(F32)).astype(BF16)


def dot(a, b):
    return jnp.dot(a, b, preferred_element_type=F32)


def window_of(row, col):
    return (
        pl.multiple_of(row // SUBLANES * SUBLANES, SUBLANES),
        pl.multiple_of(col // LANES * LANES, LANES),
        row % SUBLANES,
        col % LANES,
    )


def cut(wide, down, right, length):
    wide = pltpu.roll(wide, 2 * LANES - right, 1)[:, :length]
    return pltpu.roll(wide, length + SUBLANES - down, 0)[:length]


def placed_in(term, down, right):
    tall = jnp.concatenate([term, jnp.zeros((SUBLANES, term.shape[1]), F32)], axis=0)
    tall = pltpu.roll(tall, down, 0)
    return pltpu.roll(jnp.concatenate([tall, jnp.zeros_like(tall)], axis=1), right, 1)


def patches_kernel(place, extended, patch, density):
    slots, _, length, _ = patch.shape
    total = None
    for slot in range(slots):
        row, col, used = place[3 * slot], place[3 * slot + 1], place[3 * slot + 2]
        top, left, down, right = window_of(row, col)
        here = 0.0
        for part in range(2):
            wide = extended[part, pl.ds(top, length + SUBLANES), pl.ds(left, 2 * LANES)]
            window = cut(wide, down, right, length)
            patch[slot, part] = window
            here = here + window * window
        here = here * used.astype(F32)
        total = here if total is None else total + here
    density[...] = total


def wave_kernel(place, patch, probes, amplitude, table, sums, gradient, x_hi, x_lo, y_hi, y_lo, far):
    slots, _, length, _ = patch.shape
    modes = probes.shape[0]

    def from_left(which):
        for k in range(modes):
            cols = slice(k * length, (k + 1) * length)
            hi, lo = x_hi[:, cols], x_lo[:, cols]
            out = dot(table[which, 0], hi) + dot(table[which, 0], lo) + dot(table[which, 1], hi)
            hi, lo = split(out)
            rows = slice(k * length, (k + 1) * length)
            y_hi[rows, :length], y_hi[rows, length:] = hi[:length], hi[length:]
            y_lo[rows, :length], y_lo[rows, length:] = lo[:length], lo[length:]

    def from_right(which, k):
        rows = slice(k * length, (k + 1) * length)
        hi, lo = y_hi[rows], y_lo[rows]
        return dot(hi, table[which, 0]) + dot(lo, table[which, 0]) + dot(hi, table[which, 1])

    def set_columns(k, real, imag):
        cols = slice(k * length, (k + 1) * length)
        hi, lo = split(real)
        x_hi[:length, cols], x_lo[:length, cols] = hi, lo
        hi, lo = split(imag)
        x_hi[length:, cols], x_lo[length:, cols] = hi, lo

    sums[...] = jnp.zeros_like(sums)
    for slot in range(slots):
        row, col, used = place[3 * slot], place[3 * slot + 1], place[3 * slot + 2].astype(F32)
        obj_re, obj_im = patch[slot, 0], patch[slot, 1]
        for k in range(modes):
            pr, pi = probes[k, 0], probes[k, 1]
            set_columns(k, pr * obj_re - pi * obj_im, pr * obj_im + pi * obj_re)
        from_left(0)
        intensity = 0.0
        for k in range(modes):
            wave = from_right(1, k)
            far[k] = wave
            square = wave * wave
            intensity = intensity + square[:, :length] + square[:, length:]
        factor = amplitude[slot] / jnp.sqrt(jnp.maximum(intensity, 1.0))
        for k in range(modes):
            set_columns(k, far[k, :, :length] * factor, far[k, :, length:] * factor)
        from_left(1)
        num_re, num_im = 0.0, 0.0
        for k in range(modes):
            near = from_right(0, k)
            pr, pi = probes[k, 0], probes[k, 1]
            change_re = (near[:, :length] - (pr * obj_re - pi * obj_im)) * used
            change_im = (near[:, length:] - (pr * obj_im + pi * obj_re)) * used
            num_re = num_re + (pr * change_re + pi * change_im)
            num_im = num_im + (pr * change_im - pi * change_re)
            grad_re = obj_re * change_re + obj_im * change_im
            grad_im = obj_re * change_im - obj_im * change_re
            if slot == 0:
                gradient[k, 0], gradient[k, 1] = grad_re, grad_im
            else:
                gradient[k, 0] += grad_re
                gradient[k, 1] += grad_im
        top, left, down, right = window_of(row, col)
        for part, term in enumerate((num_re, num_im)):
            sums[part, pl.ds(top, length + SUBLANES), pl.ds(left, 2 * LANES)] += placed_in(term, down, right)


def weight_kernel(place, probes, weight, acc):
    modes, _, length, _ = probes.shape
    rows, cols = weight.shape
    top = acc.shape[0] - rows - length
    left = acc.shape[1] - cols - length
    power = 0.0
    for k in range(modes):
        power = power + (probes[k, 0] * probes[k, 0] + probes[k, 1] * probes[k, 1])
    acc[...] = jnp.zeros_like(acc)
    for slot in range(place.shape[0] // 3):
        row, col, used = place[3 * slot] + top, place[3 * slot + 1] + left, place[3 * slot + 2].astype(F32)
        above, before, down, right = window_of(row, col)
        acc[pl.ds(above, length + SUBLANES), pl.ds(before, 2 * LANES)] += placed_in(power * used, down, right)
    weight[...] = acc[pl.ds(top, rows), pl.ds(left, cols)]


VMEM = pl.BlockSpec(memory_space=pltpu.VMEM)
SMEM = pl.BlockSpec(memory_space=pltpu.SMEM)


def call(kernel, out_shape, in_specs, scratch=(), flops=0, moved=0):
    return pl.pallas_call(
        kernel,
        out_shape=out_shape,
        in_specs=in_specs,
        out_specs=jax.tree.map(lambda _: VMEM, out_shape),
        scratch_shapes=list(scratch),
        compiler_params=pltpu.CompilerParams(vmem_limit_bytes=32 * 2**20),
        cost_estimate=pl.CostEstimate(flops=flops, bytes_accessed=moved, transcendentals=0),
    )


def local(object_field, probe, amplitude, offsets, counts):
    tile_rows, band_cols = object_field.shape[1:]
    modes = lax.axis_size("mode")
    length = probe.shape[2]
    slots = amplitude.shape[0]
    reach = -(-length // tile_rows)
    ext_rows, ext_cols = tile_rows + length, band_cols + length
    table = jnp.asarray(fresnel_parts(length))
    used = (jnp.arange(slots, dtype=jnp.int32) < counts[0]).astype(jnp.int32)
    place = jnp.stack([offsets[:, 0] % tile_rows, offsets[:, 1] % band_cols, used], axis=1)

    before = jnp.stack([place, shifted(place, "mode", 1) - jnp.array([0, band_cols, 0], jnp.int32)])
    before = jnp.where(
        (lax.axis_index("mode") == 0) & (jnp.arange(2) == 1)[:, None, None], 0, before
    )
    windows = [before]
    for step in range(1, reach + 1):
        arrived = shifted(before, "scan", step) - jnp.array([step * tile_rows, 0, 0], jnp.int32)
        windows.append(jnp.where(lax.axis_index("scan") < step, 0, arrived))
    windows = jnp.concatenate(windows).reshape(-1)
    place = place.reshape(-1)

    def sds(*shape):
        return jax.ShapeDtypeStruct(shape, F32)

    wave_flops = slots * modes * 4 * 3 * 2 * 4 * length**3
    for iteration in range(ITERS):
        probes = gathered(probe, "mode")
        pieces = [object_field]
        for step in range(1, reach + 1):
            pieces.append(shifted(object_field, "scan", -step)[:, : length - (step - 1) * tile_rows])
        extended_rows = jnp.concatenate(pieces, axis=1)
        beside = shifted(extended_rows[:, :, :length], "mode", -1)
        extended = jnp.concatenate([extended_rows, beside], axis=2)
        patch, density = call(
            patches_kernel,
            (sds(slots, 2, length, length), sds(length, length)),
            [SMEM, VMEM],
            flops=2**20,
            moved=2**20,
        )(place, extended)
        sums, gradient = call(
            wave_kernel,
            (sds(2, ext_rows, ext_cols), sds(modes, 2, length, length)),
            [SMEM, VMEM, VMEM, VMEM, VMEM],
            [pltpu.VMEM((2 * length, modes * length), BF16)] * 2
            + [pltpu.VMEM((modes * length, 2 * length), BF16)] * 2
            + [pltpu.VMEM((modes, length, 2 * length), F32)],
            flops=wave_flops,
            moved=4 * 2**20,
        )(place, patch, probes, amplitude, table)
        weight = call(
            weight_kernel,
            sds(tile_rows, band_cols),
            [SMEM, VMEM],
            [pltpu.VMEM((reach * tile_rows + tile_rows + length, 2 * band_cols + length), F32)],
            flops=2**20,
            moved=2**20,
        )(windows, probes)
        density = summed(summed(density, "mode"), "scan")
        own = summed(scattered(gradient, "mode"), "scan")
        margin = shifted(sums[:, :, band_cols:], "mode", 1)
        folded = sums[:, :, :band_cols].at[:, :, :length].add(margin)
        block = folded[:, :tile_rows]
        for step in range(1, reach + 1):
            rows = folded[:, step * tile_rows : (step + 1) * tile_rows]
            arrived = shifted(rows, "scan", step)
            block = block.at[:, : arrived.shape[1]].add(arrived)
        object_field = object_field + block / (weight + 1.0)
        probe = probe + own / (density + 1.0)
    return (object_field, probe)


def solution(mesh):
    placed = (
        P(None, "scan", "mode"),
        P("mode", None, None, None),
        P(("scan", "mode"), None, None),
        P(("scan", "mode"), None),
        P(("scan", "mode")),
    )
    return jax.shard_map(
        local,
        mesh=mesh,
        in_specs=placed,
        out_specs=(P(None, "scan", "mode"), P("mode", None, None, None)),
        check_vma=False,
    )
```

time: 414 us -> 133 us (0.32)
  waiting for transfers between devices: 257 us -> 50.3 us
  matrix products: 47.3 us -> 0 us
  starting transfers between devices: 34.7 us -> 63.3 us
  loops' own time: 18.2 us -> 0 us
  blocking collectives: 18 us -> 0 us
  local copies, waits for them, and re-layouts: 16.6 us -> 2.71 us
  between operations: 14.5 us -> 2.01 us
  Pallas kernels: 0 us -> 12.1 us
  other arithmetic: 7.29 us -> 2.31 us
    psum x2 -> x0, waiting for transfers between devices: 244 us -> none  [local(): lax.psum((gradient, density), ('scan', 'mode'))]
    dot_general x64 -> x0, matrix products: 47.3 us -> none  [product(): return jnp.einsum(form, first, second, precision=lax.Precision.HIGHEST)]
    ppermute x12 -> x39, waiting for transfers between devices: 12.4 us -> 50.3 us  [the longest x24 48.2 us: swapped(): lax.ppermute(value, axis, [(i, i ^ bit) for i in range(lax.axis_size(axis...]
    ppermute x12 -> x39, starting transfers between devices: 34.6 us -> 63.3 us  [the longest x15 36.9 us: shifted(): lax.ppermute(value, axis, [(source, source + steps) for source in range(i...]
    another operation x2 -> x0, loops' own time: 18.2 us -> none  [local(): lax.fori_loop(0, slot_count, add_position, initial)]
    all_gather x2 -> x0, blocking collectives: 18 us -> none  [local(): probes = lax.all_gather(probe, 'mode', axis=0, tiled=True)]
    pallas_call x0 -> x6, Pallas kernels: none -> 12.1 us  [the longest x2 8.35 us: local(): call(wave_kernel, (sds(2, ext_rows, ext_cols), sds(modes, 2, length, leng...]
    dynamic_update_slice x4 -> x0, local copies, waits for them, and re-layouts: 8.97 us -> none  [add_position(): lax.dynamic_update_slice(sums, current + used * numerator, (start_zero, r...]
  transfers between devices with their start and end apart: 14 -> 39, of which waited for: 8 -> 13; matrix products, arithmetic and copies ran while one was open for 1% -> 2% of each run, Pallas kernels for 0% -> 9%
where the time goes in v1:
time: 133 us
  starting transfers between devices  63.3 us (48%)
  waiting for transfers between devices  50.3 us (38%)
  Pallas kernels  12.1 us (9%)
  local copies, waits for them, and re-layouts  2.71 us (2%)
  other arithmetic  2.31 us (2%)
  between operations  2.01 us (2%)
    ppermute x24, waiting for transfers between devices, swapped(): lax.ppermute(value, axis, [(i, i ^ bit) for i in range(lax.axis_size(axis...  48.2 us
    ppermute x15, starting transfers between devices, shifted(): lax.ppermute(value, axis, [(source, source + steps) for source in range(i...  36.9 us
    ppermute x24, starting transfers between devices, swapped(): lax.ppermute(value, axis, [(i, i ^ bit) for i in range(lax.axis_size(axis...  26.4 us
    pallas_call x2, Pallas kernels, local(): call(wave_kernel, (sds(2, ext_rows, ext_cols), sds(modes, 2, length, leng...  8.35 us
  transfers between devices with their start and end apart: 39, of which 13 were waited for; matrix products, arithmetic and copies ran while one was open for 2% of the time, Pallas kernels for 9%

profile of v1, /device:TPU:0, one launch (start us, length us, event | category | flops | bytes accessed | tf_op | source)
XLA Modules:
  0.0 132.7 jit_solution(15130419732489376281)
XLA Ops:
  4.7 2.3 %collective-permute-start.8 = (s32[2,3]{1,0:T(2,128)S(1)}, s32[2,3]{1,0:T(2,128)S(1)}, u32[]{:S(2)}, u32[]{:S(2)}) collective-permute-start(s32[2,3]{1,0:T(2,128)S(1)} %pad_add_fusion.1), channel_id=1, source_target_pairs={{0,1},{1,2},{2,3},{4,5},{5,6},{6,7},{8,9},{9,10},{10,11},{12,13},{... | collective-permute-start | bytes 80 | tf_op jit(solution)/shard_map/ppermute | solution.py:21
  7.1 2.6 %collective-permute-start.3 = (f32[1,2,128,128]{3,2,1,0:T(8,128)}, f32[1,2,128,128]{3,2,1,0:T(8,128)S(1)}, u32[]{:S(2)}, u32[]{:S(2)}) collective-permute-start(f32[1,2,128,128]{3,2,1,0:T(8,128)} %param.30), channel_id=1, source_target_pairs={{0,2},{1,3},{2,0},{3,1},{4,6},{5,7},{6,4},{7,5},{8,10},{9,11},{10,... | collective-permute-start | bytes 393224 | tf_op jit(solution)/shard_map/ppermute | solution.py:25
  11.5 5.5 %collective-permute-start.10 = (s32[2,2,3]{2,1,0:T(2,128)S(1)}, s32[2,2,3]{2,1,0:T(2,128)S(1)}, u32[]{:S(2)}, u32[]{:S(2)}) collective-permute-start(s32[2,2,3]{2,1,0:T(2,128)S(1)} %add_select_fusion), channel_id=1, source_target_pairs={{0,8},{4,12},{8,16},{12,20},{16,24},{20,28},{1,9},{5,13},{9,17},{1... | collective-permute-start | bytes 152 | tf_op jit(solution)/shard_map/ppermute | solution.py:21
  17.0 3.6 %collective-permute-start.9 = (s32[2,2,3]{2,1,0:T(2,128)S(1)}, s32[2,2,3]{2,1,0:T(2,128)S(1)}, u32[]{:S(2)}, u32[]{:S(2)}) collective-permute-start(s32[2,2,3]{2,1,0:T(2,128)S(1)} %add_select_fusion), channel_id=1, source_target_pairs={{0,4},{4,8},{8,12},{12,16},{16,20},{20,24},{24,28},{1,5},{5,9},{9,... | collective-permute-start | bytes 152 | tf_op jit(solution)/shard_map/ppermute | solution.py:21
  22.2 2.0 %collective-permute-done.2 = f32[2,192,128]{2,1,0:T(8,128)S(1)} collective-permute-done((f32[2,192,128]{2,1,0:T(8,128)S(1)}, f32[2,192,128]{2,1,0:T(8,128)S(1)}, u32[]{:S(2)}, u32[]{:S(2)}) %collective-permute-start.2) | collective-permute-done | bytes 196640 | tf_op jit(solution)/shard_map/ppermute | solution.py:21
  25.0 4.2 %collective-permute-start.19 = (f32[128,128]{1,0:T(8,128)S(1)}, f32[128,128]{1,0:T(8,128)S(1)}, u32[]{:S(2)}, u32[]{:S(2)}) collective-permute-start(f32[128,128]{1,0:T(8,128)S(1)} %get-tuple-element.118), channel_id=1, source_target_pairs={{0,1},{1,0},{2,3},{3,2},{4,5},{5,4},{6,7},{7,6},{8,9},{9,8},{10,11... | collective-permute-start | bytes 196616 | tf_op jit(solution)/shard_map/ppermute | solution.py:25
  29.3 4.2 %shard_map.125 = (f32[2,192,384]{2,1,0:T(8,128)S(1)}, f32[4,2,128,128]{3,2,1,0:T(8,128)S(1)}) custom-call(s32[6]{0:T(128)S(1)} %reshape.225.place, f32[2,2,128,128]{3,2,1,0:T(8,128)S(1)} %get-tuple-element.114.patch, f32[4,2,128,128]{3,2,1,0:T(8,128)S(1)} %constant_dynamic-update-slice_fusion.3.probes, f32[2,128,128]{2,1,0:T(8,128)S(1)} %copy-done, ...), custom_call_target="tpu_custom_call" | custom-call | flops 1610612736 | bytes 4194304 | tf_op jit(solution)/shard_map/pallas_call | solution.py:251
  33.5 2.7 %collective-permute-start.5 = (f32[2,192,128]{2,1,0:T(8,128)S(1)}, f32[2,192,128]{2,1,0:T(8,128)S(1)}, u32[]{:S(2)}, u32[]{:S(2)}) collective-permute-start(f32[2,192,128]{2,1,0:T(8,128)S(1)} %slice.197), channel_id=1, source_target_pairs={{0,1},{1,2},{2,3},{4,5},{5,6},{6,7},{8,9},{9,10},{10,11},{12,13},{... | collective-permute-start | bytes 589832 | tf_op jit(solution)/shard_map/ppermute | solution.py:21
  36.5 4.1 %collective-permute-done.20 = f32[128,128]{1,0:T(8,128)S(1)} collective-permute-done((f32[128,128]{1,0:T(8,128)S(1)}, f32[128,128]{1,0:T(8,128)S(1)}, u32[]{:S(2)}, u32[]{:S(2)}) %collective-permute-start.20) | collective-permute-done | bytes 65568 | tf_op jit(solution)/shard_map/ppermute | solution.py:25
  40.6 2.5 %collective-permute-start.21 = (f32[128,128]{1,0:T(8,128)S(1)}, f32[128,128]{1,0:T(8,128)S(1)}, u32[]{:S(2)}, u32[]{:S(2)}) collective-permute-start(f32[128,128]{1,0:T(8,128)S(1)} %add.159), channel_id=1, source_target_pairs={{0,4},{4,0},{8,12},{12,8},{16,20},{20,16},{24,28},{28,24},{1,5},{5... | collective-permute-start | bytes 196616 | tf_op jit(solution)/shard_map/ppermute | solution.py:25
  45.4 1.6 %collective-permute-start.22 = (f32[128,128]{1,0:T(8,128)S(1)}, f32[128,128]{1,0:T(8,128)S(1)}, u32[]{:S(2)}, u32[]{:S(2)}) collective-permute-start(f32[128,128]{1,0:T(8,128)S(1)} %add.160), channel_id=1, source_target_pairs={{0,8},{4,12},{8,0},{12,4},{16,24},{20,28},{24,16},{28,20},{1,9},{5... | collective-permute-start | bytes 196616 | tf_op jit(solution)/shard_map/ppermute | solution.py:25
  48.2 4.1 %collective-permute-start.6 = (f32[2,64,256]{2,1,0:T(8,128)S(1)}, f32[2,64,256]{2,1,0:T(8,128)S(1)}, u32[]{:S(2)}, u32[]{:S(2)}) collective-permute-start(f32[2,64,256]{2,1,0:T(8,128)S(1)} %get-tuple-element.124), channel_id=1, source_target_pairs={{0,4},{4,8},{8,12},{12,16},{16,20},{20,24},{24,28},{1,5},{5,9},{9,... | collective-permute-start | bytes 393224 | tf_op jit(solution)/shard_map/ppermute | solution.py:21
  52.3 2.4 %collective-permute-start.7 = (f32[2,64,256]{2,1,0:T(8,128)S(1)}, f32[2,64,256]{2,1,0:T(8,128)S(1)}, u32[]{:S(2)}, u32[]{:S(2)}) collective-permute-start(f32[2,64,256]{2,1,0:T(8,128)S(1)} %get-tuple-element.125), channel_id=1, source_target_pairs={{0,8},{4,12},{8,16},{12,20},{16,24},{20,28},{1,9},{5,13},{9,17},{1... | collective-permute-start | bytes 393224 | tf_op jit(solution)/shard_map/ppermute | solution.py:21
  55.0 1.5 %collective-permute-start.23 = (f32[128,128]{1,0:T(8,128)S(1)}, f32[128,128]{1,0:T(8,128)S(1)}, u32[]{:S(2)}, u32[]{:S(2)}) collective-permute-start(f32[128,128]{1,0:T(8,128)S(1)} %add.161), channel_id=1, source_target_pairs={{0,16},{4,20},{8,24},{12,28},{16,0},{20,4},{24,8},{28,12},{1,17},{... | collective-permute-start | bytes 196616 | tf_op jit(solution)/shard_map/ppermute | solution.py:25
  56.6 3.2 %collective-permute-done.16 = f32[1,2,128,128]{3,2,1,0:T(8,128)S(1)} collective-permute-done((f32[1,2,128,128]{3,2,1,0:T(8,128)S(1)}, f32[1,2,128,128]{3,2,1,0:T(8,128)S(1)}, u32[]{:S(2)}, u32[]{:S(2)}) %collective-permute-start.16) | collective-permute-done | bytes 131104 | tf_op jit(solution)/shard_map/ppermute | solution.py:25
  62.7 3.4 %collective-permute-done.17 = f32[1,2,128,128]{3,2,1,0:T(8,128)S(1)} collective-permute-done((f32[1,2,128,128]{3,2,1,0:T(8,128)S(1)}, f32[1,2,128,128]{3,2,1,0:T(8,128)S(1)}, u32[]{:S(2)}, u32[]{:S(2)}) %collective-permute-start.17) | collective-permute-done | bytes 131104 | tf_op jit(solution)/shard_map/ppermute | solution.py:25
  66.2 2.8 %collective-permute-start.18 = (f32[1,2,128,128]{3,2,1,0:T(8,128)S(1)}, f32[1,2,128,128]{3,2,1,0:T(8,128)S(1)}, u32[]{:S(2)}, u32[]{:S(2)}) collective-permute-start(f32[1,2,128,128]{3,2,1,0:T(8,128)S(1)} %add.156), channel_id=1, source_target_pairs={{0,16},{4,20},{8,24},{12,28},{16,0},{20,4},{24,8},{28,12},{1,17},{... | collective-permute-start | bytes 393224 | tf_op jit(solution)/shard_map/ppermute | solution.py:25
  70.3 6.3 %collective-permute-done.18 = f32[1,2,128,128]{3,2,1,0:T(8,128)S(1)} collective-permute-done((f32[1,2,128,128]{3,2,1,0:T(8,128)S(1)}, f32[1,2,128,128]{3,2,1,0:T(8,128)S(1)}, u32[]{:S(2)}, u32[]{:S(2)}) %collective-permute-start.18) | collective-permute-done | bytes 131104 | tf_op jit(solution)/shard_map/ppermute | solution.py:25
  78.2 3.6 %collective-permute-done.24 = f32[1,2,128,128]{3,2,1,0:T(8,128)S(1)} collective-permute-done((f32[1,2,128,128]{3,2,1,0:T(8,128)S(1)}, f32[1,2,128,128]{3,2,1,0:T(8,128)S(1)}, u32[]{:S(2)}, u32[]{:S(2)}) %collective-permute-start.24) | collective-permute-done | bytes 131104 | tf_op jit(solution)/shard_map/ppermute | solution.py:25
  82.4 4.0 %collective-permute-done.35 = f32[128,128]{1,0:T(8,128)S(1)} collective-permute-done((f32[128,128]{1,0:T(8,128)S(1)}, f32[128,128]{1,0:T(8,128)S(1)}, u32[]{:S(2)}, u32[]{:S(2)}) %collective-permute-start.35) | collective-permute-done | bytes 65568 | tf_op jit(solution)/shard_map/ppermute | solution.py:25
  86.5 4.3 %collective-permute-done.36 = f32[128,128]{1,0:T(8,128)S(1)} collective-permute-done((f32[128,128]{1,0:T(8,128)S(1)}, f32[128,128]{1,0:T(8,128)S(1)}, u32[]{:S(2)}, u32[]{:S(2)}) %collective-permute-start.36) | collective-permute-done | bytes 65568 | tf_op jit(solution)/shard_map/ppermute | solution.py:25
  90.8 2.4 %collective-permute-start.37 = (f32[128,128]{1,0:T(8,128)S(1)}, f32[128,128]{1,0:T(8,128)S(1)}, u32[]{:S(2)}, u32[]{:S(2)}) collective-permute-start(f32[128,128]{1,0:T(8,128)S(1)} %add.177), channel_id=1, source_target_pairs={{0,8},{4,12},{8,0},{12,4},{16,24},{20,28},{24,16},{28,20},{1,9},{5... | collective-permute-start | bytes 196616 | tf_op jit(solution)/shard_map/ppermute | solution.py:25
  93.2 2.2 %collective-permute-done.37 = f32[128,128]{1,0:T(8,128)S(1)} collective-permute-done((f32[128,128]{1,0:T(8,128)S(1)}, f32[128,128]{1,0:T(8,128)S(1)}, u32[]{:S(2)}, u32[]{:S(2)}) %collective-permute-start.37) | collective-permute-done | bytes 65568 | tf_op jit(solution)/shard_map/ppermute | solution.py:25
  95.5 1.6 %collective-permute-start.38 = (f32[128,128]{1,0:T(8,128)S(1)}, f32[128,128]{1,0:T(8,128)S(1)}, u32[]{:S(2)}, u32[]{:S(2)}) collective-permute-start(f32[128,128]{1,0:T(8,128)S(1)} %add.178), channel_id=1, source_target_pairs={{0,16},{4,20},{8,24},{12,28},{16,0},{20,4},{24,8},{28,12},{1,17},{... | collective-permute-start | bytes 196616 | tf_op jit(solution)/shard_map/ppermute | solution.py:25
  97.1 4.2 %shard_map.128 = (f32[2,192,384]{2,1,0:T(8,128)S(1)}, f32[4,2,128,128]{3,2,1,0:T(8,128)S(1)}) custom-call(s32[6]{0:T(128)S(1)} %reshape.225.place, f32[2,2,128,128]{3,2,1,0:T(8,128)S(1)} %get-tuple-element.116.patch, f32[4,2,128,128]{3,2,1,0:T(8,128)S(1)} %pad_maximum_fusion.2.probes, f32[2,128,128]{2,1,0:T(8,128)S(1)} %copy-done, ...), custom_call_target="tpu_custom_call" | custom-call | flops 1610612736 | bytes 4194304 | tf_op jit(solution)/shard_map/pallas_call | solution.py:251
  101.5 2.4 %collective-permute-start.26 = (f32[2,192,128]{2,1,0:T(8,128)S(1)}, f32[2,192,128]{2,1,0:T(8,128)S(1)}, u32[]{:S(2)}, u32[]{:S(2)}) collective-permute-start(f32[2,192,128]{2,1,0:T(8,128)S(1)} %slice.208), channel_id=1, source_target_pairs={{0,1},{1,2},{2,3},{4,5},{5,6},{6,7},{8,9},{9,10},{10,11},{12,13},{... | collective-permute-start | bytes 589832 | tf_op jit(solution)/shard_map/ppermute | solution.py:21
  105.5 5.1 %collective-permute-done.30 = f32[1,2,128,128]{3,2,1,0:T(8,128)S(1)} collective-permute-done((f32[1,2,128,128]{3,2,1,0:T(8,128)S(1)}, f32[1,2,128,128]{3,2,1,0:T(8,128)S(1)}, u32[]{:S(2)}, u32[]{:S(2)}) %collective-permute-start.30) | collective-permute-done | bytes 131104 | tf_op jit(solution)/shard_map/ppermute | solution.py:25
  111.8 2.8 %collective-permute-start.27 = (f32[2,64,256]{2,1,0:T(8,128)S(1)}, f32[2,64,256]{2,1,0:T(8,128)S(1)}, u32[]{:S(2)}, u32[]{:S(2)}) collective-permute-start(f32[2,64,256]{2,1,0:T(8,128)S(1)} %get-tuple-element.122), channel_id=1, source_target_pairs={{0,4},{4,8},{8,12},{12,16},{16,20},{20,24},{24,28},{1,5},{5,9},{9,... | collective-permute-start | bytes 393224 | tf_op jit(solution)/shard_map/ppermute | solution.py:21
  114.6 3.3 %collective-permute-start.28 = (f32[2,64,256]{2,1,0:T(8,128)S(1)}, f32[2,64,256]{2,1,0:T(8,128)S(1)}, u32[]{:S(2)}, u32[]{:S(2)}) collective-permute-start(f32[2,64,256]{2,1,0:T(8,128)S(1)} %get-tuple-element.123), channel_id=1, source_target_pairs={{0,8},{4,12},{8,16},{12,20},{16,24},{20,28},{1,9},{5,13},{9,17},{1... | collective-permute-start | bytes 393224 | tf_op jit(solution)/shard_map/ppermute | solution.py:21
  118.6 5.1 %collective-permute-done.32 = f32[1,2,128,128]{3,2,1,0:T(8,128)S(1)} collective-permute-done((f32[1,2,128,128]{3,2,1,0:T(8,128)S(1)}, f32[1,2,128,128]{3,2,1,0:T(8,128)S(1)}, u32[]{:S(2)}, u32[]{:S(2)}) %collective-permute-start.32) | collective-permute-done | bytes 131104 | tf_op jit(solution)/shard_map/ppermute | solution.py:25
  123.6 1.8 %collective-permute-start.33 = (f32[1,2,128,128]{3,2,1,0:T(8,128)S(1)}, f32[1,2,128,128]{3,2,1,0:T(8,128)S(1)}, u32[]{:S(2)}, u32[]{:S(2)}) collective-permute-start(f32[1,2,128,128]{3,2,1,0:T(8,128)S(1)} %add.173), channel_id=1, source_target_pairs={{0,16},{4,20},{8,24},{12,28},{16,0},{20,4},{24,8},{28,12},{1,17},{... | collective-permute-start | bytes 393224 | tf_op jit(solution)/shard_map/ppermute | solution.py:25
  126.1 5.9 %collective-permute-done.33 = f32[1,2,128,128]{3,2,1,0:T(8,128)S(1)} collective-permute-done((f32[1,2,128,128]{3,2,1,0:T(8,128)S(1)}, f32[1,2,128,128]{3,2,1,0:T(8,128)S(1)}, u32[]{:S(2)}, u32[]{:S(2)}) %collective-permute-start.33) | collective-permute-done | bytes 131104 | tf_op jit(solution)/shard_map/ppermute | solution.py:25
  (129 shorter events, 22.9 us)
Async XLA Ops:
  0.6 20.1 %collective-permute-start.1 = (f32[2,64,256]{2,1,0:T(8,128)}, f32[2,64,256]{2,1,0:T(8,128)S(1)}, u32[]{:S(2)}, u32[]{:S(2)}) collective-permute-start(f32[2,64,256]{2,1,0:T(8,128)} %param.29), channel_id=1, source_target_pairs={{8,0},{12,4},{16,8},{20,12},{24,16},{28,20},{9,1},{13,5},{17,9},{2... | collective-permute-start | bytes 393224 | tf_op jit(solution)/shard_map/ppermute | solution.py:21
  1.9 18.8 %collective-permute-start = (f32[2,64,256]{2,1,0:T(8,128)}, f32[2,64,256]{2,1,0:T(8,128)S(1)}, u32[]{:S(2)}, u32[]{:S(2)}) collective-permute-start(f32[2,64,256]{2,1,0:T(8,128)} %param.29), channel_id=1, source_target_pairs={{4,0},{8,4},{12,8},{16,12},{20,16},{24,20},{28,24},{5,1},{9,5},{13... | collective-permute-start | bytes 393224 | tf_op jit(solution)/shard_map/ppermute | solution.py:21
  4.7 6.1 %collective-permute-start.8 = (s32[2,3]{1,0:T(2,128)S(1)}, s32[2,3]{1,0:T(2,128)S(1)}, u32[]{:S(2)}, u32[]{:S(2)}) collective-permute-start(s32[2,3]{1,0:T(2,128)S(1)} %pad_add_fusion.1), channel_id=1, source_target_pairs={{0,1},{1,2},{2,3},{4,5},{5,6},{6,7},{8,9},{9,10},{10,11},{12,13},{... | collective-permute-start | bytes 80 | tf_op jit(solution)/shard_map/ppermute | solution.py:21
  7.1 13.6 %collective-permute-start.3 = (f32[1,2,128,128]{3,2,1,0:T(8,128)}, f32[1,2,128,128]{3,2,1,0:T(8,128)S(1)}, u32[]{:S(2)}, u32[]{:S(2)}) collective-permute-start(f32[1,2,128,128]{3,2,1,0:T(8,128)} %param.30), channel_id=1, source_target_pairs={{0,2},{1,3},{2,0},{3,1},{4,6},{5,7},{6,4},{7,5},{8,10},{9,11},{10,... | collective-permute-start | bytes 393224 | tf_op jit(solution)/shard_map/ppermute | solution.py:25
  11.5 10.6 %collective-permute-start.10 = (s32[2,2,3]{2,1,0:T(2,128)S(1)}, s32[2,2,3]{2,1,0:T(2,128)S(1)}, u32[]{:S(2)}, u32[]{:S(2)}) collective-permute-start(s32[2,2,3]{2,1,0:T(2,128)S(1)} %add_select_fusion), channel_id=1, source_target_pairs={{0,8},{4,12},{8,16},{12,20},{16,24},{20,28},{1,9},{5,13},{9,17},{1... | collective-permute-start | bytes 152 | tf_op jit(solution)/shard_map/ppermute | solution.py:21
  17.0 19.3 %collective-permute-start.9 = (s32[2,2,3]{2,1,0:T(2,128)S(1)}, s32[2,2,3]{2,1,0:T(2,128)S(1)}, u32[]{:S(2)}, u32[]{:S(2)}) collective-permute-start(s32[2,2,3]{2,1,0:T(2,128)S(1)} %add_select_fusion), channel_id=1, source_target_pairs={{0,4},{4,8},{8,12},{12,16},{16,20},{20,24},{24,28},{1,5},{5,9},{9,... | collective-permute-start | bytes 152 | tf_op jit(solution)/shard_map/ppermute | solution.py:21
  20.7 8.6 %collective-permute-start.4 = (f32[2,2,128,128]{3,2,1,0:T(8,128)S(1)}, f32[2,2,128,128]{3,2,1,0:T(8,128)S(1)}, u32[]{:S(2)}, u32[]{:S(2)}) collective-permute-start(f32[2,2,128,128]{3,2,1,0:T(8,128)S(1)} %pad_maximum_fusion.3), channel_id=1, source_target_pairs={{0,1},{1,0},{2,3},{3,2},{4,5},{5,4},{6,7},{7,6},{8,9},{9,8},{10,11... | collective-permute-start | bytes 786440 | tf_op jit(solution)/shard_map/ppermute | solution.py:25
  25.0 11.2 %collective-permute-start.19 = (f32[128,128]{1,0:T(8,128)S(1)}, f32[128,128]{1,0:T(8,128)S(1)}, u32[]{:S(2)}, u32[]{:S(2)}) collective-permute-start(f32[128,128]{1,0:T(8,128)S(1)} %get-tuple-element.118), channel_id=1, source_target_pairs={{0,1},{1,0},{2,3},{3,2},{4,5},{5,4},{6,7},{7,6},{8,9},{9,8},{10,11... | collective-permute-start | bytes 196616 | tf_op jit(solution)/shard_map/ppermute | solution.py:25
  33.5 13.5 %collective-permute-start.5 = (f32[2,192,128]{2,1,0:T(8,128)S(1)}, f32[2,192,128]{2,1,0:T(8,128)S(1)}, u32[]{:S(2)}, u32[]{:S(2)}) collective-permute-start(f32[2,192,128]{2,1,0:T(8,128)S(1)} %slice.197), channel_id=1, source_target_pairs={{0,1},{1,2},{2,3},{4,5},{5,6},{6,7},{8,9},{9,10},{10,11},{12,13},{... | collective-permute-start | bytes 589832 | tf_op jit(solution)/shard_map/ppermute | solution.py:21
  36.4 10.6 %collective-permute-start.14 = (f32[2,2,128,128]{3,2,1,0:T(8,128)S(1)}, f32[2,2,128,128]{3,2,1,0:T(8,128)S(1)}, u32[]{:S(2)}, u32[]{:S(2)}) collective-permute-start(f32[2,2,128,128]{3,2,1,0:T(8,128)S(1)} %slice.203), channel_id=1, source_target_pairs={{0,1},{1,0},{2,3},{3,2},{4,5},{5,4},{6,7},{7,6},{8,9},{9,8},{10,11... | collective-permute-start | bytes 786440 | tf_op jit(solution)/shard_map/ppermute | solution.py:25
  40.6 4.7 %collective-permute-start.21 = (f32[128,128]{1,0:T(8,128)S(1)}, f32[128,128]{1,0:T(8,128)S(1)}, u32[]{:S(2)}, u32[]{:S(2)}) collective-permute-start(f32[128,128]{1,0:T(8,128)S(1)} %add.159), channel_id=1, source_target_pairs={{0,4},{4,0},{8,12},{12,8},{16,20},{20,16},{24,28},{28,24},{1,5},{5... | collective-permute-start | bytes 196616 | tf_op jit(solution)/shard_map/ppermute | solution.py:25
  45.4 9.7 %collective-permute-start.22 = (f32[128,128]{1,0:T(8,128)S(1)}, f32[128,128]{1,0:T(8,128)S(1)}, u32[]{:S(2)}, u32[]{:S(2)}) collective-permute-start(f32[128,128]{1,0:T(8,128)S(1)} %add.160), channel_id=1, source_target_pairs={{0,8},{4,12},{8,0},{12,4},{16,24},{20,28},{24,16},{28,20},{1,9},{5... | collective-permute-start | bytes 196616 | tf_op jit(solution)/shard_map/ppermute | solution.py:25
  47.1 7.6 %collective-permute-start.15 = (f32[1,2,128,128]{3,2,1,0:T(8,128)S(1)}, f32[1,2,128,128]{3,2,1,0:T(8,128)S(1)}, u32[]{:S(2)}, u32[]{:S(2)}) collective-permute-start(f32[1,2,128,128]{3,2,1,0:T(8,128)S(1)} %slice.221), channel_id=1, source_target_pairs={{0,2},{1,3},{2,0},{3,1},{4,6},{5,7},{6,4},{7,5},{8,10},{9,11},{10,... | collective-permute-start | bytes 393224 | tf_op jit(solution)/shard_map/ppermute | solution.py:25
  48.2 11.9 %collective-permute-start.6 = (f32[2,64,256]{2,1,0:T(8,128)S(1)}, f32[2,64,256]{2,1,0:T(8,128)S(1)}, u32[]{:S(2)}, u32[]{:S(2)}) collective-permute-start(f32[2,64,256]{2,1,0:T(8,128)S(1)} %get-tuple-element.124), channel_id=1, source_target_pairs={{0,4},{4,8},{8,12},{12,16},{16,20},{20,24},{24,28},{1,5},{5,9},{9,... | collective-permute-start | bytes 393224 | tf_op jit(solution)/shard_map/ppermute | solution.py:21
  52.3 7.7 %collective-permute-start.7 = (f32[2,64,256]{2,1,0:T(8,128)S(1)}, f32[2,64,256]{2,1,0:T(8,128)S(1)}, u32[]{:S(2)}, u32[]{:S(2)}) collective-permute-start(f32[2,64,256]{2,1,0:T(8,128)S(1)} %get-tuple-element.125), channel_id=1, source_target_pairs={{0,8},{4,12},{8,16},{12,20},{16,24},{20,28},{1,9},{5,13},{9,17},{1... | collective-permute-start | bytes 393224 | tf_op jit(solution)/shard_map/ppermute | solution.py:21
  54.7 5.0 %collective-permute-start.16 = (f32[1,2,128,128]{3,2,1,0:T(8,128)S(1)}, f32[1,2,128,128]{3,2,1,0:T(8,128)S(1)}, u32[]{:S(2)}, u32[]{:S(2)}) collective-permute-start(f32[1,2,128,128]{3,2,1,0:T(8,128)S(1)} %slice_add_fusion.4), channel_id=1, source_target_pairs={{0,4},{4,0},{8,12},{12,8},{16,20},{20,16},{24,28},{28,24},{1,5},{5... | collective-permute-start | bytes 393224 | tf_op jit(solution)/shard_map/ppermute | solution.py:25
  55.0 13.9 %collective-permute-start.23 = (f32[128,128]{1,0:T(8,128)S(1)}, f32[128,128]{1,0:T(8,128)S(1)}, u32[]{:S(2)}, u32[]{:S(2)}) collective-permute-start(f32[128,128]{1,0:T(8,128)S(1)} %add.161), channel_id=1, source_target_pairs={{0,16},{4,20},{8,24},{12,28},{16,0},{20,4},{24,8},{28,12},{1,17},{... | collective-permute-start | bytes 196616 | tf_op jit(solution)/shard_map/ppermute | solution.py:25
  59.8 6.3 %collective-permute-start.17 = (f32[1,2,128,128]{3,2,1,0:T(8,128)S(1)}, f32[1,2,128,128]{3,2,1,0:T(8,128)S(1)}, u32[]{:S(2)}, u32[]{:S(2)}) collective-permute-start(f32[1,2,128,128]{3,2,1,0:T(8,128)S(1)} %add.155), channel_id=1, source_target_pairs={{0,8},{4,12},{8,0},{12,4},{16,24},{20,28},{24,16},{28,20},{1,9},{5... | collective-permute-start | bytes 393224 | tf_op jit(solution)/shard_map/ppermute | solution.py:25
  60.1 8.9 %collective-permute-start.12 = (f32[2,64,256]{2,1,0:T(8,128)S(1)}, f32[2,64,256]{2,1,0:T(8,128)S(1)}, u32[]{:S(2)}, u32[]{:S(2)}) collective-permute-start(f32[2,64,256]{2,1,0:T(8,128)S(1)} %fusion.5), channel_id=1, source_target_pairs={{8,0},{12,4},{16,8},{20,12},{24,16},{28,20},{9,1},{13,5},{17,9},{2... | collective-permute-start | bytes 393224 | tf_op jit(solution)/shard_map/ppermute | solution.py:21
  61.4 7.6 %collective-permute-start.11 = (f32[2,64,256]{2,1,0:T(8,128)S(1)}, f32[2,64,256]{2,1,0:T(8,128)S(1)}, u32[]{:S(2)}, u32[]{:S(2)}) collective-permute-start(f32[2,64,256]{2,1,0:T(8,128)S(1)} %fusion.5), channel_id=1, source_target_pairs={{4,0},{8,4},{12,8},{16,12},{20,16},{24,20},{28,24},{5,1},{9,5},{13... | collective-permute-start | bytes 393224 | tf_op jit(solution)/shard_map/ppermute | solution.py:21
  66.2 10.5 %collective-permute-start.18 = (f32[1,2,128,128]{3,2,1,0:T(8,128)S(1)}, f32[1,2,128,128]{3,2,1,0:T(8,128)S(1)}, u32[]{:S(2)}, u32[]{:S(2)}) collective-permute-start(f32[1,2,128,128]{3,2,1,0:T(8,128)S(1)} %add.156), channel_id=1, source_target_pairs={{0,16},{4,20},{8,24},{12,28},{16,0},{20,4},{24,8},{28,12},{1,17},{... | collective-permute-start | bytes 393224 | tf_op jit(solution)/shard_map/ppermute | solution.py:25
  69.0 8.2 %collective-permute-start.13 = (f32[2,192,128]{2,1,0:T(8,128)S(1)}, f32[2,192,128]{2,1,0:T(8,128)S(1)}, u32[]{:S(2)}, u32[]{:S(2)}) collective-permute-start(f32[2,192,128]{2,1,0:T(8,128)S(1)} %pad_maximum_fusion.5), channel_id=1, source_target_pairs={{1,0},{2,1},{3,2},{5,4},{6,5},{7,6},{9,8},{10,9},{11,10},{13,12},{... | collective-permute-start | bytes 589832 | tf_op jit(solution)/shard_map/ppermute | solution.py:21
  76.7 5.0 %collective-permute-start.24 = (f32[1,2,128,128]{3,2,1,0:T(8,128)S(1)}, f32[1,2,128,128]{3,2,1,0:T(8,128)S(1)}, u32[]{:S(2)}, u32[]{:S(2)}) collective-permute-start(f32[1,2,128,128]{3,2,1,0:T(8,128)S(1)} %divide_add_fusion.1), channel_id=1, source_target_pairs={{0,2},{1,3},{2,0},{3,1},{4,6},{5,7},{6,4},{7,5},{8,10},{9,11},{10,... | collective-permute-start | bytes 393224 | tf_op jit(solution)/shard_map/ppermute | solution.py:25
  81.8 15.3 %collective-permute-start.25 = (f32[2,2,128,128]{3,2,1,0:T(8,128)S(1)}, f32[2,2,128,128]{3,2,1,0:T(8,128)S(1)}, u32[]{:S(2)}, u32[]{:S(2)}) collective-permute-start(f32[2,2,128,128]{3,2,1,0:T(8,128)S(1)} %pad_maximum_fusion.4), channel_id=1, source_target_pairs={{0,1},{1,0},{2,3},{3,2},{4,5},{5,4},{6,7},{7,6},{8,9},{9,8},{10,11... | collective-permute-start | bytes 786440 | tf_op jit(solution)/shard_map/ppermute | solution.py:25
  90.8 4.7 %collective-permute-start.37 = (f32[128,128]{1,0:T(8,128)S(1)}, f32[128,128]{1,0:T(8,128)S(1)}, u32[]{:S(2)}, u32[]{:S(2)}) collective-permute-start(f32[128,128]{1,0:T(8,128)S(1)} %add.177), channel_id=1, source_target_pairs={{0,8},{4,12},{8,0},{12,4},{16,24},{20,28},{24,16},{28,20},{1,9},{5... | collective-permute-start | bytes 196616 | tf_op jit(solution)/shard_map/ppermute | solution.py:25
  95.5 6.0 %collective-permute-start.38 = (f32[128,128]{1,0:T(8,128)S(1)}, f32[128,128]{1,0:T(8,128)S(1)}, u32[]{:S(2)}, u32[]{:S(2)}) collective-permute-start(f32[128,128]{1,0:T(8,128)S(1)} %add.178), channel_id=1, source_target_pairs={{0,16},{4,20},{8,24},{12,28},{16,0},{20,4},{24,8},{28,12},{1,17},{... | collective-permute-start | bytes 196616 | tf_op jit(solution)/shard_map/ppermute | solution.py:25
  105.1 5.5 %collective-permute-start.30 = (f32[1,2,128,128]{3,2,1,0:T(8,128)S(1)}, f32[1,2,128,128]{3,2,1,0:T(8,128)S(1)}, u32[]{:S(2)}, u32[]{:S(2)}) collective-permute-start(f32[1,2,128,128]{3,2,1,0:T(8,128)S(1)} %slice.226), channel_id=1, source_target_pairs={{0,2},{1,3},{2,0},{3,1},{4,6},{5,7},{6,4},{7,5},{8,10},{9,11},{10,... | collective-permute-start | bytes 393224 | tf_op jit(solution)/shard_map/ppermute | solution.py:25
  110.6 7.4 %collective-permute-start.31 = (f32[1,2,128,128]{3,2,1,0:T(8,128)S(1)}, f32[1,2,128,128]{3,2,1,0:T(8,128)S(1)}, u32[]{:S(2)}, u32[]{:S(2)}) collective-permute-start(f32[1,2,128,128]{3,2,1,0:T(8,128)S(1)} %slice_add_fusion.2), channel_id=1, source_target_pairs={{0,4},{4,0},{8,12},{12,8},{16,20},{20,16},{24,28},{28,24},{1,5},{5... | collective-permute-start | bytes 393224 | tf_op jit(solution)/shard_map/ppermute | solution.py:25
  111.8 13.6 %collective-permute-start.27 = (f32[2,64,256]{2,1,0:T(8,128)S(1)}, f32[2,64,256]{2,1,0:T(8,128)S(1)}, u32[]{:S(2)}, u32[]{:S(2)}) collective-permute-start(f32[2,64,256]{2,1,0:T(8,128)S(1)} %get-tuple-element.122), channel_id=1, source_target_pairs={{0,4},{4,8},{8,12},{12,16},{16,20},{20,24},{24,28},{1,5},{5,9},{9,... | collective-permute-start | bytes 393224 | tf_op jit(solution)/shard_map/ppermute | solution.py:21
  114.6 10.8 %collective-permute-start.28 = (f32[2,64,256]{2,1,0:T(8,128)S(1)}, f32[2,64,256]{2,1,0:T(8,128)S(1)}, u32[]{:S(2)}, u32[]{:S(2)}) collective-permute-start(f32[2,64,256]{2,1,0:T(8,128)S(1)} %get-tuple-element.123), channel_id=1, source_target_pairs={{0,8},{4,12},{8,16},{12,20},{16,24},{20,28},{1,9},{5,13},{9,17},{1... | collective-permute-start | bytes 393224 | tf_op jit(solution)/shard_map/ppermute | solution.py:21
  118.0 5.6 %collective-permute-start.32 = (f32[1,2,128,128]{3,2,1,0:T(8,128)S(1)}, f32[1,2,128,128]{3,2,1,0:T(8,128)S(1)}, u32[]{:S(2)}, u32[]{:S(2)}) collective-permute-start(f32[1,2,128,128]{3,2,1,0:T(8,128)S(1)} %add.172), channel_id=1, source_target_pairs={{0,8},{4,12},{8,0},{12,4},{16,24},{20,28},{24,16},{28,20},{1,9},{5... | collective-permute-start | bytes 393224 | tf_op jit(solution)/shard_map/ppermute | solution.py:25
  123.6 8.4 %collective-permute-start.33 = (f32[1,2,128,128]{3,2,1,0:T(8,128)S(1)}, f32[1,2,128,128]{3,2,1,0:T(8,128)S(1)}, u32[]{:S(2)}, u32[]{:S(2)}) collective-permute-start(f32[1,2,128,128]{3,2,1,0:T(8,128)S(1)} %add.173), channel_id=1, source_target_pairs={{0,16},{4,20},{8,24},{12,28},{16,0},{20,4},{24,8},{28,12},{1,17},{... | collective-permute-start | bytes 393224 | tf_op jit(solution)/shard_map/ppermute | solution.py:25
  (15 other events, 48.8 us)

commit v2 on v1

v2 whole, which is shorter than its diff:
```python
import functools
import math

import jax
import jax.numpy as jnp
import numpy as np
from jax import lax
from jax.experimental import pallas as pl
from jax.experimental.pallas import tpu as pltpu
from jax.sharding import PartitionSpec as P

ITERS = 2
SUBLANES, LANES = 8, 128
F32 = jnp.float32
BF16 = jnp.bfloat16
TABLE = 8


def shifted(value, axis, steps):
    count = lax.axis_size(axis)
    initial, last = (max(0, -steps), min(count, count - steps))
    return lax.ppermute(value, axis, [(source, source + steps) for source in range(initial, last)])


def swapped(value, axis, bit):
    return lax.ppermute(value, axis, [(i, i ^ bit) for i in range(lax.axis_size(axis))])


def paired(value, axis, step, phase):
    lower = [i for i in range(lax.axis_size(axis) - step) if i // step % 2 == phase]
    return lax.ppermute(value, axis, [(i, i + step) for i in lower] + [(i + step, i) for i in lower])


def across(value, scan_bit, mode_bit):
    scans, modes = lax.axis_size("scan"), lax.axis_size("mode")
    other = scan_bit * modes + mode_bit
    return lax.ppermute(value, ("scan", "mode"), [(i, i ^ other) for i in range(scans * modes)])


def bits_of(axis):
    return [1 << b for b in range(lax.axis_size(axis).bit_length() - 1)]


def gathered(value, axis):
    for bit in reversed(bits_of(axis)):
        value = jnp.concatenate([value, swapped(value, axis, bit)], axis=0)
    return value


@functools.lru_cache
def fresnel_parts(length):
    ids = np.arange(length, dtype=np.int64)
    phase = ids[:, None] * ids[None, :] % length
    centred = ids - length // 2
    chirp = centred * centred % (4 * length)
    angle = -2.0 * math.pi / length * phase + math.pi / (2 * length) * chirp[None, :]
    real, imag = np.cos(angle) / math.sqrt(length), np.sin(angle) / math.sqrt(length)
    whole = np.block([[real, -imag], [imag, real]])
    parts = []
    for matrix in (whole, whole.T):
        high = matrix.astype(jnp.bfloat16)
        low = (matrix - high.astype(np.float64)).astype(jnp.bfloat16)
        parts.append(np.stack([high, low]))
    return np.stack(parts)


def split(value):
    high = value.astype(BF16)
    return high, (value - high.astype(F32)).astype(BF16)


def dot(a, b):
    return jnp.dot(a, b, preferred_element_type=F32)


def window_of(row, col):
    return (
        pl.multiple_of(row // SUBLANES * SUBLANES, SUBLANES),
        pl.multiple_of(col // LANES * LANES, LANES),
        row % SUBLANES,
        col % LANES,
    )


def cut(wide, down, right, length):
    wide = pltpu.roll(wide, 2 * LANES - right, 1)[:, :length]
    return pltpu.roll(wide, length + SUBLANES - down, 0)[:length]


def placed_in(term, down, right):
    tall = jnp.concatenate([term, jnp.zeros((SUBLANES, term.shape[1]), F32)], axis=0)
    tall = pltpu.roll(tall, down, 0)
    return pltpu.roll(jnp.concatenate([tall, jnp.zeros_like(tall)], axis=1), right, 1)


def patches_kernel(place, first, second, third, patch, density, extended):
    slots, _, length, _ = patch.shape
    rows = first.shape[1]
    for step, tile in enumerate((first, second, third)):
        extended[:, step * rows : (step + 1) * rows] = tile[...]
    total = None
    for slot in range(slots):
        row, col, used = place[3 * slot], place[3 * slot + 1], place[3 * slot + 2]
        top, left, down, right = window_of(row, col)
        here = 0.0
        for part in range(2):
            wide = extended[part, pl.ds(top, length + SUBLANES), pl.ds(left, 2 * LANES)]
            window = cut(wide, down, right, length)
            patch[slot, part] = window
            here = here + window * window
        here = here * used.astype(F32)
        total = here if total is None else total + here
    density[...] = total


def whole_probe(probes, k, part, parity):
    return jnp.concatenate([probes[k, parity, part], probes[k, 1 - parity, part]], axis=0)


def wave_kernel(place, me, patch, density, probes, amplitude, table, windows, *rest):
    (kept, sent, *terms), (sums, x_hi, x_lo, y_hi, y_lo, far, own_probe) = rest[:-7], rest[-7:]
    slots, _, length, _ = patch.shape
    modes = probes.shape[0]
    half = length // 2
    scan = me[0]
    parity = scan % 2

    def from_left(which):
        for k in range(modes):
            cols = slice(k * length, (k + 1) * length)
            hi, lo = x_hi[:, cols], x_lo[:, cols]
            out = dot(table[which, 0], hi) + dot(table[which, 0], lo) + dot(table[which, 1], hi)
            hi, lo = split(out)
            rows = slice(k * length, (k + 1) * length)
            y_hi[rows, :length], y_hi[rows, length:] = hi[:length], hi[length:]
            y_lo[rows, :length], y_lo[rows, length:] = lo[:length], lo[length:]

    def from_right(which, k):
        rows = slice(k * length, (k + 1) * length)
        hi, lo = y_hi[rows], y_lo[rows]
        return dot(hi, table[which, 0]) + dot(lo, table[which, 0]) + dot(hi, table[which, 1])

    def set_columns(k, real, imag):
        cols = slice(k * length, (k + 1) * length)
        hi, lo = split(real)
        x_hi[:length, cols], x_lo[:length, cols] = hi, lo
        hi, lo = split(imag)
        x_hi[length:, cols], x_lo[length:, cols] = hi, lo

    sums[...] = jnp.zeros_like(sums)
    for k in range(modes):
        for part in range(2):
            own_probe[k, part] = whole_probe(probes, k, part, parity)
    for slot in range(slots):
        row, col, used = place[3 * slot], place[3 * slot + 1], place[3 * slot + 2].astype(F32)
        obj_re, obj_im = patch[slot, 0], patch[slot, 1]
        for k in range(modes):
            pr, pi = own_probe[k, 0], own_probe[k, 1]
            set_columns(k, pr * obj_re - pi * obj_im, pr * obj_im + pi * obj_re)
        from_left(0)
        intensity = 0.0
        for k in range(modes):
            wave = from_right(1, k)
            far[k] = wave
            square = wave * wave
            intensity = intensity + square[:, :length] + square[:, length:]
        factor = amplitude[slot] / jnp.sqrt(jnp.maximum(intensity, 1.0))
        for k in range(modes):
            set_columns(k, far[k, :, :length] * factor, far[k, :, length:] * factor)
        from_left(1)
        num_re, num_im = 0.0, 0.0
        for k in range(modes):
            near = from_right(0, k)
            pr, pi = own_probe[k, 0], own_probe[k, 1]
            change_re = (near[:, :length] - (pr * obj_re - pi * obj_im)) * used
            change_im = (near[:, length:] - (pr * obj_im + pi * obj_re)) * used
            num_re = num_re + (pr * change_re + pi * change_im)
            num_im = num_im + (pr * change_im - pi * change_re)
            grad_re = obj_re * change_re + obj_im * change_im
            grad_im = obj_re * change_im - obj_im * change_re
            out, at = (kept, k) if k < modes // 2 else (sent, k - modes // 2)
            for part, grad in enumerate((grad_re, grad_im)):
                for top in range(2):
                    where = (at, parity ^ top, slice(part * half, (part + 1) * half))
                    piece = grad[top * half : (top + 1) * half]
                    out[where] = piece if slot == 0 else out[where] + piece
        top, left, down, right = window_of(row, col)
        for part, term in enumerate((num_re, num_im)):
            sums[part, pl.ds(top, length + SUBLANES), pl.ds(left, 2 * LANES)] += placed_in(term, down, right)
    for out in (kept, sent):
        for at in range(modes // 2):
            for top in range(2):
                out[at, parity ^ top, 2 * half :] = density[top * half : (top + 1) * half]
    terms, rims = terms[:3], terms[3:]
    data_rows = terms[0].shape[0] - windows.shape[0]
    tile_rows = data_rows // 2
    for step, out in enumerate(terms):
        for part in range(2):
            out[part * tile_rows : (part + 1) * tile_rows] = sums[part, step * tile_rows : (step + 1) * tile_rows]
        out[data_rows:] = jnp.zeros((windows.shape[0], out.shape[1]), F32)
        out[data_rows:, LANES : 2 * LANES] = windows[...]
    for phase, rim in enumerate(rims):
        right = ((me[1] + phase) % 2 == 0).astype(jnp.int32)
        start = pl.multiple_of(right * (sums.shape[2] - length), LANES)
        for step in range(3):
            for part in range(2):
                at = (2 * step + part) * tile_rows
                rim[at : at + tile_rows] = sums[part, step * tile_rows : (step + 1) * tile_rows, pl.ds(start, length)]
        rim[3 * data_rows :] = windows[...]


def weight_of(table, me, probes, grid, scan_steps, mode_steps, rows, cols, tile_rows, band_cols, acc):
    modes, length = probes.shape[0], probes.shape[-1]
    above, left = (acc.shape[0] - rows - length, acc.shape[1] - cols - length)
    scan, mode = me[0], me[1]
    power = 0.0
    for k in range(modes):
        real, imag = (whole_probe(probes, k, part, scan % 2) for part in range(2))
        power = power + (real * real + imag * imag)
    acc[...] = jnp.zeros_like(acc)
    for ds in scan_steps:
        for dm in mode_steps:
            inside = (scan + ds >= 0) & (scan + ds < grid[0]) & (mode + dm >= 0) & (mode + dm < grid[1])
            first = jnp.where(inside, (scan + ds) * grid[1] + mode + dm, 0) * TABLE
            for slot in range(TABLE // 3):
                row = table[first + 3 * slot] - scan * tile_rows
                col = table[first + 3 * slot + 1] - mode * band_cols
                used = inside & (table[first + 3 * slot + 2] > 0)
                used &= (row > -length) & (row < rows) & (col > -length) & (col < cols)

                @pl.when(used)
                def _():
                    top, before, down, right = window_of(row + above, col + left)
                    acc[pl.ds(top, length + SUBLANES), pl.ds(before, 2 * LANES)] += placed_in(power, down, right)

    return acc[pl.ds(above, rows), pl.ds(left, cols)] + 1.0


def inner_kernel(grid, band_cols, table, me, first, third, probes, inner, outer, from_a, from_b, new_first, new_third, passed, acc):
    _, tile_rows, cols = first.shape
    scan, mode = me[0], me[1]
    weight = weight_of(
        table, me, probes, grid, range(-2, 3), range(-1, 2), 3 * tile_rows, cols, tile_rows, band_cols, acc
    )
    lower = (scan // 2 % 2 == 0).astype(F32)
    inside = jnp.where(lax.broadcasted_iota(jnp.int32, (tile_rows, cols), 1) < (grid[1] - mode) * band_cols, 1.0, 0.0)
    beyond = inside * (scan + 2 < grid[0]).astype(F32)
    is_first = (scan % 2).astype(F32)
    for part in range(2):
        rows = slice(part * tile_rows, (part + 1) * tile_rows)
        a, b = from_a[rows], from_b[rows]
        own = inner[rows] + (b * lower + a * (1.0 - lower))
        own = first[part] + inside * own / weight[:tile_rows]
        after = outer[rows] + (a * lower + b * (1.0 - lower))
        after = third[part] + beyond * after / weight[2 * tile_rows :]
        new_first[part], new_third[part] = own, after
        passed[part] = own * is_first + after * (1.0 - is_first)


def last_kernel(grid, table, me, probes, weight, acc):
    rows, cols = weight.shape
    weight[...] = weight_of(table, me, probes, grid, range(-2, 1), range(-1, 1), rows, cols, rows, cols, acc)


VMEM = pl.BlockSpec(memory_space=pltpu.VMEM)
SMEM = pl.BlockSpec(memory_space=pltpu.SMEM)


def call(kernel, out_shape, in_specs, scratch=(), flops=0, moved=0):
    return pl.pallas_call(
        kernel,
        out_shape=out_shape,
        in_specs=in_specs,
        out_specs=jax.tree.map(lambda _: VMEM, out_shape),
        scratch_shapes=list(scratch),
        compiler_params=pltpu.CompilerParams(vmem_limit_bytes=16 * 2**20),
        cost_estimate=pl.CostEstimate(flops=flops, bytes_accessed=moved, transcendentals=0),
    )


def local(object_field, probe, amplitude, offsets, counts):
    tile_rows, band_cols = object_field.shape[1:]
    scans, modes = lax.axis_size("scan"), lax.axis_size("mode")
    scan, mode = lax.axis_index("scan"), lax.axis_index("mode")
    length = probe.shape[2]
    slots = amplitude.shape[0]
    reach = -(-length // tile_rows)
    ext_rows, ext_cols = tile_rows + length, band_cols + length
    table = jnp.asarray(fresnel_parts(length))
    used = (jnp.arange(slots, dtype=jnp.int32) < counts[0]).astype(jnp.int32)
    corner = jnp.stack([scan * tile_rows, mode * band_cols]).astype(jnp.int32)
    place = jnp.concatenate([offsets - corner, used[:, None]], axis=1).reshape(-1)

    me = jnp.stack([scan, mode]).astype(jnp.int32)
    parity = scan % 2
    near, far = bits_of("mode")
    half = length // 2

    entry = jnp.concatenate([offsets, used[:, None]], axis=1).reshape(-1)
    entry = jnp.pad(entry, (0, TABLE - entry.shape[0])).astype(F32)
    table_rows = -(-scans * modes * TABLE // (SUBLANES * LANES)) * SUBLANES
    blocks = jnp.arange(table_rows * LANES // TABLE)
    windows = jnp.where((blocks == scan * modes + mode)[:, None], entry[None, :], 0.0).reshape(-1, LANES)
    data_rows = 2 * tile_rows
    even, odd = (parity == 0).astype(F32), (parity == 1).astype(F32)
    even_mode = (mode % 2 == 0).astype(F32)
    lower = (scan // 2 % 2 == 0).astype(F32)

    def sds(*shape):
        return jax.ShapeDtypeStruct(shape, F32)

    def as_halves(value):
        value = value.reshape(value.shape[0], 2, 2, half, length).swapaxes(1, 2)
        return jnp.where(parity == 0, value, value[:, ::-1])

    def scratch(rows, cols):
        return [pltpu.VMEM((reach * tile_rows + rows + length, band_cols + cols + length), F32)]

    def inner_update(first, third, probes, terms, rims):
        a, b = (paired(rim, "mode", 1, phase) for phase, rim in enumerate(rims))
        left, right = b * even_mode + a * (1.0 - even_mode), a * even_mode + b * (1.0 - even_mode)
        joined = []
        for step, term in enumerate(terms):
            rows = slice(step * data_rows, (step + 1) * data_rows)
            parts = [term[:data_rows, :length] + left[rows], term[:data_rows, length:band_cols], term[:data_rows, band_cols:] + right[rows]]
            joined.append(jnp.concatenate(parts, axis=1))
        here = terms[0][data_rows:, LANES : 2 * LANES] + (a + b)[3 * data_rows :]
        here = jnp.pad(here, ((0, 0), (0, ext_cols - LANES)))
        arrived = swapped(jnp.concatenate([joined[1], here]), "scan", 1)
        entries = here + arrived[data_rows:]
        inner = joined[0] + arrived[:data_rows] * odd
        outer = joined[2] + arrived[:data_rows] * even
        a = paired(jnp.concatenate([outer * lower + inner * (1.0 - lower), entries]), "scan", 2, 0)
        b = paired(jnp.concatenate([inner * lower + outer * (1.0 - lower), entries]), "scan", 2, 1)
        entries = (entries + a[data_rows:] + b[data_rows:])[:, :LANES].astype(jnp.int32).reshape(-1)
        first, third, passed = call(
            functools.partial(inner_kernel, (scans, modes), band_cols),
            [sds(2, tile_rows, ext_cols)] * 3,
            [SMEM, SMEM] + [VMEM] * 7,
            scratch(3 * tile_rows, ext_cols),
            flops=2**20,
            moved=2**20,
        )(entries, me, first, third, probes, inner, outer, a, b)
        return first, third, passed, entries

    def last_update(tile, probes, terms, entries):
        arrived = swapped(terms[1][:data_rows], "scan", 1)
        third = terms[2][:data_rows] + arrived * even
        first = terms[0][:data_rows] + arrived * odd + shifted(third, "scan", 2)
        return first

    def last_part(tile, probes, first, entries):
        weight = call(
            functools.partial(last_kernel, (scans, modes)),
            sds(tile_rows, band_cols),
            [SMEM, SMEM, VMEM],
            scratch(tile_rows, band_cols),
            flops=2**20,
            moved=2**20,
        )(entries, me, probes)
        margin = shifted(first[:, band_cols:], "mode", 1)
        terms = jnp.concatenate([first[:, :length] + margin, first[:, length:band_cols]], axis=1)
        return tile[:, :, :band_cols] + terms.reshape(2, tile_rows, band_cols) / weight

    probes = gathered(as_halves(probe), "mode")
    tiles = [object_field, shifted(object_field, "scan", -1), shifted(object_field, "scan", -2)]
    tiles = jnp.concatenate(tiles, axis=1)
    tiles = jnp.concatenate([tiles, shifted(tiles[:, :, :length], "mode", -1)], axis=2)
    first, second, third = (tiles[:, step * tile_rows : (step + 1) * tile_rows] for step in range(3))
    for iteration in range(ITERS):
        last = iteration == ITERS - 1
        patch, density = call(
            patches_kernel,
            (sds(slots, 2, length, length), sds(length, length)),
            [SMEM] + [VMEM] * 3,
            [pltpu.VMEM((2, ext_rows, ext_cols), F32)],
            flops=2**20,
            moved=2**20,
        )(place, first, second, third)
        rows_out = data_rows + table_rows
        kept, sent, *terms = call(
            wave_kernel,
            (*[sds(modes // 2, 2, 3 * half, length)] * 2, *[sds(rows_out, ext_cols)] * 3, *[sds(2 * data_rows + rows_out, length)] * (0 if last else 2)),
            [SMEM, SMEM] + [VMEM] * 6,
            [pltpu.VMEM((2, ext_rows, ext_cols), F32)]
            + [pltpu.VMEM((2 * length, modes * length), BF16)] * 2
            + [pltpu.VMEM((modes * length, 2 * length), BF16)] * 2
            + [pltpu.VMEM((modes, length, 2 * length), F32), pltpu.VMEM((modes, 2, length, length), F32)],
            flops=slots * modes * 4 * 3 * 2 * 4 * length**3,
            moved=4 * 2**20,
        )(place, me, patch, density, probes, amplitude, table, windows)
        kept = kept + swapped(sent, "mode", near)
        if last:
            kept, terms = lax.optimization_barrier((kept, terms))
        own = kept[0, 0] + across(kept[0, 1], 1, 0) + across(kept[1, 0], 0, far) + across(kept[1, 1], 1, far)
        for bit in bits_of("scan")[1:]:
            own = own + swapped(own, "scan", bit)
        if not last:
            first, third, passed, entries = inner_update(first, third, probes, terms[:3], terms[3:])
            own, passed = lax.optimization_barrier((own, passed))
        else:
            inner = last_update(first, probes, terms[:3], entries)
            own, inner = lax.optimization_barrier((own, inner))
        probe = probes[0, 0] + own[: 2 * half].reshape(2, half, length) / (own[2 * half :] + 1.0)
        if not last:
            second = swapped(passed, "scan", 1)
            probes = jnp.stack(
                [
                    jnp.stack([probe, across(probe, 1, 0)]),
                    jnp.stack([across(probe, 0, far), across(probe, 1, far)]),
                ]
            )
            probes, second = lax.optimization_barrier((probes, second))
            probes = jnp.concatenate([probes, swapped(probes, "mode", near)], axis=0)
        else:
            object_field = last_part(first, probes, inner, entries)
            probe = jnp.stack([probe, across(probe, 1, 0)])
            probe = jnp.where(parity == 0, probe, probe[::-1]).swapaxes(0, 1).reshape(1, 2, length, length)
    return (object_field, probe)


def solution(mesh):
    placed = (
        P(None, "scan", "mode"),
        P("mode", None, None, None),
        P(("scan", "mode"), None, None),
        P(("scan", "mode"), None),
        P(("scan", "mode")),
    )
    return jax.shard_map(
        local,
        mesh=mesh,
        in_specs=placed,
        out_specs=(P(None, "scan", "mode"), P("mode", None, None, None)),
        check_vma=False,
    )
```

time: 133 us -> 103 us (0.77)
  starting transfers between devices: 63.3 us -> 46.2 us
  waiting for transfers between devices: 50.3 us -> 33.4 us
    ppermute x15 -> x5, starting transfers between devices: 36.9 us -> 7.36 us  [shifted(): lax.ppermute(value, axis, [(source, source + steps) for source in range(i...]
    ppermute x24 -> x12, waiting for transfers between devices: 48.2 us -> 18.8 us  [swapped(): lax.ppermute(value, axis, [(i, i ^ bit) for i in range(lax.axis_size(axis...]
    ppermute x0 -> x14, starting transfers between devices: none -> 22.6 us  [the longest x10 14.6 us: across(): lax.ppermute(value, ('scan', 'mode'), [(i, i ^ other) for i in range(scan...]
    ppermute x0 -> x14, waiting for transfers between devices: none -> 10.3 us  [the longest x10 10.3 us: across(): lax.ppermute(value, ('scan', 'mode'), [(i, i ^ other) for i in range(scan...]
    ppermute x24 -> x12, starting transfers between devices: 26.4 us -> 16.2 us  [swapped(): lax.ppermute(value, axis, [(i, i ^ bit) for i in range(lax.axis_size(axis...]
    ppermute x15 -> x5, waiting for transfers between devices: 2.02 us -> 4.23 us  [shifted(): lax.ppermute(value, axis, [(source, source + steps) for source in range(i...]
  transfers between devices with their start and end apart: 39 -> 31, of which waited for: 13 -> 17; matrix products, arithmetic and copies ran while one was open for 2% -> 5% of each run, Pallas kernels for 9% -> 5%
where the time goes in v2:
time: 103 us; the launch traced here: 102 us
  starting transfers between devices  46.2 us (45%)
  waiting for transfers between devices  33.4 us (32%)
  Pallas kernels  13.1 us (13%)
  local copies, waits for them, and re-layouts  3.84 us (4%)
  other arithmetic  3.48 us (3%)
  between operations  1.8 us (2%)
    ppermute x12, waiting for transfers between devices, swapped(): lax.ppermute(value, axis, [(i, i ^ bit) for i in range(lax.axis_size(axis...  18.8 us
    ppermute x12, starting transfers between devices, swapped(): lax.ppermute(value, axis, [(i, i ^ bit) for i in range(lax.axis_size(axis...  16.2 us
    ppermute x10, starting transfers between devices, across(): lax.ppermute(value, ('scan', 'mode'), [(i, i ^ other) for i in range(scan...  14.6 us
    ppermute x10, waiting for transfers between devices, across(): lax.ppermute(value, ('scan', 'mode'), [(i, i ^ other) for i in range(scan...  10.3 us
    pallas_call x2, Pallas kernels, local(): call(wave_kernel, (*[sds(modes // 2, 2, 3 * half, length)] * 2, *[sds(row...  8.37 us
    ppermute x4, starting transfers between devices, paired(): lax.ppermute(value, axis, [(i, i + step) for i in lower] + [(i + step, i)...  8.08 us
    ppermute x5, starting transfers between devices, shifted(): lax.ppermute(value, axis, [(source, source + steps) for source in range(i...  7.36 us
    ppermute x5, waiting for transfers between devices, shifted(): lax.ppermute(value, axis, [(source, source + steps) for source in range(i...  4.23 us
  transfers between devices with their start and end apart: 31, of which 17 were waited for; matrix products, arithmetic and copies ran while one was open for 5% of the time, Pallas kernels for 5%

profile of v2, /device:TPU:0, one launch (start us, length us, event | category | flops | bytes accessed | tf_op | source)
XLA Modules:
  0.0 101.7 jit_solution(9757532928874250388)
XLA Ops:
  0.6 1.3 %collective-permute-start = (f32[2,64,256]{2,1,0:T(8,128)}, f32[2,64,256]{2,1,0:T(8,128)S(1)}, u32[]{:S(2)}, u32[]{:S(2)}) collective-permute-start(f32[2,64,256]{2,1,0:T(8,128)} %param.6), channel_id=1, source_target_pairs={{4,0},{8,4},{12,8},{16,12},{20,16},{24,20},{28,24},{5,1},{9,5},{13... | collective-permute-start | bytes 393224 | tf_op jit(solution)/shard_map/ppermute | solution.py:22
  1.9 1.3 %collective-permute-start.1 = (f32[2,64,256]{2,1,0:T(8,128)}, f32[2,64,256]{2,1,0:T(8,128)S(1)}, u32[]{:S(2)}, u32[]{:S(2)}) collective-permute-start(f32[2,64,256]{2,1,0:T(8,128)} %param.6), channel_id=1, source_target_pairs={{8,0},{12,4},{16,8},{20,12},{24,16},{28,20},{9,1},{13,5},{17,9},{2... | collective-permute-start | bytes 393224 | tf_op jit(solution)/shard_map/ppermute | solution.py:22
  4.2 3.0 %collective-permute-start.3 = (f32[1,2,2,64,128]{4,3,2,1,0:T(8,128)S(1)}, f32[1,2,2,64,128]{4,3,2,1,0:T(8,128)S(1)}, u32[]{:S(2)}, u32[]{:S(2)}) collective-permute-start(f32[1,2,2,64,128]{4,3,2,1,0:T(8,128)S(1)} %reverse_select_fusion.1), channel_id=1, source_target_pairs={{0,2},{1,3},{2,0},{3,1},{4,6},{5,7},{6,4},{7,5},{8,10},{9,11},{10,... | collective-permute-start | bytes 393224 | tf_op jit(solution)/shard_map/ppermute | solution.py:26
  9.0 1.7 %collective-permute-done.3 = f32[1,2,2,64,128]{4,3,2,1,0:T(8,128)S(1)} collective-permute-done((f32[1,2,2,64,128]{4,3,2,1,0:T(8,128)S(1)}, f32[1,2,2,64,128]{4,3,2,1,0:T(8,128)S(1)}, u32[]{:S(2)}, u32[]{:S(2)}) %collective-permute-start.3) | collective-permute-done | bytes 131104 | tf_op jit(solution)/shard_map/ppermute | solution.py:26
  10.8 2.4 %collective-permute-done.1 = f32[2,64,256]{2,1,0:T(8,128)S(1)} collective-permute-done((f32[2,64,256]{2,1,0:T(8,128)}, f32[2,64,256]{2,1,0:T(8,128)S(1)}, u32[]{:S(2)}, u32[]{:S(2)}) %collective-permute-start.1) | collective-permute-done | bytes 131104 | tf_op jit(solution)/shard_map/ppermute | solution.py:22
  14.7 1.9 %collective-permute-done.2 = f32[2,192,128]{2,1,0:T(8,128)S(1)} collective-permute-done((f32[2,192,128]{2,1,0:T(8,128)S(1)}, f32[2,192,128]{2,1,0:T(8,128)S(1)}, u32[]{:S(2)}, u32[]{:S(2)}) %collective-permute-start.2) | collective-permute-done | bytes 196640 | tf_op jit(solution)/shard_map/ppermute | solution.py:22
  18.5 4.2 %shard_map.78 = (f32[2,2,192,128]{3,2,1,0:T(8,128)S(1)}, f32[2,2,192,128]{3,2,1,0:T(8,128)S(1)}, f32[136,384]{1,0:T(8,128)S(1)}, f32[136,384]{1,0:T(8,128)S(1)},...) custom-call(s32[6]{0:T(128)S(1)} %reshape.96.place, s32[2]{0:T(128)S(1)} %pad_add_fusion.3.me, ...), custom_call_target="tpu_custom_call" | custom-call | flops 1610612736 | bytes 4194304 | tf_op jit(solution)/shard_map/pallas_call | solution.py:381
  22.8 3.6 %collective-permute-start.5 = (f32[392,128]{1,0:T(8,128)S(1)}, f32[392,128]{1,0:T(8,128)}, u32[]{:S(2)}, u32[]{:S(2)}) collective-permute-start(f32[392,128]{1,0:T(8,128)S(1)} %get-tuple-element.34), channel_id=1, source_target_pairs={{0,1},{2,3},{1,0},{3,2},{4,5},{6,7},{5,4},{7,6},{8,9},{10,11},{9,8... | collective-permute-start | bytes 602120 | tf_op jit(solution)/shard_map/ppermute | solution.py:31
  26.3 1.3 %collective-permute-start.6 = (f32[392,128]{1,0:T(8,128)S(1)}, f32[392,128]{1,0:T(8,128)}, u32[]{:S(2)}, u32[]{:S(2)}) collective-permute-start(f32[392,128]{1,0:T(8,128)S(1)} %get-tuple-element.35), channel_id=1, source_target_pairs={{1,2},{2,1},{5,6},{6,5},{9,10},{10,9},{13,14},{14,13},{17,18},{18,... | collective-permute-start | bytes 602120 | tf_op jit(solution)/shard_map/ppermute | solution.py:31
  31.1 1.4 %collective-permute-start.11 = (f32[192,128]{1,0:T(8,128)S(1)}, f32[192,128]{1,0:T(8,128)S(1)}, u32[]{:S(2)}, u32[]{:S(2)}) collective-permute-start(f32[192,128]{1,0:T(8,128)S(1)} %get-tuple-element.71), channel_id=1, source_target_pairs={{0,4},{1,5},{2,6},{3,7},{4,0},{5,1},{6,2},{7,3},{8,12},{9,13},{10,... | collective-permute-start | bytes 294920 | tf_op jit(solution)/shard_map/ppermute | solution.py:37
  32.5 5.0 %collective-permute-start.12 = (f32[192,128]{1,0:T(8,128)S(1)}, f32[192,128]{1,0:T(8,128)S(1)}, u32[]{:S(2)}, u32[]{:S(2)}) collective-permute-start(f32[192,128]{1,0:T(8,128)S(1)} %get-tuple-element.73), channel_id=1, source_target_pairs={{0,2},{1,3},{2,0},{3,1},{4,6},{5,7},{6,4},{7,5},{8,10},{9,11},{10,... | collective-permute-start | bytes 294920 | tf_op jit(solution)/shard_map/ppermute | solution.py:37
  37.8 2.5 %collective-permute-start.8 = (f32[136,384]{1,0:T(8,128)S(1)}, f32[136,384]{1,0:T(8,128)S(1)}, u32[]{:S(2)}, u32[]{:S(2)}) collective-permute-start(f32[136,384]{1,0:T(8,128)S(1)} %get-tuple-element.94), channel_id=1, source_target_pairs={{0,8},{4,12},{16,24},{20,28},{8,0},{12,4},{24,16},{28,20},{1,9},{5... | collective-permute-start | bytes 626696 | tf_op jit(solution)/shard_map/ppermute | solution.py:31
  41.0 2.5 %collective-permute-done.13 = f32[192,128]{1,0:T(8,128)S(1)} collective-permute-done((f32[192,128]{1,0:T(8,128)S(1)}, f32[192,128]{1,0:T(8,128)S(1)}, u32[]{:S(2)}, u32[]{:S(2)}) %collective-permute-start.13) | collective-permute-done | bytes 98336 | tf_op jit(solution)/shard_map/ppermute | solution.py:37
  43.5 2.5 %collective-permute-start.14 = (f32[192,128]{1,0:T(8,128)S(1)}, f32[192,128]{1,0:T(8,128)S(1)}, u32[]{:S(2)}, u32[]{:S(2)}) collective-permute-start(f32[192,128]{1,0:T(8,128)S(1)} %fusion.5), channel_id=1, source_target_pairs={{0,8},{4,12},{8,0},{12,4},{16,24},{20,28},{24,16},{28,20},{1,9},{5... | collective-permute-start | bytes 294920 | tf_op jit(solution)/shard_map/ppermute | solution.py:26
  46.0 2.6 %collective-permute-done.14 = f32[192,128]{1,0:T(8,128)S(1)} collective-permute-done((f32[192,128]{1,0:T(8,128)S(1)}, f32[192,128]{1,0:T(8,128)S(1)}, u32[]{:S(2)}, u32[]{:S(2)}) %collective-permute-start.14) | collective-permute-done | bytes 98336 | tf_op jit(solution)/shard_map/ppermute | solution.py:26
  48.6 4.1 %collective-permute-start.15 = (f32[192,128]{1,0:T(8,128)S(1)}, f32[192,128]{1,0:T(8,128)S(1)}, u32[]{:S(2)}, u32[]{:S(2)}) collective-permute-start(f32[192,128]{1,0:T(8,128)S(1)} %add.176), channel_id=1, source_target_pairs={{0,16},{4,20},{8,24},{12,28},{16,0},{20,4},{24,8},{28,12},{1,17},{... | collective-permute-start | bytes 294920 | tf_op jit(solution)/shard_map/ppermute | solution.py:26
  52.7 2.1 %shard_map.79 = (f32[2,64,384]{2,1,0:T(8,128)S(1)}, f32[2,64,384]{2,1,0:T(8,128)S(1)}, f32[2,64,384]{2,1,0:T(8,128)S(1)}) custom-call(s32[1024]{0:T(1024)S(1)} %fusion.9.table, s32[2]{0:T(128)S(1)} %pad_add_fusion.3.me, f32[2,64,384]{2,1,0:T(8,128)S(1)} %get-tuple-element.64.first, f32[2,64,384]{2,1,0:T(8,128)S(1)} %get-tuple-element.63.third, ...), custom_call_target="tpu_custom_call" | custom-call | flops 1048576 | bytes 1048576 | tf_op jit(solution)/shard_map/pallas_call | solution.py:336
  54.8 2.8 %collective-permute-done.15 = f32[192,128]{1,0:T(8,128)S(1)} collective-permute-done((f32[192,128]{1,0:T(8,128)S(1)}, f32[192,128]{1,0:T(8,128)S(1)}, u32[]{:S(2)}, u32[]{:S(2)}) %collective-permute-start.15) | collective-permute-done | bytes 98336 | tf_op jit(solution)/shard_map/ppermute | solution.py:26
  58.7 2.6 %collective-permute-start.18 = (f32[2,64,128]{2,1,0:T(8,128)S(1)}, f32[2,64,128]{2,1,0:T(8,128)S(1)}, u32[]{:S(2)}, u32[]{:S(2)}) collective-permute-start(f32[2,64,128]{2,1,0:T(8,128)S(1)} %bitcast_add_fusion.3), channel_id=1, source_target_pairs={{0,6},{1,7},{2,4},{3,5},{4,2},{5,3},{6,0},{7,1},{8,14},{9,15},{10,... | collective-permute-start | bytes 196616 | tf_op jit(solution)/shard_map/ppermute | solution.py:37
  63.0 1.3 %collective-permute-done.18 = f32[2,64,128]{2,1,0:T(8,128)S(1)} collective-permute-done((f32[2,64,128]{2,1,0:T(8,128)S(1)}, f32[2,64,128]{2,1,0:T(8,128)S(1)}, u32[]{:S(2)}, u32[]{:S(2)}) %collective-permute-start.18) | collective-permute-done | bytes 65568 | tf_op jit(solution)/shard_map/ppermute | solution.py:37
  64.4 3.3 %collective-permute-done.19.second = f32[2,64,384]{2,1,0:T(8,128)S(1)} collective-permute-done((f32[2,64,384]{2,1,0:T(8,128)S(1)}, f32[2,64,384]{2,1,0:T(8,128)S(1)}, u32[]{:S(2)}, u32[]{:S(2)}) %collective-permute-start.19) | collective-permute-done | bytes 196640 | tf_op jit(solution)/shard_map/ppermute | solution.py:26
  69.2 4.2 %shard_map.81 = (f32[2,2,192,128]{3,2,1,0:T(8,128)S(1)}, f32[2,2,192,128]{3,2,1,0:T(8,128)S(1)}, f32[136,384]{1,0:T(8,128)S(1)}, f32[136,384]{1,0:T(8,128)S(1)}, f32[136,384]{1,0:T(8,128)S(1)}) custom-call(s32[6]{0:T(128)S(1)} %reshape.96.place, s32[2]{0:T(128)S(1)} %pad_add_fusion.3.me, f32[2,2,128,128]{3,2,1,0:T(8,128)S(1)} %get-tuple-element.46.patch, ...), custom_call_target="tpu_custom_call" | custom-call | flops 1610612736 | bytes 4194304 | tf_op jit(solution)/shard_map/pallas_call | solution.py:381
  73.6 1.6 %collective-permute-done.21 = f32[2,2,192,128]{3,2,1,0:T(8,128)S(1)} collective-permute-done((f32[2,2,192,128]{3,2,1,0:T(8,128)S(1)}, f32[2,2,192,128]{3,2,1,0:T(8,128)S(1)}, u32[]{:S(2)}, u32[]{:S(2)}) %collective-permute-start.21) | collective-permute-done | bytes 393248 | tf_op jit(solution)/shard_map/ppermute | solution.py:26
  76.6 2.2 %collective-permute-start.24 = (f32[192,128]{1,0:T(8,128)S(1)}, f32[192,128]{1,0:T(8,128)S(1)}, u32[]{:S(2)}, u32[]{:S(2)}) collective-permute-start(f32[192,128]{1,0:T(8,128)S(1)} %get-tuple-element.69), channel_id=1, source_target_pairs={{0,6},{1,7},{2,4},{3,5},{4,2},{5,3},{6,0},{7,1},{8,14},{9,15},{10,... | collective-permute-start | bytes 294920 | tf_op jit(solution)/shard_map/ppermute | solution.py:37
  80.2 1.7 %collective-permute-done.23 = f32[192,128]{1,0:T(8,128)S(1)} collective-permute-done((f32[192,128]{1,0:T(8,128)S(1)}, f32[192,128]{1,0:T(8,128)S(1)}, u32[]{:S(2)}, u32[]{:S(2)}) %collective-permute-start.23) | collective-permute-done | bytes 98336 | tf_op jit(solution)/shard_map/ppermute | solution.py:37
  81.9 1.7 %collective-permute-done.24 = f32[192,128]{1,0:T(8,128)S(1)} collective-permute-done((f32[192,128]{1,0:T(8,128)S(1)}, f32[192,128]{1,0:T(8,128)S(1)}, u32[]{:S(2)}, u32[]{:S(2)}) %collective-permute-start.24) | collective-permute-done | bytes 98336 | tf_op jit(solution)/shard_map/ppermute | solution.py:37
  83.8 3.1 %collective-permute-done.27 = f32[128,384]{1,0:T(8,128)S(1)} collective-permute-done((f32[128,384]{1,0:T(8,128)S(1)}, f32[128,384]{1,0:T(8,128)S(1)}, u32[]{:S(2)}, u32[]{:S(2)}) %collective-permute-start.27) | collective-permute-done | bytes 196640 | tf_op jit(solution)/shard_map/ppermute | solution.py:26
  86.9 2.2 %collective-permute-start.28 = (f32[128,384]{1,0:T(8,128)S(1)}, f32[128,384]{1,0:T(8,128)S(1)}, u32[]{:S(2)}, u32[]{:S(2)}) collective-permute-start(f32[128,384]{1,0:T(8,128)S(1)} %multiply_add_fusion.2), channel_id=1, source_target_pairs={{0,8},{4,12},{8,16},{12,20},{16,24},{20,28},{1,9},{5,13},{9,17},{1... | collective-permute-start | bytes 589832 | tf_op jit(solution)/shard_map/ppermute | solution.py:22
  89.1 2.7 %collective-permute-start.26 = (f32[192,128]{1,0:T(8,128)S(1)}, f32[192,128]{1,0:T(8,128)S(1)}, u32[]{:S(2)}, u32[]{:S(2)}) collective-permute-start(f32[192,128]{1,0:T(8,128)S(1)} %add.185), channel_id=1, source_target_pairs={{0,16},{4,20},{8,24},{12,28},{16,0},{20,4},{24,8},{28,12},{1,17},{... | collective-permute-start | bytes 294920 | tf_op jit(solution)/shard_map/ppermute | solution.py:26
  92.7 3.1 %collective-permute-done.26 = f32[192,128]{1,0:T(8,128)S(1)} collective-permute-done((f32[192,128]{1,0:T(8,128)S(1)}, f32[192,128]{1,0:T(8,128)S(1)}, u32[]{:S(2)}, u32[]{:S(2)}) %collective-permute-start.26) | collective-permute-done | bytes 98336 | tf_op jit(solution)/shard_map/ppermute | solution.py:26
  97.0 1.3 %collective-permute-start.29 = (f32[128,128]{1,0:T(8,128)S(1)}, f32[128,128]{1,0:T(8,128)S(1)}, u32[]{:S(2)}, u32[]{:S(2)}) collective-permute-start(f32[128,128]{1,0:T(8,128)S(1)} %slice.184), channel_id=1, source_target_pairs={{0,1},{1,2},{2,3},{4,5},{5,6},{6,7},{8,9},{9,10},{10,11},{12,13},{... | collective-permute-start | bytes 196616 | tf_op jit(solution)/shard_map/ppermute | solution.py:22
  98.3 2.1 %collective-permute-done.30 = f32[2,64,128]{2,1,0:T(8,128)S(1)} collective-permute-done((f32[2,64,128]{2,1,0:T(8,128)S(1)}, f32[2,64,128]{2,1,0:T(8,128)S(1)}, u32[]{:S(2)}, u32[]{:S(2)}) %collective-permute-start.30) | collective-permute-done | bytes 65568 | tf_op jit(solution)/shard_map/ppermute | solution.py:37
  (112 shorter events, 21.0 us)
Async XLA Ops:
  0.6 10.2 %collective-permute-start = (f32[2,64,256]{2,1,0:T(8,128)}, f32[2,64,256]{2,1,0:T(8,128)S(1)}, u32[]{:S(2)}, u32[]{:S(2)}) collective-permute-start(f32[2,64,256]{2,1,0:T(8,128)} %param.6), channel_id=1, source_target_pairs={{4,0},{8,4},{12,8},{16,12},{20,16},{24,20},{28,24},{5,1},{9,5},{13... | collective-permute-start | bytes 393224 | tf_op jit(solution)/shard_map/ppermute | solution.py:22
  1.9 11.3 %collective-permute-start.1 = (f32[2,64,256]{2,1,0:T(8,128)}, f32[2,64,256]{2,1,0:T(8,128)S(1)}, u32[]{:S(2)}, u32[]{:S(2)}) collective-permute-start(f32[2,64,256]{2,1,0:T(8,128)} %param.6), channel_id=1, source_target_pairs={{8,0},{12,4},{16,8},{20,12},{24,16},{28,20},{9,1},{13,5},{17,9},{2... | collective-permute-start | bytes 393224 | tf_op jit(solution)/shard_map/ppermute | solution.py:22
  4.2 3.0 %copy-start.2 = (f32[2,64,256]{2,1,0:T(8,128)S(1)}, f32[2,64,256]{2,1,0:T(8,128)}, u32[]{:S(2)}) copy-start(f32[2,64,256]{2,1,0:T(8,128)} %param.6) | copy-start | bytes 393220
  4.2 6.5 %collective-permute-start.3 = (f32[1,2,2,64,128]{4,3,2,1,0:T(8,128)S(1)}, f32[1,2,2,64,128]{4,3,2,1,0:T(8,128)S(1)}, u32[]{:S(2)}, u32[]{:S(2)}) collective-permute-start(f32[1,2,2,64,128]{4,3,2,1,0:T(8,128)S(1)} %reverse_select_fusion.1), channel_id=1, source_target_pairs={{0,2},{1,3},{2,0},{3,1},{4,6},{5,7},{6,4},{7,5},{8,10},{9,11},{10,... | collective-permute-start | bytes 393224 | tf_op jit(solution)/shard_map/ppermute | solution.py:26
  10.7 6.7 %collective-permute-start.4 = (f32[2,2,2,64,128]{4,3,2,1,0:T(8,128)S(1)}, f32[2,2,2,64,128]{4,3,2,1,0:T(8,128)S(1)}, u32[]{:S(2)}, u32[]{:S(2)}) collective-permute-start(f32[2,2,2,64,128]{4,3,2,1,0:T(8,128)S(1)} %pad_maximum_fusion.3), channel_id=1, source_target_pairs={{0,1},{1,0},{2,3},{3,2},{4,5},{5,4},{6,7},{7,6},{8,9},{9,8},{10,11... | collective-permute-start | bytes 786440 | tf_op jit(solution)/shard_map/ppermute | solution.py:26
  13.2 3.3 %collective-permute-start.2 = (f32[2,192,128]{2,1,0:T(8,128)S(1)}, f32[2,192,128]{2,1,0:T(8,128)S(1)}, u32[]{:S(2)}, u32[]{:S(2)}) collective-permute-start(f32[2,192,128]{2,1,0:T(8,128)S(1)} %slice.189), channel_id=1, source_target_pairs={{1,0},{2,1},{3,2},{5,4},{6,5},{7,6},{9,8},{10,9},{11,10},{13,12},{... | collective-permute-start | bytes 589832 | tf_op jit(solution)/shard_map/ppermute | solution.py:22
  22.8 5.7 %collective-permute-start.5 = (f32[392,128]{1,0:T(8,128)S(1)}, f32[392,128]{1,0:T(8,128)}, u32[]{:S(2)}, u32[]{:S(2)}) collective-permute-start(f32[392,128]{1,0:T(8,128)S(1)} %get-tuple-element.34), channel_id=1, source_target_pairs={{0,1},{2,3},{1,0},{3,2},{4,5},{6,7},{5,4},{7,6},{8,9},{10,11},{9,8... | collective-permute-start | bytes 602120 | tf_op jit(solution)/shard_map/ppermute | solution.py:31
  26.3 2.1 %collective-permute-start.6 = (f32[392,128]{1,0:T(8,128)S(1)}, f32[392,128]{1,0:T(8,128)}, u32[]{:S(2)}, u32[]{:S(2)}) collective-permute-start(f32[392,128]{1,0:T(8,128)S(1)} %get-tuple-element.35), channel_id=1, source_target_pairs={{1,2},{2,1},{5,6},{6,5},{9,10},{10,9},{13,14},{14,13},{17,18},{18,... | collective-permute-start | bytes 602120 | tf_op jit(solution)/shard_map/ppermute | solution.py:31
  27.7 3.3 %collective-permute-start.10 = (f32[2,2,192,128]{3,2,1,0:T(8,128)S(1)}, f32[2,2,192,128]{3,2,1,0:T(8,128)S(1)}, u32[]{:S(2)}, u32[]{:S(2)}) collective-permute-start(f32[2,2,192,128]{3,2,1,0:T(8,128)S(1)} %get-tuple-element.40), channel_id=1, source_target_pairs={{0,1},{1,0},{2,3},{3,2},{4,5},{5,4},{6,7},{7,6},{8,9},{9,8},{10,11... | collective-permute-start | bytes 1179656 | tf_op jit(solution)/shard_map/ppermute | solution.py:26
  30.3 7.3 %collective-permute-start.7 = (f32[136,384]{1,0:T(8,128)S(1)}, f32[136,384]{1,0:T(8,128)S(1)}, u32[]{:S(2)}, u32[]{:S(2)}) collective-permute-start(f32[136,384]{1,0:T(8,128)S(1)} %pad_maximum_fusion.5), channel_id=1, source_target_pairs={{0,4},{4,0},{8,12},{12,8},{16,20},{20,16},{24,28},{28,24},{1,5},{5... | collective-permute-start | bytes 626696 | tf_op jit(solution)/shard_map/ppermute | solution.py:26
  31.1 9.8 %collective-permute-start.11 = (f32[192,128]{1,0:T(8,128)S(1)}, f32[192,128]{1,0:T(8,128)S(1)}, u32[]{:S(2)}, u32[]{:S(2)}) collective-permute-start(f32[192,128]{1,0:T(8,128)S(1)} %get-tuple-element.71), channel_id=1, source_target_pairs={{0,4},{1,5},{2,6},{3,7},{4,0},{5,1},{6,2},{7,3},{8,12},{9,13},{10,... | collective-permute-start | bytes 294920 | tf_op jit(solution)/shard_map/ppermute | solution.py:37
  32.5 8.4 %collective-permute-start.12 = (f32[192,128]{1,0:T(8,128)S(1)}, f32[192,128]{1,0:T(8,128)S(1)}, u32[]{:S(2)}, u32[]{:S(2)}) collective-permute-start(f32[192,128]{1,0:T(8,128)S(1)} %get-tuple-element.73), channel_id=1, source_target_pairs={{0,2},{1,3},{2,0},{3,1},{4,6},{5,7},{6,4},{7,5},{8,10},{9,11},{10,... | collective-permute-start | bytes 294920 | tf_op jit(solution)/shard_map/ppermute | solution.py:37
  37.5 5.9 %collective-permute-start.13 = (f32[192,128]{1,0:T(8,128)S(1)}, f32[192,128]{1,0:T(8,128)S(1)}, u32[]{:S(2)}, u32[]{:S(2)}) collective-permute-start(f32[192,128]{1,0:T(8,128)S(1)} %get-tuple-element.72), channel_id=1, source_target_pairs={{0,6},{1,7},{2,4},{3,5},{4,2},{5,3},{6,0},{7,1},{8,14},{9,15},{10,... | collective-permute-start | bytes 294920 | tf_op jit(solution)/shard_map/ppermute | solution.py:37
  37.8 14.9 %collective-permute-start.8 = (f32[136,384]{1,0:T(8,128)S(1)}, f32[136,384]{1,0:T(8,128)S(1)}, u32[]{:S(2)}, u32[]{:S(2)}) collective-permute-start(f32[136,384]{1,0:T(8,128)S(1)} %get-tuple-element.94), channel_id=1, source_target_pairs={{0,8},{4,12},{16,24},{20,28},{8,0},{12,4},{24,16},{28,20},{1,9},{5... | collective-permute-start | bytes 626696 | tf_op jit(solution)/shard_map/ppermute | solution.py:31
  40.3 12.4 %collective-permute-start.9 = (f32[136,384]{1,0:T(8,128)S(1)}, f32[136,384]{1,0:T(8,128)S(1)}, u32[]{:S(2)}, u32[]{:S(2)}) collective-permute-start(f32[136,384]{1,0:T(8,128)S(1)} %get-tuple-element.95), channel_id=1, source_target_pairs={{8,16},{12,20},{16,8},{20,12},{9,17},{13,21},{17,9},{21,13},{10,18... | collective-permute-start | bytes 626696 | tf_op jit(solution)/shard_map/ppermute | solution.py:31
  43.5 5.1 %collective-permute-start.14 = (f32[192,128]{1,0:T(8,128)S(1)}, f32[192,128]{1,0:T(8,128)S(1)}, u32[]{:S(2)}, u32[]{:S(2)}) collective-permute-start(f32[192,128]{1,0:T(8,128)S(1)} %fusion.5), channel_id=1, source_target_pairs={{0,8},{4,12},{8,0},{12,4},{16,24},{20,28},{24,16},{28,20},{1,9},{5... | collective-permute-start | bytes 294920 | tf_op jit(solution)/shard_map/ppermute | solution.py:26
  48.6 9.1 %collective-permute-start.15 = (f32[192,128]{1,0:T(8,128)S(1)}, f32[192,128]{1,0:T(8,128)S(1)}, u32[]{:S(2)}, u32[]{:S(2)}) collective-permute-start(f32[192,128]{1,0:T(8,128)S(1)} %add.176), channel_id=1, source_target_pairs={{0,16},{4,20},{8,24},{12,28},{16,0},{20,4},{24,8},{28,12},{1,17},{... | collective-permute-start | bytes 294920 | tf_op jit(solution)/shard_map/ppermute | solution.py:26
  57.7 5.3 %collective-permute-start.16 = (f32[2,64,128]{2,1,0:T(8,128)S(1)}, f32[2,64,128]{2,1,0:T(8,128)S(1)}, u32[]{:S(2)}, u32[]{:S(2)}) collective-permute-start(f32[2,64,128]{2,1,0:T(8,128)S(1)} %bitcast_add_fusion.3), channel_id=1, source_target_pairs={{0,4},{1,5},{2,6},{3,7},{4,0},{5,1},{6,2},{7,3},{8,12},{9,13},{10,... | collective-permute-start | bytes 196616 | tf_op jit(solution)/shard_map/ppermute | solution.py:37
  58.7 4.3 %collective-permute-start.17 = (f32[2,64,128]{2,1,0:T(8,128)S(1)}, f32[2,64,128]{2,1,0:T(8,128)S(1)}, u32[]{:S(2)}, u32[]{:S(2)}) collective-permute-start(f32[2,64,128]{2,1,0:T(8,128)S(1)} %bitcast_add_fusion.3), channel_id=1, source_target_pairs={{0,2},{1,3},{2,0},{3,1},{4,6},{5,7},{6,4},{7,5},{8,10},{9,11},{10,... | collective-permute-start | bytes 196616 | tf_op jit(solution)/shard_map/ppermute | solution.py:37
  58.7 5.6 %collective-permute-start.18 = (f32[2,64,128]{2,1,0:T(8,128)S(1)}, f32[2,64,128]{2,1,0:T(8,128)S(1)}, u32[]{:S(2)}, u32[]{:S(2)}) collective-permute-start(f32[2,64,128]{2,1,0:T(8,128)S(1)} %bitcast_add_fusion.3), channel_id=1, source_target_pairs={{0,6},{1,7},{2,4},{3,5},{4,2},{5,3},{6,0},{7,1},{8,14},{9,15},{10,... | collective-permute-start | bytes 196616 | tf_op jit(solution)/shard_map/ppermute | solution.py:37
  61.3 6.4 %collective-permute-start.19 = (f32[2,64,384]{2,1,0:T(8,128)S(1)}, f32[2,64,384]{2,1,0:T(8,128)S(1)}, u32[]{:S(2)}, u32[]{:S(2)}) collective-permute-start(f32[2,64,384]{2,1,0:T(8,128)S(1)} %get-tuple-element.43), channel_id=1, source_target_pairs={{0,4},{4,0},{8,12},{12,8},{16,20},{20,16},{24,28},{28,24},{1,5},{5... | collective-permute-start | bytes 589832 | tf_op jit(solution)/shard_map/ppermute | solution.py:26
  67.7 1.5 %collective-permute-start.20 = (f32[2,2,2,64,128]{4,3,2,1,0:T(8,128)S(1)}, f32[2,2,2,64,128]{4,3,2,1,0:T(8,128)S(1)}, u32[]{:S(2)}, u32[]{:S(2)}) collective-permute-start(f32[2,2,2,64,128]{4,3,2,1,0:T(8,128)S(1)} %pad_maximum_fusion.4), channel_id=1, source_target_pairs={{0,1},{1,0},{2,3},{3,2},{4,5},{5,4},{6,7},{7,6},{8,9},{9,8},{10,11... | collective-permute-start | bytes 786440 | tf_op jit(solution)/shard_map/ppermute | solution.py:26
  73.4 1.8 %collective-permute-start.21 = (f32[2,2,192,128]{3,2,1,0:T(8,128)S(1)}, f32[2,2,192,128]{3,2,1,0:T(8,128)S(1)}, u32[]{:S(2)}, u32[]{:S(2)}) collective-permute-start(f32[2,2,192,128]{3,2,1,0:T(8,128)S(1)} %get-tuple-element.50), channel_id=1, source_target_pairs={{0,1},{1,0},{2,3},{3,2},{4,5},{5,4},{6,7},{7,6},{8,9},{9,8},{10,11... | collective-permute-start | bytes 1179656 | tf_op jit(solution)/shard_map/ppermute | solution.py:26
  75.3 4.9 %collective-permute-start.22 = (f32[192,128]{1,0:T(8,128)S(1)}, f32[192,128]{1,0:T(8,128)S(1)}, u32[]{:S(2)}, u32[]{:S(2)}) collective-permute-start(f32[192,128]{1,0:T(8,128)S(1)} %get-tuple-element.68), channel_id=1, source_target_pairs={{0,4},{1,5},{2,6},{3,7},{4,0},{5,1},{6,2},{7,3},{8,12},{9,13},{10,... | collective-permute-start | bytes 294920 | tf_op jit(solution)/shard_map/ppermute | solution.py:37
  76.2 5.6 %collective-permute-start.23 = (f32[192,128]{1,0:T(8,128)S(1)}, f32[192,128]{1,0:T(8,128)S(1)}, u32[]{:S(2)}, u32[]{:S(2)}) collective-permute-start(f32[192,128]{1,0:T(8,128)S(1)} %get-tuple-element.70), channel_id=1, source_target_pairs={{0,2},{1,3},{2,0},{3,1},{4,6},{5,7},{6,4},{7,5},{8,10},{9,11},{10,... | collective-permute-start | bytes 294920 | tf_op jit(solution)/shard_map/ppermute | solution.py:37
  76.6 6.9 %collective-permute-start.24 = (f32[192,128]{1,0:T(8,128)S(1)}, f32[192,128]{1,0:T(8,128)S(1)}, u32[]{:S(2)}, u32[]{:S(2)}) collective-permute-start(f32[192,128]{1,0:T(8,128)S(1)} %get-tuple-element.69), channel_id=1, source_target_pairs={{0,6},{1,7},{2,4},{3,5},{4,2},{5,3},{6,0},{7,1},{8,14},{9,15},{10,... | collective-permute-start | bytes 294920 | tf_op jit(solution)/shard_map/ppermute | solution.py:37
  78.8 8.0 %collective-permute-start.27 = (f32[128,384]{1,0:T(8,128)S(1)}, f32[128,384]{1,0:T(8,128)S(1)}, u32[]{:S(2)}, u32[]{:S(2)}) collective-permute-start(f32[128,384]{1,0:T(8,128)S(1)} %slice.181), channel_id=1, source_target_pairs={{0,4},{4,0},{8,12},{12,8},{16,20},{20,16},{24,28},{28,24},{1,5},{5... | collective-permute-start | bytes 589832 | tf_op jit(solution)/shard_map/ppermute | solution.py:26
  83.6 5.5 %collective-permute-start.25 = (f32[192,128]{1,0:T(8,128)S(1)}, f32[192,128]{1,0:T(8,128)S(1)}, u32[]{:S(2)}, u32[]{:S(2)}) collective-permute-start(f32[192,128]{1,0:T(8,128)S(1)} %fusion.7), channel_id=1, source_target_pairs={{0,8},{4,12},{8,0},{12,4},{16,24},{20,28},{24,16},{28,20},{1,9},{5... | collective-permute-start | bytes 294920 | tf_op jit(solution)/shard_map/ppermute | solution.py:26
  86.9 9.0 %collective-permute-start.28 = (f32[128,384]{1,0:T(8,128)S(1)}, f32[128,384]{1,0:T(8,128)S(1)}, u32[]{:S(2)}, u32[]{:S(2)}) collective-permute-start(f32[128,384]{1,0:T(8,128)S(1)} %multiply_add_fusion.2), channel_id=1, source_target_pairs={{0,8},{4,12},{8,16},{12,20},{16,24},{20,28},{1,9},{5,13},{9,17},{1... | collective-permute-start | bytes 589832 | tf_op jit(solution)/shard_map/ppermute | solution.py:22
  89.1 6.8 %collective-permute-start.26 = (f32[192,128]{1,0:T(8,128)S(1)}, f32[192,128]{1,0:T(8,128)S(1)}, u32[]{:S(2)}, u32[]{:S(2)}) collective-permute-start(f32[192,128]{1,0:T(8,128)S(1)} %add.185), channel_id=1, source_target_pairs={{0,16},{4,20},{8,24},{12,28},{16,0},{20,4},{24,8},{28,12},{1,17},{... | collective-permute-start | bytes 294920 | tf_op jit(solution)/shard_map/ppermute | solution.py:26
  96.0 4.3 %collective-permute-start.30 = (f32[2,64,128]{2,1,0:T(8,128)S(1)}, f32[2,64,128]{2,1,0:T(8,128)S(1)}, u32[]{:S(2)}, u32[]{:S(2)}) collective-permute-start(f32[2,64,128]{2,1,0:T(8,128)S(1)} %bitcast_add_fusion.1), channel_id=1, source_target_pairs={{0,4},{1,5},{2,6},{3,7},{4,0},{5,1},{6,2},{7,3},{8,12},{9,13},{10,... | collective-permute-start | bytes 196616 | tf_op jit(solution)/shard_map/ppermute | solution.py:37
  97.0 4.1 %collective-permute-start.29 = (f32[128,128]{1,0:T(8,128)S(1)}, f32[128,128]{1,0:T(8,128)S(1)}, u32[]{:S(2)}, u32[]{:S(2)}) collective-permute-start(f32[128,128]{1,0:T(8,128)S(1)} %slice.184), channel_id=1, source_target_pairs={{0,1},{1,2},{2,3},{4,5},{5,6},{6,7},{8,9},{9,10},{10,11},{12,13},{... | collective-permute-start | bytes 196616 | tf_op jit(solution)/shard_map/ppermute | solution.py:22
  (3 other events, 2.7 us)

commit v3 on v2

--- a/solution.py
+++ b/solution.py
@@ -35,6 +35,10 @@
     scans, modes = lax.axis_size("scan"), lax.axis_size("mode")
     other = scan_bit * modes + mode_bit
     return lax.ppermute(value, ("scan", "mode"), [(i, i ^ other) for i in range(scans * modes)])
+
+
+def after(value, others):
+    return lax.optimization_barrier((value, others))[0]
 
 
 def bits_of(axis):
@@ -89,8 +93,9 @@
 
 def placed_in(term, down, right):
     tall = jnp.concatenate([term, jnp.zeros((SUBLANES, term.shape[1]), F32)], axis=0)
-    tall = pltpu.roll(tall, down, 0)
-    return pltpu.roll(jnp.concatenate([tall, jnp.zeros_like(tall)], axis=1), right, 1)
+    tall = pltpu.roll(pltpu.roll(tall, down, 0), right, 1)
+    first = lax.broadcasted_iota(jnp.int32, tall.shape, 1) >= right
+    return jnp.concatenate([jnp.where(first, tall, 0.0), jnp.where(first, 0.0, tall)], axis=1)
 
 
 def patches_kernel(place, first, second, third, patch, density, extended):
@@ -126,14 +131,16 @@
     parity = scan % 2
 
     def from_left(which):
-        for k in range(modes):
-            cols = slice(k * length, (k + 1) * length)
+        for pair in range(modes // 2):
+            cols = slice(2 * pair * length, 2 * (pair + 1) * length)
             hi, lo = x_hi[:, cols], x_lo[:, cols]
             out = dot(table[which, 0], hi) + dot(table[which, 0], lo) + dot(table[which, 1], hi)
             hi, lo = split(out)
-            rows = slice(k * length, (k + 1) * length)
-            y_hi[rows, :length], y_hi[rows, length:] = hi[:length], hi[length:]
-            y_lo[rows, :length], y_lo[rows, length:] = lo[:length], lo[length:]
+            for k in range(2):
+                rows = slice((2 * pair + k) * length, (2 * pair + k + 1) * length)
+                cols = slice(k * length, (k + 1) * length)
+                y_hi[rows, :length], y_hi[rows, length:] = hi[:length, cols], hi[length:, cols]
+                y_lo[rows, :length], y_lo[rows, length:] = lo[:length, cols], lo[length:, cols]
 
     def from_right(which, k):
         rows = slice(k * length, (k + 1) * length)
@@ -191,7 +198,6 @@
         for at in range(modes // 2):
             for top in range(2):
                 out[at, parity ^ top, 2 * half :] = density[top * half : (top + 1) * half]
-    terms, rims = terms[:3], terms[3:]
     data_rows = terms[0].shape[0] - windows.shape[0]
     tile_rows = data_rows // 2
     for step, out in enumerate(terms):
@@ -199,14 +205,6 @@
             out[part * tile_rows : (part + 1) * tile_rows] = sums[part, step * tile_rows : (step + 1) * tile_rows]
         out[data_rows:] = jnp.zeros((windows.shape[0], out.shape[1]), F32)
         out[data_rows:, LANES : 2 * LANES] = windows[...]
-    for phase, rim in enumerate(rims):
-        right = ((me[1] + phase) % 2 == 0).astype(jnp.int32)
-        start = pl.multiple_of(right * (sums.shape[2] - length), LANES)
-        for step in range(3):
-            for part in range(2):
-                at = (2 * step + part) * tile_rows
-                rim[at : at + tile_rows] = sums[part, step * tile_rows : (step + 1) * tile_rows, pl.ds(start, length)]
-        rim[3 * data_rows :] = windows[...]
 
 
 def weight_of(table, me, probes, grid, scan_steps, mode_steps, rows, cols, tile_rows, band_cols, acc):
@@ -236,25 +234,45 @@
     return acc[pl.ds(above, rows), pl.ds(left, cols)] + 1.0
 
 
+def join_kernel(band_cols, me, inner, outer, entries, from_a, from_b, new_inner, new_outer, for_a, for_b):
+    data_rows = inner.shape[0]
+    rim = for_a.shape[1]
+    lower = (me[0] // 2 % 2 == 0).astype(F32)
+    even = (me[1] % 2 == 0).astype(F32)
+    a, b = from_a[:data_rows], from_b[:data_rows]
+    tiles = (inner[...] + b * lower + a * (1.0 - lower), outer[...] + a * lower + b * (1.0 - lower))
+    new_inner[...], new_outer[...] = tiles
+    for at, tile in enumerate(tiles):
+        rows = slice(at * data_rows, (at + 1) * data_rows)
+        left, right = tile[:, :rim], tile[:, band_cols:]
+        for_a[rows] = right * even + left * (1.0 - even)
+        for_b[rows] = left * even + right * (1.0 - even)
+    rest = entries[...] + from_a[data_rows:, LANES : 2 * LANES] + from_b[data_rows:, LANES : 2 * LANES]
+    for_a[2 * data_rows :] = rest
+    for_b[2 * data_rows :] = rest
+
+
 def inner_kernel(grid, band_cols, table, me, first, third, probes, inner, outer, from_a, from_b, new_first, new_third, passed, acc):
     _, tile_rows, cols = first.shape
+    rim = from_a.shape[1]
     scan, mode = me[0], me[1]
     weight = weight_of(
         table, me, probes, grid, range(-2, 3), range(-1, 2), 3 * tile_rows, cols, tile_rows, band_cols, acc
     )
-    lower = (scan // 2 % 2 == 0).astype(F32)
     inside = jnp.where(lax.broadcasted_iota(jnp.int32, (tile_rows, cols), 1) < (grid[1] - mode) * band_cols, 1.0, 0.0)
     beyond = inside * (scan + 2 < grid[0]).astype(F32)
     is_first = (scan % 2).astype(F32)
+    even = (mode % 2 == 0).astype(F32)
     for part in range(2):
-        rows = slice(part * tile_rows, (part + 1) * tile_rows)
-        a, b = from_a[rows], from_b[rows]
-        own = inner[rows] + (b * lower + a * (1.0 - lower))
-        own = first[part] + inside * own / weight[:tile_rows]
-        after = outer[rows] + (a * lower + b * (1.0 - lower))
-        after = third[part] + beyond * after / weight[2 * tile_rows :]
-        new_first[part], new_third[part] = own, after
-        passed[part] = own * is_first + after * (1.0 - is_first)
+        updated = []
+        for at, (term, tile, keep) in enumerate(((inner, first, inside), (outer, third, beyond))):
+            a, b = (ref[slice((2 * at + part) * tile_rows, (2 * at + part + 1) * tile_rows)] for ref in (from_a, from_b))
+            left, right = b * even + a * (1.0 - even), a * even + b * (1.0 - even)
+            term = term[part * tile_rows : (part + 1) * tile_rows]
+            term = jnp.concatenate([term[:, :rim] + left, term[:, rim:band_cols], term[:, band_cols:] + right], axis=1)
+            updated.append(tile[part] + keep * term / weight[2 * at * tile_rows : (2 * at + 1) * tile_rows])
+        new_first[part], new_third[part] = updated
+        passed[part] = updated[0] * is_first + updated[1] * (1.0 - is_first)
 
 
 def last_kernel(grid, table, me, probes, weight, acc):
@@ -316,23 +334,25 @@
     def scratch(rows, cols):
         return [pltpu.VMEM((reach * tile_rows + rows + length, band_cols + cols + length), F32)]
 
-    def inner_update(first, third, probes, terms, rims):
-        a, b = (paired(rim, "mode", 1, phase) for phase, rim in enumerate(rims))
-        left, right = b * even_mode + a * (1.0 - even_mode), a * even_mode + b * (1.0 - even_mode)
-        joined = []
-        for step, term in enumerate(terms):
-            rows = slice(step * data_rows, (step + 1) * data_rows)
-            parts = [term[:data_rows, :length] + left[rows], term[:data_rows, length:band_cols], term[:data_rows, band_cols:] + right[rows]]
-            joined.append(jnp.concatenate(parts, axis=1))
-        here = terms[0][data_rows:, LANES : 2 * LANES] + (a + b)[3 * data_rows :]
-        here = jnp.pad(here, ((0, 0), (0, ext_cols - LANES)))
-        arrived = swapped(jnp.concatenate([joined[1], here]), "scan", 1)
-        entries = here + arrived[data_rows:]
-        inner = joined[0] + arrived[:data_rows] * odd
-        outer = joined[2] + arrived[:data_rows] * even
+    def joined_rows(terms):
+        arrived = swapped(terms[1], "scan", 1)
+        inner = terms[0][:data_rows] + arrived[:data_rows] * odd
+        outer = terms[2][:data_rows] + arrived[:data_rows] * even
+        entries = terms[0][data_rows:] + arrived[data_rows:]
         a = paired(jnp.concatenate([outer * lower + inner * (1.0 - lower), entries]), "scan", 2, 0)
         b = paired(jnp.concatenate([inner * lower + outer * (1.0 - lower), entries]), "scan", 2, 1)
-        entries = (entries + a[data_rows:] + b[data_rows:])[:, :LANES].astype(jnp.int32).reshape(-1)
+        rows = 2 * data_rows + table_rows
+        return call(
+            functools.partial(join_kernel, band_cols),
+            [sds(data_rows, ext_cols)] * 2 + [sds(rows, length)] * 2,
+            [SMEM] + [VMEM] * 5,
+            flops=2**20,
+            moved=2**20,
+        )(me, inner, outer, entries[:, LANES : 2 * LANES], a, b)
+
+    def inner_update(first, third, probes, inner, outer, for_a, for_b):
+        a, b = paired(for_a, "mode", 1, 0), paired(for_b, "mode", 1, 1)
+        entries = (for_a + a + b)[2 * data_rows :].astype(jnp.int32).reshape(-1)
         first, third, passed = call(
             functools.partial(inner_kernel, (scans, modes), band_cols),
             [sds(2, tile_rows, ext_cols)] * 3,
@@ -362,10 +382,13 @@
         terms = jnp.concatenate([first[:, :length] + margin, first[:, length:band_cols]], axis=1)
         return tile[:, :, :band_cols] + terms.reshape(2, tile_rows, band_cols) / weight
 
-    probes = gathered(as_halves(probe), "mode")
+    probes = as_halves(probe)
+    probes = jnp.concatenate([probes, swapped(probes, "mode", far)], axis=0)
     tiles = [object_field, shifted(object_field, "scan", -1), shifted(object_field, "scan", -2)]
     tiles = jnp.concatenate(tiles, axis=1)
     tiles = jnp.concatenate([tiles, shifted(tiles[:, :, :length], "mode", -1)], axis=2)
+    probes = after(probes, tiles)
+    probes = jnp.concatenate([probes, swapped(probes, "mode", near)], axis=0)
     first, second, third = (tiles[:, step * tile_rows : (step + 1) * tile_rows] for step in range(3))
     for iteration in range(ITERS):
         last = iteration == ITERS - 1
@@ -380,7 +403,7 @@
         rows_out = data_rows + table_rows
         kept, sent, *terms = call(
             wave_kernel,
-            (*[sds(modes // 2, 2, 3 * half, length)] * 2, *[sds(rows_out, ext_cols)] * 3, *[sds(2 * data_rows + rows_out, length)] * (0 if last else 2)),
+            (*[sds(modes // 2, 2, 3 * half, length)] * 2, *[sds(rows_out, ext_cols)] * 3),
             [SMEM, SMEM] + [VMEM] * 6,
             [pltpu.VMEM((2, ext_rows, ext_cols), F32)]
             + [pltpu.VMEM((2 * length, modes * length), BF16)] * 2
@@ -392,15 +415,20 @@
         kept = kept + swapped(sent, "mode", near)
         if last:
             kept, terms = lax.optimization_barrier((kept, terms))
+        pass
         own = kept[0, 0] + across(kept[0, 1], 1, 0) + across(kept[1, 0], 0, far) + across(kept[1, 1], 1, far)
+        if not last:
+            joined = joined_rows(terms)
+        pass
         for bit in bits_of("scan")[1:]:
             own = own + swapped(own, "scan", bit)
+            pass
         if not last:
-            first, third, passed, entries = inner_update(first, third, probes, terms[:3], terms[3:])
-            own, passed = lax.optimization_barrier((own, passed))
+            first, third, passed, entries = inner_update(first, third, probes, *joined)
+            own = after(own, passed)
         else:
             inner = last_update(first, probes, terms[:3], entries)
-            own, inner = lax.optimization_barrier((own, inner))
+            own = after(own, inner)
         probe = probes[0, 0] + own[: 2 * half].reshape(2, half, length) / (own[2 * half :] + 1.0)
         if not last:
             second = swapped(passed, "scan", 1)
@@ -410,7 +438,7 @@
                     jnp.stack([across(probe, 0, far), across(probe, 1, far)]),
                 ]
             )
-            probes, second = lax.optimization_barrier((probes, second))
+            probes = after(probes, second)
             probes = jnp.concatenate([probes, swapped(probes, "mode", near)], axis=0)
         else:
             object_field = last_part(first, probes, inner, entries)

time: 103 us -> 99.5 us (0.966)
  starting transfers between devices: 46.2 us -> 43.4 us
  other arithmetic: 3.48 us -> 1.65 us
    ppermute x4, starting transfers between devices: 8.08 us -> 3.34 us  [paired(): lax.ppermute(value, axis, [(i, i + step) for i in lower] + [(i + step, i)...]
    ppermute x12, starting transfers between devices: 16.2 us -> 19 us  [swapped(): lax.ppermute(value, axis, [(i, i ^ bit) for i in range(lax.axis_size(axis...]
    ppermute x10, waiting for transfers between devices: 10.3 us -> 12.7 us  [across(): lax.ppermute(value, ('scan', 'mode'), [(i, i ^ other) for i in range(scan...]
    ppermute x12, waiting for transfers between devices: 18.8 us -> 16.8 us  [swapped(): lax.ppermute(value, axis, [(i, i ^ bit) for i in range(lax.axis_size(axis...]
    add x6 -> x3, other arithmetic: 1.92 us -> 0.11 us  [the longest x1 0.06 us: joined_rows(): inner * lower + outer * (1.0 - lower)]
    ppermute x10, starting transfers between devices: 14.6 us -> 13.5 us  [across(): lax.ppermute(value, ('scan', 'mode'), [(i, i ^ other) for i in range(scan...]
  transfers between devices with their start and end apart: 31 -> 31, of which waited for: 17 -> 18; matrix products, arithmetic and copies ran while one was open for 5% -> 3% of each run, Pallas kernels for 5% -> 6%
where the time goes in v3:
time: 99.5 us; the launch traced here: 98.1 us
  starting transfers between devices  43.4 us (44%)
  waiting for transfers between devices  33.7 us (34%)
  Pallas kernels  13.8 us (14%)
  local copies, waits for them, and re-layouts  3.72 us (4%)
  between operations  1.82 us (2%)
  other arithmetic  1.65 us (2%)
    ppermute x12, starting transfers between devices, swapped(): lax.ppermute(value, axis, [(i, i ^ bit) for i in range(lax.axis_size(axis...  19 us
    ppermute x12, waiting for transfers between devices, swapped(): lax.ppermute(value, axis, [(i, i ^ bit) for i in range(lax.axis_size(axis...  16.8 us
    ppermute x10, starting transfers between devices, across(): lax.ppermute(value, ('scan', 'mode'), [(i, i ^ other) for i in range(scan...  13.5 us
    ppermute x10, waiting for transfers between devices, across(): lax.ppermute(value, ('scan', 'mode'), [(i, i ^ other) for i in range(scan...  12.7 us
    pallas_call x2, Pallas kernels, local(): call(wave_kernel, (*[sds(modes // 2, 2, 3 * half, length)] * 2, *[sds(row...  8.16 us
    ppermute x5, starting transfers between devices, shifted(): lax.ppermute(value, axis, [(source, source + steps) for source in range(i...  7.59 us
    ppermute x5, waiting for transfers between devices, shifted(): lax.ppermute(value, axis, [(source, source + steps) for source in range(i...  4.22 us
    ppermute x4, starting transfers between devices, paired(): lax.ppermute(value, axis, [(i, i + step) for i in lower] + [(i + step, i)...  3.34 us
  transfers between devices with their start and end apart: 31, of which 18 were waited for; matrix products, arithmetic and copies ran while one was open for 3% of the time, Pallas kernels for 6%

profile of v3, /device:TPU:0, one launch (start us, length us, event | category | flops | bytes accessed | tf_op | source)
XLA Modules:
  0.0 98.1 jit_solution(7805992581754584331)
XLA Ops:
  0.6 1.3 %collective-permute-start = (f32[2,64,256]{2,1,0:T(8,128)}, f32[2,64,256]{2,1,0:T(8,128)S(1)}, u32[]{:S(2)}, u32[]{:S(2)}) collective-permute-start(f32[2,64,256]{2,1,0:T(8,128)} %param.6), channel_id=1, source_target_pairs={{4,0},{8,4},{12,8},{16,12},{20,16},{24,20},{28,24},{5,1},{9,5},{13... | collective-permute-start | bytes 393224 | tf_op jit(solution)/shard_map/ppermute | solution.py:22
  1.9 1.3 %collective-permute-start.1 = (f32[2,64,256]{2,1,0:T(8,128)}, f32[2,64,256]{2,1,0:T(8,128)S(1)}, u32[]{:S(2)}, u32[]{:S(2)}) collective-permute-start(f32[2,64,256]{2,1,0:T(8,128)} %param.6), channel_id=1, source_target_pairs={{8,0},{12,4},{16,8},{20,12},{24,16},{28,20},{9,1},{13,5},{17,9},{2... | collective-permute-start | bytes 393224 | tf_op jit(solution)/shard_map/ppermute | solution.py:22
  4.2 3.0 %collective-permute-start.3 = (f32[1,2,2,64,128]{4,3,2,1,0:T(8,128)S(1)}, f32[1,2,2,64,128]{4,3,2,1,0:T(8,128)S(1)}, u32[]{:S(2)}, u32[]{:S(2)}) collective-permute-start(f32[1,2,2,64,128]{4,3,2,1,0:T(8,128)S(1)} %reverse_select_fusion.1), channel_id=1, source_target_pairs={{0,2},{1,3},{2,0},{3,1},{4,6},{5,7},{6,4},{7,5},{8,10},{9,11},{10,... | collective-permute-start | bytes 393224 | tf_op jit(solution)/shard_map/ppermute | solution.py:26
  9.1 1.6 %collective-permute-done.3 = f32[1,2,2,64,128]{4,3,2,1,0:T(8,128)S(1)} collective-permute-done((f32[1,2,2,64,128]{4,3,2,1,0:T(8,128)S(1)}, f32[1,2,2,64,128]{4,3,2,1,0:T(8,128)S(1)}, u32[]{:S(2)}, u32[]{:S(2)}) %collective-permute-start.3) | collective-permute-done | bytes 131104 | tf_op jit(solution)/shard_map/ppermute | solution.py:26
  10.8 2.4 %collective-permute-done.1 = f32[2,64,256]{2,1,0:T(8,128)S(1)} collective-permute-done((f32[2,64,256]{2,1,0:T(8,128)}, f32[2,64,256]{2,1,0:T(8,128)S(1)}, u32[]{:S(2)}, u32[]{:S(2)}) %collective-permute-start.1) | collective-permute-done | bytes 131104 | tf_op jit(solution)/shard_map/ppermute | solution.py:22
  13.2 1.3 %collective-permute-start.2 = (f32[2,192,128]{2,1,0:T(8,128)S(1)}, f32[2,192,128]{2,1,0:T(8,128)S(1)}, u32[]{:S(2)}, u32[]{:S(2)}) collective-permute-start(f32[2,192,128]{2,1,0:T(8,128)S(1)} %slice.129), channel_id=1, source_target_pairs={{1,0},{2,1},{3,2},{5,4},{6,5},{7,6},{9,8},{10,9},{11,10},{13,12},{... | collective-permute-start | bytes 589832 | tf_op jit(solution)/shard_map/ppermute | solution.py:22
  14.7 1.9 %collective-permute-done.2 = f32[2,192,128]{2,1,0:T(8,128)S(1)} collective-permute-done((f32[2,192,128]{2,1,0:T(8,128)S(1)}, f32[2,192,128]{2,1,0:T(8,128)S(1)}, u32[]{:S(2)}, u32[]{:S(2)}) %collective-permute-start.2) | collective-permute-done | bytes 196640 | tf_op jit(solution)/shard_map/ppermute | solution.py:22
  18.4 4.1 %shard_map.78 = (f32[2,2,192,128]{3,2,1,0:T(8,128)S(1)}, f32[2,2,192,128]{3,2,1,0:T(8,128)S(1)}, f32[136,384]{1,0:T(8,128)S(1)}, f32[136,384]{1,0:T(8,128)S(1)}, f32[136,384]{1,0:T(8,128)S(1)}) custom-call(s32[6]{0:T(128)S(1)} %reshape.96.place, s32[2]{0:T(128)S(1)} %pad_add_fusion.2.me, f32[2,2,128,128]{3,2,1,0:T(8,128)S(1)} %get-tuple-element.31.patch, ...), custom_call_target="tpu_custom_call" | custom-call | flops 1610612736 | bytes 4194304 | tf_op jit(solution)/shard_map/pallas_call | solution.py:404
  22.6 3.9 %collective-permute-start.11 = (f32[2,2,192,128]{3,2,1,0:T(8,128)S(1)}, f32[2,2,192,128]{3,2,1,0:T(8,128)S(1)}, u32[]{:S(2)}, u32[]{:S(2)}) collective-permute-start(f32[2,2,192,128]{3,2,1,0:T(8,128)S(1)} %get-tuple-element.47), channel_id=1, source_target_pairs={{0,1},{1,0},{2,3},{3,2},{4,5},{5,4},{6,7},{7,6},{8,9},{9,8},{10,11... | collective-permute-start | bytes 1179656 | tf_op jit(solution)/shard_map/ppermute | solution.py:26
  26.5 1.9 %collective-permute-done.5 = f32[136,384]{1,0:T(8,128)S(1)} collective-permute-done((f32[136,384]{1,0:T(8,128)S(1)}, f32[136,384]{1,0:T(8,128)S(1)}, u32[]{:S(2)}, u32[]{:S(2)}) %collective-permute-start.5) | collective-permute-done | bytes 208928 | tf_op jit(solution)/shard_map/ppermute | solution.py:26
  28.5 1.9 %collective-permute-start.6 = (f32[136,384]{1,0:T(8,128)S(1)}, f32[136,384]{1,0:T(8,128)S(1)}, u32[]{:S(2)}, u32[]{:S(2)}) collective-permute-start(f32[136,384]{1,0:T(8,128)S(1)} %get-tuple-element.75), channel_id=1, source_target_pairs={{0,8},{4,12},{16,24},{20,28},{8,0},{12,4},{24,16},{28,20},{1,9},{5... | collective-permute-start | bytes 626696 | tf_op jit(solution)/shard_map/ppermute | solution.py:31
  31.9 3.9 %collective-permute-start.13 = (f32[192,128]{1,0:T(8,128)S(1)}, f32[192,128]{1,0:T(8,128)S(1)}, u32[]{:S(2)}, u32[]{:S(2)}) collective-permute-start(f32[192,128]{1,0:T(8,128)S(1)} %get-tuple-element.71), channel_id=1, source_target_pairs={{0,2},{1,3},{2,0},{3,1},{4,6},{5,7},{6,4},{7,5},{8,10},{9,11},{10,... | collective-permute-start | bytes 294920 | tf_op jit(solution)/shard_map/ppermute | solution.py:37
  38.1 1.3 %collective-permute-done.13 = f32[192,128]{1,0:T(8,128)S(1)} collective-permute-done((f32[192,128]{1,0:T(8,128)S(1)}, f32[192,128]{1,0:T(8,128)S(1)}, u32[]{:S(2)}, u32[]{:S(2)}) %collective-permute-start.13) | collective-permute-done | bytes 98336 | tf_op jit(solution)/shard_map/ppermute | solution.py:37
  39.3 2.7 %collective-permute-done.14 = f32[192,128]{1,0:T(8,128)S(1)} collective-permute-done((f32[192,128]{1,0:T(8,128)S(1)}, f32[192,128]{1,0:T(8,128)S(1)}, u32[]{:S(2)}, u32[]{:S(2)}) %collective-permute-start.14) | collective-permute-done | bytes 98336 | tf_op jit(solution)/shard_map/ppermute | solution.py:37
  42.0 4.6 %collective-permute-start.15 = (f32[192,128]{1,0:T(8,128)S(1)}, f32[192,128]{1,0:T(8,128)S(1)}, u32[]{:S(2)}, u32[]{:S(2)}) collective-permute-start(f32[192,128]{1,0:T(8,128)S(1)} %fusion.6), channel_id=1, source_target_pairs={{0,8},{4,12},{8,0},{12,4},{16,24},{20,28},{24,16},{28,20},{1,9},{5... | collective-permute-start | bytes 294920 | tf_op jit(solution)/shard_map/ppermute | solution.py:26
  46.6 2.8 %collective-permute-done.15 = f32[192,128]{1,0:T(8,128)S(1)} collective-permute-done((f32[192,128]{1,0:T(8,128)S(1)}, f32[192,128]{1,0:T(8,128)S(1)}, u32[]{:S(2)}, u32[]{:S(2)}) %collective-permute-start.15) | collective-permute-done | bytes 98336 | tf_op jit(solution)/shard_map/ppermute | solution.py:26
  49.5 2.1 %collective-permute-start.16 = (f32[192,128]{1,0:T(8,128)S(1)}, f32[192,128]{1,0:T(8,128)S(1)}, u32[]{:S(2)}, u32[]{:S(2)}) collective-permute-start(f32[192,128]{1,0:T(8,128)S(1)} %add.130), channel_id=1, source_target_pairs={{0,16},{4,20},{8,24},{12,28},{16,0},{20,4},{24,8},{28,12},{1,17},{... | collective-permute-start | bytes 294920 | tf_op jit(solution)/shard_map/ppermute | solution.py:26
  51.6 2.2 %shard_map.80 = (f32[2,64,384]{2,1,0:T(8,128)S(1)}, f32[2,64,384]{2,1,0:T(8,128)S(1)}, f32[2,64,384]{2,1,0:T(8,128)S(1)}) custom-call(s32[1024]{0:T(1024)S(1)} %fusion.10.table, s32[2]{0:T(128)S(1)} %pad_add_fusion.2.me, f32[2,64,384]{2,1,0:T(8,128)S(1)} %get-tuple-element.65.first, f32[2,64,384]{2,1,0:T(8,128)S(1)} %get-tuple-element.63.third, ...), custom_call_target="tpu_custom_call" | custom-call | flops 1048576 | bytes 1048576 | tf_op jit(solution)/shard_map/pallas_call | solution.py:356
  54.9 2.1 %collective-permute-done.16 = f32[192,128]{1,0:T(8,128)S(1)} collective-permute-done((f32[192,128]{1,0:T(8,128)S(1)}, f32[192,128]{1,0:T(8,128)S(1)}, u32[]{:S(2)}, u32[]{:S(2)}) %collective-permute-start.16) | collective-permute-done | bytes 98336 | tf_op jit(solution)/shard_map/ppermute | solution.py:26
  57.8 2.8 %collective-permute-start.19 = (f32[2,64,128]{2,1,0:T(8,128)S(1)}, f32[2,64,128]{2,1,0:T(8,128)S(1)}, u32[]{:S(2)}, u32[]{:S(2)}) collective-permute-start(f32[2,64,128]{2,1,0:T(8,128)S(1)} %bitcast_add_fusion.3), channel_id=1, source_target_pairs={{0,6},{1,7},{2,4},{3,5},{4,2},{5,3},{6,0},{7,1},{8,14},{9,15},{10,... | collective-permute-start | bytes 196616 | tf_op jit(solution)/shard_map/ppermute | solution.py:37
  60.6 2.3 %collective-permute-done.17 = f32[2,64,128]{2,1,0:T(8,128)S(1)} collective-permute-done((f32[2,64,128]{2,1,0:T(8,128)S(1)}, f32[2,64,128]{2,1,0:T(8,128)S(1)}, u32[]{:S(2)}, u32[]{:S(2)}) %collective-permute-start.17) | collective-permute-done | bytes 65568 | tf_op jit(solution)/shard_map/ppermute | solution.py:37
  65.3 4.1 %shard_map.82 = (f32[2,2,192,128]{3,2,1,0:T(8,128)S(1)}, f32[2,2,192,128]{3,2,1,0:T(8,128)S(1)}, f32[136,384]{1,0:T(8,128)S(1)}, f32[136,384]{1,0:T(8,128)S(1)}, f32[136,384]{1,0:T(8,128)S(1)}) custom-call(s32[6]{0:T(128)S(1)} %reshape.96.place, s32[2]{0:T(128)S(1)} %pad_add_fusion.2.me, f32[2,2,128,128]{3,2,1,0:T(8,128)S(1)} %get-tuple-element.44.patch, ...), custom_call_target="tpu_custom_call" | custom-call | flops 1610612736 | bytes 4194304 | tf_op jit(solution)/shard_map/pallas_call | solution.py:404
  69.5 1.6 %collective-permute-done.21 = f32[2,2,192,128]{3,2,1,0:T(8,128)S(1)} collective-permute-done((f32[2,2,192,128]{3,2,1,0:T(8,128)S(1)}, f32[2,2,192,128]{3,2,1,0:T(8,128)S(1)}, u32[]{:S(2)}, u32[]{:S(2)}) %collective-permute-start.21) | collective-permute-done | bytes 393248 | tf_op jit(solution)/shard_map/ppermute | solution.py:26
  72.2 1.8 %collective-permute-start.26 = (f32[192,128]{1,0:T(8,128)S(1)}, f32[192,128]{1,0:T(8,128)S(1)}, u32[]{:S(2)}, u32[]{:S(2)}) collective-permute-start(f32[192,128]{1,0:T(8,128)S(1)} %get-tuple-element.68), channel_id=1, source_target_pairs={{0,2},{1,3},{2,0},{3,1},{4,6},{5,7},{6,4},{7,5},{8,10},{9,11},{10,... | collective-permute-start | bytes 294920 | tf_op jit(solution)/shard_map/ppermute | solution.py:37
  76.1 1.3 %collective-permute-done.26 = f32[192,128]{1,0:T(8,128)S(1)} collective-permute-done((f32[192,128]{1,0:T(8,128)S(1)}, f32[192,128]{1,0:T(8,128)S(1)}, u32[]{:S(2)}, u32[]{:S(2)}) %collective-permute-start.26) | collective-permute-done | bytes 98336 | tf_op jit(solution)/shard_map/ppermute | solution.py:37
  77.4 2.2 %collective-permute-done.27 = f32[192,128]{1,0:T(8,128)S(1)} collective-permute-done((f32[192,128]{1,0:T(8,128)S(1)}, f32[192,128]{1,0:T(8,128)S(1)}, u32[]{:S(2)}, u32[]{:S(2)}) %collective-permute-start.27) | collective-permute-done | bytes 98336 | tf_op jit(solution)/shard_map/ppermute | solution.py:37
  80.4 2.7 %collective-permute-done.22 = f32[128,384]{1,0:T(8,128)S(1)} collective-permute-done((f32[128,384]{1,0:T(8,128)S(1)}, f32[128,384]{1,0:T(8,128)S(1)}, u32[]{:S(2)}, u32[]{:S(2)}) %collective-permute-start.22) | collective-permute-done | bytes 196640 | tf_op jit(solution)/shard_map/ppermute | solution.py:26
  83.1 2.4 %collective-permute-start.23 = (f32[128,384]{1,0:T(8,128)S(1)}, f32[128,384]{1,0:T(8,128)S(1)}, u32[]{:S(2)}, u32[]{:S(2)}) collective-permute-start(f32[128,384]{1,0:T(8,128)S(1)} %multiply_add_fusion), channel_id=1, source_target_pairs={{0,8},{4,12},{8,16},{12,20},{16,24},{20,28},{1,9},{5,13},{9,17},{1... | collective-permute-start | bytes 589832 | tf_op jit(solution)/shard_map/ppermute | solution.py:22
  85.6 2.2 %collective-permute-start.29 = (f32[192,128]{1,0:T(8,128)S(1)}, f32[192,128]{1,0:T(8,128)S(1)}, u32[]{:S(2)}, u32[]{:S(2)}) collective-permute-start(f32[192,128]{1,0:T(8,128)S(1)} %add.144), channel_id=1, source_target_pairs={{0,16},{4,20},{8,24},{12,28},{16,0},{20,4},{24,8},{28,12},{1,17},{... | collective-permute-start | bytes 294920 | tf_op jit(solution)/shard_map/ppermute | solution.py:26
  88.8 3.4 %collective-permute-done.29 = f32[192,128]{1,0:T(8,128)S(1)} collective-permute-done((f32[192,128]{1,0:T(8,128)S(1)}, f32[192,128]{1,0:T(8,128)S(1)}, u32[]{:S(2)}, u32[]{:S(2)}) %collective-permute-start.29) | collective-permute-done | bytes 98336 | tf_op jit(solution)/shard_map/ppermute | solution.py:26
  93.4 1.3 %collective-permute-start.24 = (f32[128,128]{1,0:T(8,128)S(1)}, f32[128,128]{1,0:T(8,128)S(1)}, u32[]{:S(2)}, u32[]{:S(2)}) collective-permute-start(f32[128,128]{1,0:T(8,128)S(1)} %slice.147), channel_id=1, source_target_pairs={{0,1},{1,2},{2,3},{4,5},{5,6},{6,7},{8,9},{9,10},{10,11},{12,13},{... | collective-permute-start | bytes 196616 | tf_op jit(solution)/shard_map/ppermute | solution.py:22
  94.7 2.0 %collective-permute-done.30 = f32[2,64,128]{2,1,0:T(8,128)S(1)} collective-permute-done((f32[2,64,128]{2,1,0:T(8,128)S(1)}, f32[2,64,128]{2,1,0:T(8,128)S(1)}, u32[]{:S(2)}, u32[]{:S(2)}) %collective-permute-start.30) | collective-permute-done | bytes 65568 | tf_op jit(solution)/shard_map/ppermute | solution.py:37
  (108 shorter events, 20.1 us)
Async XLA Ops:
  0.6 10.2 %collective-permute-start = (f32[2,64,256]{2,1,0:T(8,128)}, f32[2,64,256]{2,1,0:T(8,128)S(1)}, u32[]{:S(2)}, u32[]{:S(2)}) collective-permute-start(f32[2,64,256]{2,1,0:T(8,128)} %param.6), channel_id=1, source_target_pairs={{4,0},{8,4},{12,8},{16,12},{20,16},{24,20},{28,24},{5,1},{9,5},{13... | collective-permute-start | bytes 393224 | tf_op jit(solution)/shard_map/ppermute | solution.py:22
  1.9 11.3 %collective-permute-start.1 = (f32[2,64,256]{2,1,0:T(8,128)}, f32[2,64,256]{2,1,0:T(8,128)S(1)}, u32[]{:S(2)}, u32[]{:S(2)}) collective-permute-start(f32[2,64,256]{2,1,0:T(8,128)} %param.6), channel_id=1, source_target_pairs={{8,0},{12,4},{16,8},{20,12},{24,16},{28,20},{9,1},{13,5},{17,9},{2... | collective-permute-start | bytes 393224 | tf_op jit(solution)/shard_map/ppermute | solution.py:22
  4.2 4.9 %copy-start.2 = (f32[2,64,256]{2,1,0:T(8,128)S(1)}, f32[2,64,256]{2,1,0:T(8,128)}, u32[]{:S(2)}) copy-start(f32[2,64,256]{2,1,0:T(8,128)} %param.6) | copy-start | bytes 393220
  4.2 6.5 %collective-permute-start.3 = (f32[1,2,2,64,128]{4,3,2,1,0:T(8,128)S(1)}, f32[1,2,2,64,128]{4,3,2,1,0:T(8,128)S(1)}, u32[]{:S(2)}, u32[]{:S(2)}) collective-permute-start(f32[1,2,2,64,128]{4,3,2,1,0:T(8,128)S(1)} %reverse_select_fusion.1), channel_id=1, source_target_pairs={{0,2},{1,3},{2,0},{3,1},{4,6},{5,7},{6,4},{7,5},{8,10},{9,11},{10,... | collective-permute-start | bytes 393224 | tf_op jit(solution)/shard_map/ppermute | solution.py:26
  10.7 6.7 %collective-permute-start.4 = (f32[2,2,2,64,128]{4,3,2,1,0:T(8,128)S(1)}, f32[2,2,2,64,128]{4,3,2,1,0:T(8,128)S(1)}, u32[]{:S(2)}, u32[]{:S(2)}) collective-permute-start(f32[2,2,2,64,128]{4,3,2,1,0:T(8,128)S(1)} %pad_maximum_fusion.3), channel_id=1, source_target_pairs={{0,1},{1,0},{2,3},{3,2},{4,5},{5,4},{6,7},{7,6},{8,9},{9,8},{10,11... | collective-permute-start | bytes 786440 | tf_op jit(solution)/shard_map/ppermute | solution.py:26
  13.2 3.3 %collective-permute-start.2 = (f32[2,192,128]{2,1,0:T(8,128)S(1)}, f32[2,192,128]{2,1,0:T(8,128)S(1)}, u32[]{:S(2)}, u32[]{:S(2)}) collective-permute-start(f32[2,192,128]{2,1,0:T(8,128)S(1)} %slice.129), channel_id=1, source_target_pairs={{1,0},{2,1},{3,2},{5,4},{6,5},{7,6},{9,8},{10,9},{11,10},{13,12},{... | collective-permute-start | bytes 589832 | tf_op jit(solution)/shard_map/ppermute | solution.py:22
  22.5 5.9 %collective-permute-start.5 = (f32[136,384]{1,0:T(8,128)S(1)}, f32[136,384]{1,0:T(8,128)S(1)}, u32[]{:S(2)}, u32[]{:S(2)}) collective-permute-start(f32[136,384]{1,0:T(8,128)S(1)} %get-tuple-element.35), channel_id=1, source_target_pairs={{0,4},{4,0},{8,12},{12,8},{16,20},{20,16},{24,28},{28,24},{1,5},{5... | collective-permute-start | bytes 626696 | tf_op jit(solution)/shard_map/ppermute | solution.py:26
  22.6 8.5 %collective-permute-start.11 = (f32[2,2,192,128]{3,2,1,0:T(8,128)S(1)}, f32[2,2,192,128]{3,2,1,0:T(8,128)S(1)}, u32[]{:S(2)}, u32[]{:S(2)}) collective-permute-start(f32[2,2,192,128]{3,2,1,0:T(8,128)S(1)} %get-tuple-element.47), channel_id=1, source_target_pairs={{0,1},{1,0},{2,3},{3,2},{4,5},{5,4},{6,7},{7,6},{8,9},{9,8},{10,11... | collective-permute-start | bytes 1179656 | tf_op jit(solution)/shard_map/ppermute | solution.py:26
  28.5 8.1 %collective-permute-start.6 = (f32[136,384]{1,0:T(8,128)S(1)}, f32[136,384]{1,0:T(8,128)S(1)}, u32[]{:S(2)}, u32[]{:S(2)}) collective-permute-start(f32[136,384]{1,0:T(8,128)S(1)} %get-tuple-element.75), channel_id=1, source_target_pairs={{0,8},{4,12},{16,24},{20,28},{8,0},{12,4},{24,16},{28,20},{1,9},{5... | collective-permute-start | bytes 626696 | tf_op jit(solution)/shard_map/ppermute | solution.py:31
  30.4 6.2 %collective-permute-start.7 = (f32[136,384]{1,0:T(8,128)S(1)}, f32[136,384]{1,0:T(8,128)S(1)}, u32[]{:S(2)}, u32[]{:S(2)}) collective-permute-start(f32[136,384]{1,0:T(8,128)S(1)} %get-tuple-element.74), channel_id=1, source_target_pairs={{8,16},{12,20},{16,8},{20,12},{9,17},{13,21},{17,9},{21,13},{10,18... | collective-permute-start | bytes 626696 | tf_op jit(solution)/shard_map/ppermute | solution.py:31
  31.2 6.8 %collective-permute-start.12 = (f32[192,128]{1,0:T(8,128)S(1)}, f32[192,128]{1,0:T(8,128)S(1)}, u32[]{:S(2)}, u32[]{:S(2)}) collective-permute-start(f32[192,128]{1,0:T(8,128)S(1)} %get-tuple-element.69), channel_id=1, source_target_pairs={{0,4},{1,5},{2,6},{3,7},{4,0},{5,1},{6,2},{7,3},{8,12},{9,13},{10,... | collective-permute-start | bytes 294920 | tf_op jit(solution)/shard_map/ppermute | solution.py:37
  31.9 7.4 %collective-permute-start.13 = (f32[192,128]{1,0:T(8,128)S(1)}, f32[192,128]{1,0:T(8,128)S(1)}, u32[]{:S(2)}, u32[]{:S(2)}) collective-permute-start(f32[192,128]{1,0:T(8,128)S(1)} %get-tuple-element.71), channel_id=1, source_target_pairs={{0,2},{1,3},{2,0},{3,1},{4,6},{5,7},{6,4},{7,5},{8,10},{9,11},{10,... | collective-permute-start | bytes 294920 | tf_op jit(solution)/shard_map/ppermute | solution.py:37
  35.8 6.2 %collective-permute-start.14 = (f32[192,128]{1,0:T(8,128)S(1)}, f32[192,128]{1,0:T(8,128)S(1)}, u32[]{:S(2)}, u32[]{:S(2)}) collective-permute-start(f32[192,128]{1,0:T(8,128)S(1)} %get-tuple-element.70), channel_id=1, source_target_pairs={{0,6},{1,7},{2,4},{3,5},{4,2},{5,3},{6,0},{7,1},{8,14},{9,15},{10,... | collective-permute-start | bytes 294920 | tf_op jit(solution)/shard_map/ppermute | solution.py:37
  37.3 14.3 %collective-permute-start.8 = (f32[264,128]{1,0:T(8,128)S(1)}, f32[264,128]{1,0:T(8,128)S(1)}, u32[]{:S(2)}, u32[]{:S(2)}) collective-permute-start(f32[264,128]{1,0:T(8,128)S(1)} %get-tuple-element.37), channel_id=1, source_target_pairs={{0,1},{2,3},{1,0},{3,2},{4,5},{6,7},{5,4},{7,6},{8,9},{10,11},{9,8... | collective-permute-start | bytes 405512 | tf_op jit(solution)/shard_map/ppermute | solution.py:31
  37.4 14.2 %collective-permute-start.9 = (f32[264,128]{1,0:T(8,128)S(1)}, f32[264,128]{1,0:T(8,128)S(1)}, u32[]{:S(2)}, u32[]{:S(2)}) collective-permute-start(f32[264,128]{1,0:T(8,128)S(1)} %get-tuple-element.38), channel_id=1, source_target_pairs={{1,2},{2,1},{5,6},{6,5},{9,10},{10,9},{13,14},{14,13},{17,18},{18,... | collective-permute-start | bytes 405512 | tf_op jit(solution)/shard_map/ppermute | solution.py:31
  42.0 7.4 %collective-permute-start.15 = (f32[192,128]{1,0:T(8,128)S(1)}, f32[192,128]{1,0:T(8,128)S(1)}, u32[]{:S(2)}, u32[]{:S(2)}) collective-permute-start(f32[192,128]{1,0:T(8,128)S(1)} %fusion.6), channel_id=1, source_target_pairs={{0,8},{4,12},{8,0},{12,4},{16,24},{20,28},{24,16},{28,20},{1,9},{5... | collective-permute-start | bytes 294920 | tf_op jit(solution)/shard_map/ppermute | solution.py:26
  49.5 7.5 %collective-permute-start.16 = (f32[192,128]{1,0:T(8,128)S(1)}, f32[192,128]{1,0:T(8,128)S(1)}, u32[]{:S(2)}, u32[]{:S(2)}) collective-permute-start(f32[192,128]{1,0:T(8,128)S(1)} %add.130), channel_id=1, source_target_pairs={{0,16},{4,20},{8,24},{12,28},{16,0},{20,4},{24,8},{28,12},{1,17},{... | collective-permute-start | bytes 294920 | tf_op jit(solution)/shard_map/ppermute | solution.py:26
  53.8 9.8 %collective-permute-start.10 = (f32[2,64,384]{2,1,0:T(8,128)S(1)}, f32[2,64,384]{2,1,0:T(8,128)S(1)}, u32[]{:S(2)}, u32[]{:S(2)}) collective-permute-start(f32[2,64,384]{2,1,0:T(8,128)S(1)} %get-tuple-element.42), channel_id=1, source_target_pairs={{0,4},{4,0},{8,12},{12,8},{16,20},{20,16},{24,28},{28,24},{1,5},{5... | collective-permute-start | bytes 589832 | tf_op jit(solution)/shard_map/ppermute | solution.py:26
  57.1 5.8 %collective-permute-start.17 = (f32[2,64,128]{2,1,0:T(8,128)S(1)}, f32[2,64,128]{2,1,0:T(8,128)S(1)}, u32[]{:S(2)}, u32[]{:S(2)}) collective-permute-start(f32[2,64,128]{2,1,0:T(8,128)S(1)} %bitcast_add_fusion.3), channel_id=1, source_target_pairs={{0,4},{1,5},{2,6},{3,7},{4,0},{5,1},{6,2},{7,3},{8,12},{9,13},{10,... | collective-permute-start | bytes 196616 | tf_op jit(solution)/shard_map/ppermute | solution.py:37
  57.8 5.1 %collective-permute-start.18 = (f32[2,64,128]{2,1,0:T(8,128)S(1)}, f32[2,64,128]{2,1,0:T(8,128)S(1)}, u32[]{:S(2)}, u32[]{:S(2)}) collective-permute-start(f32[2,64,128]{2,1,0:T(8,128)S(1)} %bitcast_add_fusion.3), channel_id=1, source_target_pairs={{0,2},{1,3},{2,0},{3,1},{4,6},{5,7},{6,4},{7,5},{8,10},{9,11},{10,... | collective-permute-start | bytes 196616 | tf_op jit(solution)/shard_map/ppermute | solution.py:37
  57.8 5.8 %collective-permute-start.19 = (f32[2,64,128]{2,1,0:T(8,128)S(1)}, f32[2,64,128]{2,1,0:T(8,128)S(1)}, u32[]{:S(2)}, u32[]{:S(2)}) collective-permute-start(f32[2,64,128]{2,1,0:T(8,128)S(1)} %bitcast_add_fusion.3), channel_id=1, source_target_pairs={{0,6},{1,7},{2,4},{3,5},{4,2},{5,3},{6,0},{7,1},{8,14},{9,15},{10,... | collective-permute-start | bytes 196616 | tf_op jit(solution)/shard_map/ppermute | solution.py:37
  63.6 1.6 %collective-permute-start.20 = (f32[2,2,2,64,128]{4,3,2,1,0:T(8,128)S(1)}, f32[2,2,2,64,128]{4,3,2,1,0:T(8,128)S(1)}, u32[]{:S(2)}, u32[]{:S(2)}) collective-permute-start(f32[2,2,2,64,128]{4,3,2,1,0:T(8,128)S(1)} %pad_maximum_fusion.4), channel_id=1, source_target_pairs={{0,1},{1,0},{2,3},{3,2},{4,5},{5,4},{6,7},{7,6},{8,9},{9,8},{10,11... | collective-permute-start | bytes 786440 | tf_op jit(solution)/shard_map/ppermute | solution.py:26
  69.3 1.8 %collective-permute-start.21 = (f32[2,2,192,128]{3,2,1,0:T(8,128)S(1)}, f32[2,2,192,128]{3,2,1,0:T(8,128)S(1)}, u32[]{:S(2)}, u32[]{:S(2)}) collective-permute-start(f32[2,2,192,128]{3,2,1,0:T(8,128)S(1)} %get-tuple-element.51), channel_id=1, source_target_pairs={{0,1},{1,0},{2,3},{3,2},{4,5},{5,4},{6,7},{7,6},{8,9},{9,8},{10,11... | collective-permute-start | bytes 1179656 | tf_op jit(solution)/shard_map/ppermute | solution.py:26
  71.2 4.9 %collective-permute-start.25 = (f32[192,128]{1,0:T(8,128)S(1)}, f32[192,128]{1,0:T(8,128)S(1)}, u32[]{:S(2)}, u32[]{:S(2)}) collective-permute-start(f32[192,128]{1,0:T(8,128)S(1)} %get-tuple-element.66), channel_id=1, source_target_pairs={{0,4},{1,5},{2,6},{3,7},{4,0},{5,1},{6,2},{7,3},{8,12},{9,13},{10,... | collective-permute-start | bytes 294920 | tf_op jit(solution)/shard_map/ppermute | solution.py:37
  72.2 5.2 %collective-permute-start.26 = (f32[192,128]{1,0:T(8,128)S(1)}, f32[192,128]{1,0:T(8,128)S(1)}, u32[]{:S(2)}, u32[]{:S(2)}) collective-permute-start(f32[192,128]{1,0:T(8,128)S(1)} %get-tuple-element.68), channel_id=1, source_target_pairs={{0,2},{1,3},{2,0},{3,1},{4,6},{5,7},{6,4},{7,5},{8,10},{9,11},{10,... | collective-permute-start | bytes 294920 | tf_op jit(solution)/shard_map/ppermute | solution.py:37
  74.0 5.6 %collective-permute-start.27 = (f32[192,128]{1,0:T(8,128)S(1)}, f32[192,128]{1,0:T(8,128)S(1)}, u32[]{:S(2)}, u32[]{:S(2)}) collective-permute-start(f32[192,128]{1,0:T(8,128)S(1)} %get-tuple-element.67), channel_id=1, source_target_pairs={{0,6},{1,7},{2,4},{3,5},{4,2},{5,3},{6,0},{7,1},{8,14},{9,15},{10,... | collective-permute-start | bytes 294920 | tf_op jit(solution)/shard_map/ppermute | solution.py:37
  74.8 8.3 %collective-permute-start.22 = (f32[128,384]{1,0:T(8,128)S(1)}, f32[128,384]{1,0:T(8,128)S(1)}, u32[]{:S(2)}, u32[]{:S(2)}) collective-permute-start(f32[128,384]{1,0:T(8,128)S(1)} %slice.117), channel_id=1, source_target_pairs={{0,4},{4,0},{8,12},{12,8},{16,20},{20,16},{24,28},{28,24},{1,5},{5... | collective-permute-start | bytes 589832 | tf_op jit(solution)/shard_map/ppermute | solution.py:26
  79.7 5.9 %collective-permute-start.28 = (f32[192,128]{1,0:T(8,128)S(1)}, f32[192,128]{1,0:T(8,128)S(1)}, u32[]{:S(2)}, u32[]{:S(2)}) collective-permute-start(f32[192,128]{1,0:T(8,128)S(1)} %fusion.8), channel_id=1, source_target_pairs={{0,8},{4,12},{8,0},{12,4},{16,24},{20,28},{24,16},{28,20},{1,9},{5... | collective-permute-start | bytes 294920 | tf_op jit(solution)/shard_map/ppermute | solution.py:26
  83.1 9.2 %collective-permute-start.23 = (f32[128,384]{1,0:T(8,128)S(1)}, f32[128,384]{1,0:T(8,128)S(1)}, u32[]{:S(2)}, u32[]{:S(2)}) collective-permute-start(f32[128,384]{1,0:T(8,128)S(1)} %multiply_add_fusion), channel_id=1, source_target_pairs={{0,8},{4,12},{8,16},{12,20},{16,24},{20,28},{1,9},{5,13},{9,17},{1... | collective-permute-start | bytes 589832 | tf_op jit(solution)/shard_map/ppermute | solution.py:22
  85.6 6.7 %collective-permute-start.29 = (f32[192,128]{1,0:T(8,128)S(1)}, f32[192,128]{1,0:T(8,128)S(1)}, u32[]{:S(2)}, u32[]{:S(2)}) collective-permute-start(f32[192,128]{1,0:T(8,128)S(1)} %add.144), channel_id=1, source_target_pairs={{0,16},{4,20},{8,24},{12,28},{16,0},{20,4},{24,8},{28,12},{1,17},{... | collective-permute-start | bytes 294920 | tf_op jit(solution)/shard_map/ppermute | solution.py:26
  92.4 4.3 %collective-permute-start.30 = (f32[2,64,128]{2,1,0:T(8,128)S(1)}, f32[2,64,128]{2,1,0:T(8,128)S(1)}, u32[]{:S(2)}, u32[]{:S(2)}) collective-permute-start(f32[2,64,128]{2,1,0:T(8,128)S(1)} %bitcast_add_fusion.1), channel_id=1, source_target_pairs={{0,4},{1,5},{2,6},{3,7},{4,0},{5,1},{6,2},{7,3},{8,12},{9,13},{10,... | collective-permute-start | bytes 196616 | tf_op jit(solution)/shard_map/ppermute | solution.py:37
  93.4 4.0 %collective-permute-start.24 = (f32[128,128]{1,0:T(8,128)S(1)}, f32[128,128]{1,0:T(8,128)S(1)}, u32[]{:S(2)}, u32[]{:S(2)}) collective-permute-start(f32[128,128]{1,0:T(8,128)S(1)} %slice.147), channel_id=1, source_target_pairs={{0,1},{1,2},{2,3},{4,5},{5,6},{6,7},{8,9},{9,10},{10,11},{12,13},{... | collective-permute-start | bytes 196616 | tf_op jit(solution)/shard_map/ppermute | solution.py:22
  (3 other events, 2.7 us)

commit v4 on v3

--- a/solution.py
+++ b/solution.py
@@ -420,12 +420,11 @@
         if not last:
             joined = joined_rows(terms)
         pass
-        for bit in bits_of("scan")[1:]:
+        for bit in bits_of("scan")[1:][:: -1 if last else 1]:
             own = own + swapped(own, "scan", bit)
             pass
         if not last:
             first, third, passed, entries = inner_update(first, third, probes, *joined)
-            own = after(own, passed)
         else:
             inner = last_update(first, probes, terms[:3], entries)
             own = after(own, inner)

time: 99.5 us -> 98.2 us (0.987)
  starting transfers between devices: 43.4 us -> 41.5 us
  waiting for transfers between devices: 33.7 us -> 34.7 us
    ppermute x12, starting transfers between devices: 19 us -> 17.1 us  [swapped(): lax.ppermute(value, axis, [(i, i ^ bit) for i in range(lax.axis_size(axis...]
where the time goes in v4:
time: 98.2 us; the launch traced here: 97 us
  starting transfers between devices  41.5 us (42%)
  waiting for transfers between devices  34.7 us (35%)
  Pallas kernels  13.7 us (14%)
  local copies, waits for them, and re-layouts  3.72 us (4%)
  between operations  1.81 us (2%)
  other arithmetic  1.65 us (2%)
    ppermute x12, waiting for transfers between devices, swapped(): lax.ppermute(value, axis, [(i, i ^ bit) for i in range(lax.axis_size(axis...  17.8 us
    ppermute x12, starting transfers between devices, swapped(): lax.ppermute(value, axis, [(i, i ^ bit) for i in range(lax.axis_size(axis...  17.1 us
    ppermute x10, starting transfers between devices, across(): lax.ppermute(value, ('scan', 'mode'), [(i, i ^ other) for i in range(scan...  13.6 us
    ppermute x10, waiting for transfers between devices, across(): lax.ppermute(value, ('scan', 'mode'), [(i, i ^ other) for i in range(scan...  12.7 us
    pallas_call x2, Pallas kernels, local(): call(wave_kernel, (*[sds(modes // 2, 2, 3 * half, length)] * 2, *[sds(row...  8.16 us
    ppermute x5, starting transfers between devices, shifted(): lax.ppermute(value, axis, [(source, source + steps) for source in range(i...  7.4 us
    ppermute x5, waiting for transfers between devices, shifted(): lax.ppermute(value, axis, [(source, source + steps) for source in range(i...  4.22 us
    ppermute x4, starting transfers between devices, paired(): lax.ppermute(value, axis, [(i, i + step) for i in lower] + [(i + step, i)...  3.35 us
  transfers between devices with their start and end apart: 31, of which 18 were waited for; matrix products, arithmetic and copies ran while one was open for 3% of the time, Pallas kernels for 6%

profile of v4, /device:TPU:0, one launch (start us, length us, event | category | flops | bytes accessed | tf_op | source)
XLA Modules:
  0.0 97.0 jit_solution(11225347253328446389)
XLA Ops:
  0.6 1.3 %collective-permute-start = (f32[2,64,256]{2,1,0:T(8,128)}, f32[2,64,256]{2,1,0:T(8,128)S(1)}, u32[]{:S(2)}, u32[]{:S(2)}) collective-permute-start(f32[2,64,256]{2,1,0:T(8,128)} %param.6), channel_id=1, source_target_pairs={{4,0},{8,4},{12,8},{16,12},{20,16},{24,20},{28,24},{5,1},{9,5},{13... | collective-permute-start | bytes 393224 | tf_op jit(solution)/shard_map/ppermute | solution.py:22
  1.9 1.3 %collective-permute-start.1 = (f32[2,64,256]{2,1,0:T(8,128)}, f32[2,64,256]{2,1,0:T(8,128)S(1)}, u32[]{:S(2)}, u32[]{:S(2)}) collective-permute-start(f32[2,64,256]{2,1,0:T(8,128)} %param.6), channel_id=1, source_target_pairs={{8,0},{12,4},{16,8},{20,12},{24,16},{28,20},{9,1},{13,5},{17,9},{2... | collective-permute-start | bytes 393224 | tf_op jit(solution)/shard_map/ppermute | solution.py:22
  4.2 3.0 %collective-permute-start.3 = (f32[1,2,2,64,128]{4,3,2,1,0:T(8,128)S(1)}, f32[1,2,2,64,128]{4,3,2,1,0:T(8,128)S(1)}, u32[]{:S(2)}, u32[]{:S(2)}) collective-permute-start(f32[1,2,2,64,128]{4,3,2,1,0:T(8,128)S(1)} %reverse_select_fusion.1), channel_id=1, source_target_pairs={{0,2},{1,3},{2,0},{3,1},{4,6},{5,7},{6,4},{7,5},{8,10},{9,11},{10,... | collective-permute-start | bytes 393224 | tf_op jit(solution)/shard_map/ppermute | solution.py:26
  9.1 1.6 %collective-permute-done.3 = f32[1,2,2,64,128]{4,3,2,1,0:T(8,128)S(1)} collective-permute-done((f32[1,2,2,64,128]{4,3,2,1,0:T(8,128)S(1)}, f32[1,2,2,64,128]{4,3,2,1,0:T(8,128)S(1)}, u32[]{:S(2)}, u32[]{:S(2)}) %collective-permute-start.3) | collective-permute-done | bytes 131104 | tf_op jit(solution)/shard_map/ppermute | solution.py:26
  10.8 2.4 %collective-permute-done.1 = f32[2,64,256]{2,1,0:T(8,128)S(1)} collective-permute-done((f32[2,64,256]{2,1,0:T(8,128)}, f32[2,64,256]{2,1,0:T(8,128)S(1)}, u32[]{:S(2)}, u32[]{:S(2)}) %collective-permute-start.1) | collective-permute-done | bytes 131104 | tf_op jit(solution)/shard_map/ppermute | solution.py:22
  13.2 1.3 %collective-permute-start.2 = (f32[2,192,128]{2,1,0:T(8,128)S(1)}, f32[2,192,128]{2,1,0:T(8,128)S(1)}, u32[]{:S(2)}, u32[]{:S(2)}) collective-permute-start(f32[2,192,128]{2,1,0:T(8,128)S(1)} %slice.129), channel_id=1, source_target_pairs={{1,0},{2,1},{3,2},{5,4},{6,5},{7,6},{9,8},{10,9},{11,10},{13,12},{... | collective-permute-start | bytes 589832 | tf_op jit(solution)/shard_map/ppermute | solution.py:22
  14.7 1.9 %collective-permute-done.2 = f32[2,192,128]{2,1,0:T(8,128)S(1)} collective-permute-done((f32[2,192,128]{2,1,0:T(8,128)S(1)}, f32[2,192,128]{2,1,0:T(8,128)S(1)}, u32[]{:S(2)}, u32[]{:S(2)}) %collective-permute-start.2) | collective-permute-done | bytes 196640 | tf_op jit(solution)/shard_map/ppermute | solution.py:22
  18.4 4.1 %shard_map.78 = (f32[2,2,192,128]{3,2,1,0:T(8,128)S(1)}, f32[2,2,192,128]{3,2,1,0:T(8,128)S(1)}, f32[136,384]{1,0:T(8,128)S(1)}, f32[136,384]{1,0:T(8,128)S(1)}, f32[136,384]{1,0:T(8,128)S(1)}) custom-call(s32[6]{0:T(128)S(1)} %reshape.96.place, s32[2]{0:T(128)S(1)} %pad_add_fusion.2.me, f32[2,2,128,128]{3,2,1,0:T(8,128)S(1)} %get-tuple-element.30.patch, ...), custom_call_target="tpu_custom_call" | custom-call | flops 1610612736 | bytes 4194304 | tf_op jit(solution)/shard_map/pallas_call | solution.py:404
  22.6 3.9 %collective-permute-start.11 = (f32[2,2,192,128]{3,2,1,0:T(8,128)S(1)}, f32[2,2,192,128]{3,2,1,0:T(8,128)S(1)}, u32[]{:S(2)}, u32[]{:S(2)}) collective-permute-start(f32[2,2,192,128]{3,2,1,0:T(8,128)S(1)} %get-tuple-element.46), channel_id=1, source_target_pairs={{0,1},{1,0},{2,3},{3,2},{4,5},{5,4},{6,7},{7,6},{8,9},{9,8},{10,11... | collective-permute-start | bytes 1179656 | tf_op jit(solution)/shard_map/ppermute | solution.py:26
  26.5 1.9 %collective-permute-done.5 = f32[136,384]{1,0:T(8,128)S(1)} collective-permute-done((f32[136,384]{1,0:T(8,128)S(1)}, f32[136,384]{1,0:T(8,128)S(1)}, u32[]{:S(2)}, u32[]{:S(2)}) %collective-permute-start.5) | collective-permute-done | bytes 208928 | tf_op jit(solution)/shard_map/ppermute | solution.py:26
  28.5 1.9 %collective-permute-start.6 = (f32[136,384]{1,0:T(8,128)S(1)}, f32[136,384]{1,0:T(8,128)S(1)}, u32[]{:S(2)}, u32[]{:S(2)}) collective-permute-start(f32[136,384]{1,0:T(8,128)S(1)} %get-tuple-element.73), channel_id=1, source_target_pairs={{0,8},{4,12},{16,24},{20,28},{8,0},{12,4},{24,16},{28,20},{1,9},{5... | collective-permute-start | bytes 626696 | tf_op jit(solution)/shard_map/ppermute | solution.py:31
  31.9 3.9 %collective-permute-start.13 = (f32[192,128]{1,0:T(8,128)S(1)}, f32[192,128]{1,0:T(8,128)S(1)}, u32[]{:S(2)}, u32[]{:S(2)}) collective-permute-start(f32[192,128]{1,0:T(8,128)S(1)} %get-tuple-element.69), channel_id=1, source_target_pairs={{0,2},{1,3},{2,0},{3,1},{4,6},{5,7},{6,4},{7,5},{8,10},{9,11},{10,... | collective-permute-start | bytes 294920 | tf_op jit(solution)/shard_map/ppermute | solution.py:37
  38.1 1.3 %collective-permute-done.13 = f32[192,128]{1,0:T(8,128)S(1)} collective-permute-done((f32[192,128]{1,0:T(8,128)S(1)}, f32[192,128]{1,0:T(8,128)S(1)}, u32[]{:S(2)}, u32[]{:S(2)}) %collective-permute-start.13) | collective-permute-done | bytes 98336 | tf_op jit(solution)/shard_map/ppermute | solution.py:37
  39.3 2.7 %collective-permute-done.14 = f32[192,128]{1,0:T(8,128)S(1)} collective-permute-done((f32[192,128]{1,0:T(8,128)S(1)}, f32[192,128]{1,0:T(8,128)S(1)}, u32[]{:S(2)}, u32[]{:S(2)}) %collective-permute-start.14) | collective-permute-done | bytes 98336 | tf_op jit(solution)/shard_map/ppermute | solution.py:37
  42.0 4.6 %collective-permute-start.15 = (f32[192,128]{1,0:T(8,128)S(1)}, f32[192,128]{1,0:T(8,128)S(1)}, u32[]{:S(2)}, u32[]{:S(2)}) collective-permute-start(f32[192,128]{1,0:T(8,128)S(1)} %fusion.6), channel_id=1, source_target_pairs={{0,8},{4,12},{8,0},{12,4},{16,24},{20,28},{24,16},{28,20},{1,9},{5... | collective-permute-start | bytes 294920 | tf_op jit(solution)/shard_map/ppermute | solution.py:26
  46.6 2.8 %collective-permute-done.15 = f32[192,128]{1,0:T(8,128)S(1)} collective-permute-done((f32[192,128]{1,0:T(8,128)S(1)}, f32[192,128]{1,0:T(8,128)S(1)}, u32[]{:S(2)}, u32[]{:S(2)}) %collective-permute-start.15) | collective-permute-done | bytes 98336 | tf_op jit(solution)/shard_map/ppermute | solution.py:26
  49.5 2.1 %collective-permute-start.16 = (f32[192,128]{1,0:T(8,128)S(1)}, f32[192,128]{1,0:T(8,128)S(1)}, u32[]{:S(2)}, u32[]{:S(2)}) collective-permute-start(f32[192,128]{1,0:T(8,128)S(1)} %add.130), channel_id=1, source_target_pairs={{0,16},{4,20},{8,24},{12,28},{16,0},{20,4},{24,8},{28,12},{1,17},{... | collective-permute-start | bytes 294920 | tf_op jit(solution)/shard_map/ppermute | solution.py:26
  51.6 2.1 %shard_map.80 = (f32[2,64,384]{2,1,0:T(8,128)S(1)}, f32[2,64,384]{2,1,0:T(8,128)S(1)}, f32[2,64,384]{2,1,0:T(8,128)S(1)}) custom-call(s32[1024]{0:T(1024)S(1)} %fusion.10.table, s32[2]{0:T(128)S(1)} %pad_add_fusion.2.me, f32[2,64,384]{2,1,0:T(8,128)S(1)} %get-tuple-element.63.first, f32[2,64,384]{2,1,0:T(8,128)S(1)} %get-tuple-element.61.third, ...), custom_call_target="tpu_custom_call" | custom-call | flops 1048576 | bytes 1048576 | tf_op jit(solution)/shard_map/pallas_call | solution.py:356
  54.7 2.3 %collective-permute-done.16 = f32[192,128]{1,0:T(8,128)S(1)} collective-permute-done((f32[192,128]{1,0:T(8,128)S(1)}, f32[192,128]{1,0:T(8,128)S(1)}, u32[]{:S(2)}, u32[]{:S(2)}) %collective-permute-start.16) | collective-permute-done | bytes 98336 | tf_op jit(solution)/shard_map/ppermute | solution.py:26
  57.8 2.8 %collective-permute-start.19 = (f32[2,64,128]{2,1,0:T(8,128)S(1)}, f32[2,64,128]{2,1,0:T(8,128)S(1)}, u32[]{:S(2)}, u32[]{:S(2)}) collective-permute-start(f32[2,64,128]{2,1,0:T(8,128)S(1)} %bitcast_add_fusion.3), channel_id=1, source_target_pairs={{0,6},{1,7},{2,4},{3,5},{4,2},{5,3},{6,0},{7,1},{8,14},{9,15},{10,... | collective-permute-start | bytes 196616 | tf_op jit(solution)/shard_map/ppermute | solution.py:37
  60.6 3.2 %collective-permute-done.17 = f32[2,64,128]{2,1,0:T(8,128)S(1)} collective-permute-done((f32[2,64,128]{2,1,0:T(8,128)S(1)}, f32[2,64,128]{2,1,0:T(8,128)S(1)}, u32[]{:S(2)}, u32[]{:S(2)}) %collective-permute-start.17) | collective-permute-done | bytes 65568 | tf_op jit(solution)/shard_map/ppermute | solution.py:37
  65.5 4.1 %shard_map.82 = (f32[2,2,192,128]{3,2,1,0:T(8,128)S(1)}, f32[2,2,192,128]{3,2,1,0:T(8,128)S(1)}, f32[136,384]{1,0:T(8,128)S(1)}, f32[136,384]{1,0:T(8,128)S(1)}, f32[136,384]{1,0:T(8,128)S(1)}) custom-call(s32[6]{0:T(128)S(1)} %reshape.96.place, s32[2]{0:T(128)S(1)} %pad_add_fusion.2.me, f32[2,2,128,128]{3,2,1,0:T(8,128)S(1)} %get-tuple-element.43.patch, ...), custom_call_target="tpu_custom_call" | custom-call | flops 1610612736 | bytes 4194304 | tf_op jit(solution)/shard_map/pallas_call | solution.py:404
  69.8 1.6 %collective-permute-done.21 = f32[2,2,192,128]{3,2,1,0:T(8,128)S(1)} collective-permute-done((f32[2,2,192,128]{3,2,1,0:T(8,128)S(1)}, f32[2,2,192,128]{3,2,1,0:T(8,128)S(1)}, u32[]{:S(2)}, u32[]{:S(2)}) %collective-permute-start.21) | collective-permute-done | bytes 393248 | tf_op jit(solution)/shard_map/ppermute | solution.py:26
  72.5 1.6 %collective-permute-start.26 = (f32[192,128]{1,0:T(8,128)S(1)}, f32[192,128]{1,0:T(8,128)S(1)}, u32[]{:S(2)}, u32[]{:S(2)}) collective-permute-start(f32[192,128]{1,0:T(8,128)S(1)} %get-tuple-element.66), channel_id=1, source_target_pairs={{0,2},{1,3},{2,0},{3,1},{4,6},{5,7},{6,4},{7,5},{8,10},{9,11},{10,... | collective-permute-start | bytes 294920 | tf_op jit(solution)/shard_map/ppermute | solution.py:37
  76.4 1.4 %collective-permute-done.26 = f32[192,128]{1,0:T(8,128)S(1)} collective-permute-done((f32[192,128]{1,0:T(8,128)S(1)}, f32[192,128]{1,0:T(8,128)S(1)}, u32[]{:S(2)}, u32[]{:S(2)}) %collective-permute-start.26) | collective-permute-done | bytes 98336 | tf_op jit(solution)/shard_map/ppermute | solution.py:37
  77.8 2.0 %collective-permute-done.27 = f32[192,128]{1,0:T(8,128)S(1)} collective-permute-done((f32[192,128]{1,0:T(8,128)S(1)}, f32[192,128]{1,0:T(8,128)S(1)}, u32[]{:S(2)}, u32[]{:S(2)}) %collective-permute-start.27) | collective-permute-done | bytes 98336 | tf_op jit(solution)/shard_map/ppermute | solution.py:37
  80.7 2.6 %collective-permute-done.22 = f32[128,384]{1,0:T(8,128)S(1)} collective-permute-done((f32[128,384]{1,0:T(8,128)S(1)}, f32[128,384]{1,0:T(8,128)S(1)}, u32[]{:S(2)}, u32[]{:S(2)}) %collective-permute-start.22) | collective-permute-done | bytes 196640 | tf_op jit(solution)/shard_map/ppermute | solution.py:26
  83.4 2.2 %collective-permute-start.23 = (f32[128,384]{1,0:T(8,128)S(1)}, f32[128,384]{1,0:T(8,128)S(1)}, u32[]{:S(2)}, u32[]{:S(2)}) collective-permute-start(f32[128,384]{1,0:T(8,128)S(1)} %multiply_add_fusion), channel_id=1, source_target_pairs={{0,8},{4,12},{8,16},{12,20},{16,24},{20,28},{1,9},{5,13},{9,17},{1... | collective-permute-start | bytes 589832 | tf_op jit(solution)/shard_map/ppermute | solution.py:22
  87.8 3.4 %collective-permute-done.29 = f32[192,128]{1,0:T(8,128)S(1)} collective-permute-done((f32[192,128]{1,0:T(8,128)S(1)}, f32[192,128]{1,0:T(8,128)S(1)}, u32[]{:S(2)}, u32[]{:S(2)}) %collective-permute-start.29) | collective-permute-done | bytes 98336 | tf_op jit(solution)/shard_map/ppermute | solution.py:26
  91.3 1.1 %collective-permute-start.30 = (f32[2,64,128]{2,1,0:T(8,128)S(1)}, f32[2,64,128]{2,1,0:T(8,128)S(1)}, u32[]{:S(2)}, u32[]{:S(2)}) collective-permute-start(f32[2,64,128]{2,1,0:T(8,128)S(1)} %bitcast_add_fusion.1), channel_id=1, source_target_pairs={{0,4},{1,5},{2,6},{3,7},{4,0},{5,1},{6,2},{7,3},{8,12},{9,13},{10,... | collective-permute-start | bytes 196616 | tf_op jit(solution)/shard_map/ppermute | solution.py:37
  92.4 1.3 %collective-permute-start.24 = (f32[128,128]{1,0:T(8,128)S(1)}, f32[128,128]{1,0:T(8,128)S(1)}, u32[]{:S(2)}, u32[]{:S(2)}) collective-permute-start(f32[128,128]{1,0:T(8,128)S(1)} %slice.149), channel_id=1, source_target_pairs={{0,1},{1,2},{2,3},{4,5},{5,6},{6,7},{8,9},{9,10},{10,11},{12,13},{... | collective-permute-start | bytes 196616 | tf_op jit(solution)/shard_map/ppermute | solution.py:22
  93.7 1.9 %collective-permute-done.30 = f32[2,64,128]{2,1,0:T(8,128)S(1)} collective-permute-done((f32[2,64,128]{2,1,0:T(8,128)S(1)}, f32[2,64,128]{2,1,0:T(8,128)S(1)}, u32[]{:S(2)}, u32[]{:S(2)}) %collective-permute-start.30) | collective-permute-done | bytes 65568 | tf_op jit(solution)/shard_map/ppermute | solution.py:37
  (108 shorter events, 19.9 us)
Async XLA Ops:
  0.6 10.2 %collective-permute-start = (f32[2,64,256]{2,1,0:T(8,128)}, f32[2,64,256]{2,1,0:T(8,128)S(1)}, u32[]{:S(2)}, u32[]{:S(2)}) collective-permute-start(f32[2,64,256]{2,1,0:T(8,128)} %param.6), channel_id=1, source_target_pairs={{4,0},{8,4},{12,8},{16,12},{20,16},{24,20},{28,24},{5,1},{9,5},{13... | collective-permute-start | bytes 393224 | tf_op jit(solution)/shard_map/ppermute | solution.py:22
  1.9 11.3 %collective-permute-start.1 = (f32[2,64,256]{2,1,0:T(8,128)}, f32[2,64,256]{2,1,0:T(8,128)S(1)}, u32[]{:S(2)}, u32[]{:S(2)}) collective-permute-start(f32[2,64,256]{2,1,0:T(8,128)} %param.6), channel_id=1, source_target_pairs={{8,0},{12,4},{16,8},{20,12},{24,16},{28,20},{9,1},{13,5},{17,9},{2... | collective-permute-start | bytes 393224 | tf_op jit(solution)/shard_map/ppermute | solution.py:22
  4.2 4.9 %copy-start.2 = (f32[2,64,256]{2,1,0:T(8,128)S(1)}, f32[2,64,256]{2,1,0:T(8,128)}, u32[]{:S(2)}) copy-start(f32[2,64,256]{2,1,0:T(8,128)} %param.6) | copy-start | bytes 393220
  4.2 6.5 %collective-permute-start.3 = (f32[1,2,2,64,128]{4,3,2,1,0:T(8,128)S(1)}, f32[1,2,2,64,128]{4,3,2,1,0:T(8,128)S(1)}, u32[]{:S(2)}, u32[]{:S(2)}) collective-permute-start(f32[1,2,2,64,128]{4,3,2,1,0:T(8,128)S(1)} %reverse_select_fusion.1), channel_id=1, source_target_pairs={{0,2},{1,3},{2,0},{3,1},{4,6},{5,7},{6,4},{7,5},{8,10},{9,11},{10,... | collective-permute-start | bytes 393224 | tf_op jit(solution)/shard_map/ppermute | solution.py:26
  10.7 6.7 %collective-permute-start.4 = (f32[2,2,2,64,128]{4,3,2,1,0:T(8,128)S(1)}, f32[2,2,2,64,128]{4,3,2,1,0:T(8,128)S(1)}, u32[]{:S(2)}, u32[]{:S(2)}) collective-permute-start(f32[2,2,2,64,128]{4,3,2,1,0:T(8,128)S(1)} %pad_maximum_fusion.3), channel_id=1, source_target_pairs={{0,1},{1,0},{2,3},{3,2},{4,5},{5,4},{6,7},{7,6},{8,9},{9,8},{10,11... | collective-permute-start | bytes 786440 | tf_op jit(solution)/shard_map/ppermute | solution.py:26
  13.2 3.3 %collective-permute-start.2 = (f32[2,192,128]{2,1,0:T(8,128)S(1)}, f32[2,192,128]{2,1,0:T(8,128)S(1)}, u32[]{:S(2)}, u32[]{:S(2)}) collective-permute-start(f32[2,192,128]{2,1,0:T(8,128)S(1)} %slice.129), channel_id=1, source_target_pairs={{1,0},{2,1},{3,2},{5,4},{6,5},{7,6},{9,8},{10,9},{11,10},{13,12},{... | collective-permute-start | bytes 589832 | tf_op jit(solution)/shard_map/ppermute | solution.py:22
  22.5 5.9 %collective-permute-start.5 = (f32[136,384]{1,0:T(8,128)S(1)}, f32[136,384]{1,0:T(8,128)S(1)}, u32[]{:S(2)}, u32[]{:S(2)}) collective-permute-start(f32[136,384]{1,0:T(8,128)S(1)} %get-tuple-element.34), channel_id=1, source_target_pairs={{0,4},{4,0},{8,12},{12,8},{16,20},{20,16},{24,28},{28,24},{1,5},{5... | collective-permute-start | bytes 626696 | tf_op jit(solution)/shard_map/ppermute | solution.py:26
  22.6 8.5 %collective-permute-start.11 = (f32[2,2,192,128]{3,2,1,0:T(8,128)S(1)}, f32[2,2,192,128]{3,2,1,0:T(8,128)S(1)}, u32[]{:S(2)}, u32[]{:S(2)}) collective-permute-start(f32[2,2,192,128]{3,2,1,0:T(8,128)S(1)} %get-tuple-element.46), channel_id=1, source_target_pairs={{0,1},{1,0},{2,3},{3,2},{4,5},{5,4},{6,7},{7,6},{8,9},{9,8},{10,11... | collective-permute-start | bytes 1179656 | tf_op jit(solution)/shard_map/ppermute | solution.py:26
  28.5 8.1 %collective-permute-start.6 = (f32[136,384]{1,0:T(8,128)S(1)}, f32[136,384]{1,0:T(8,128)S(1)}, u32[]{:S(2)}, u32[]{:S(2)}) collective-permute-start(f32[136,384]{1,0:T(8,128)S(1)} %get-tuple-element.73), channel_id=1, source_target_pairs={{0,8},{4,12},{16,24},{20,28},{8,0},{12,4},{24,16},{28,20},{1,9},{5... | collective-permute-start | bytes 626696 | tf_op jit(solution)/shard_map/ppermute | solution.py:31
  30.4 6.2 %collective-permute-start.7 = (f32[136,384]{1,0:T(8,128)S(1)}, f32[136,384]{1,0:T(8,128)S(1)}, u32[]{:S(2)}, u32[]{:S(2)}) collective-permute-start(f32[136,384]{1,0:T(8,128)S(1)} %get-tuple-element.72), channel_id=1, source_target_pairs={{8,16},{12,20},{16,8},{20,12},{9,17},{13,21},{17,9},{21,13},{10,18... | collective-permute-start | bytes 626696 | tf_op jit(solution)/shard_map/ppermute | solution.py:31
  31.2 6.8 %collective-permute-start.12 = (f32[192,128]{1,0:T(8,128)S(1)}, f32[192,128]{1,0:T(8,128)S(1)}, u32[]{:S(2)}, u32[]{:S(2)}) collective-permute-start(f32[192,128]{1,0:T(8,128)S(1)} %get-tuple-element.67), channel_id=1, source_target_pairs={{0,4},{1,5},{2,6},{3,7},{4,0},{5,1},{6,2},{7,3},{8,12},{9,13},{10,... | collective-permute-start | bytes 294920 | tf_op jit(solution)/shard_map/ppermute | solution.py:37
  31.9 7.4 %collective-permute-start.13 = (f32[192,128]{1,0:T(8,128)S(1)}, f32[192,128]{1,0:T(8,128)S(1)}, u32[]{:S(2)}, u32[]{:S(2)}) collective-permute-start(f32[192,128]{1,0:T(8,128)S(1)} %get-tuple-element.69), channel_id=1, source_target_pairs={{0,2},{1,3},{2,0},{3,1},{4,6},{5,7},{6,4},{7,5},{8,10},{9,11},{10,... | collective-permute-start | bytes 294920 | tf_op jit(solution)/shard_map/ppermute | solution.py:37
  35.8 6.2 %collective-permute-start.14 = (f32[192,128]{1,0:T(8,128)S(1)}, f32[192,128]{1,0:T(8,128)S(1)}, u32[]{:S(2)}, u32[]{:S(2)}) collective-permute-start(f32[192,128]{1,0:T(8,128)S(1)} %get-tuple-element.68), channel_id=1, source_target_pairs={{0,6},{1,7},{2,4},{3,5},{4,2},{5,3},{6,0},{7,1},{8,14},{9,15},{10,... | collective-permute-start | bytes 294920 | tf_op jit(solution)/shard_map/ppermute | solution.py:37
  37.3 14.3 %collective-permute-start.8 = (f32[264,128]{1,0:T(8,128)S(1)}, f32[264,128]{1,0:T(8,128)S(1)}, u32[]{:S(2)}, u32[]{:S(2)}) collective-permute-start(f32[264,128]{1,0:T(8,128)S(1)} %get-tuple-element.36), channel_id=1, source_target_pairs={{0,1},{2,3},{1,0},{3,2},{4,5},{6,7},{5,4},{7,6},{8,9},{10,11},{9,8... | collective-permute-start | bytes 405512 | tf_op jit(solution)/shard_map/ppermute | solution.py:31
  37.4 14.2 %collective-permute-start.9 = (f32[264,128]{1,0:T(8,128)S(1)}, f32[264,128]{1,0:T(8,128)S(1)}, u32[]{:S(2)}, u32[]{:S(2)}) collective-permute-start(f32[264,128]{1,0:T(8,128)S(1)} %get-tuple-element.37), channel_id=1, source_target_pairs={{1,2},{2,1},{5,6},{6,5},{9,10},{10,9},{13,14},{14,13},{17,18},{18,... | collective-permute-start | bytes 405512 | tf_op jit(solution)/shard_map/ppermute | solution.py:31
  42.0 7.4 %collective-permute-start.15 = (f32[192,128]{1,0:T(8,128)S(1)}, f32[192,128]{1,0:T(8,128)S(1)}, u32[]{:S(2)}, u32[]{:S(2)}) collective-permute-start(f32[192,128]{1,0:T(8,128)S(1)} %fusion.6), channel_id=1, source_target_pairs={{0,8},{4,12},{8,0},{12,4},{16,24},{20,28},{24,16},{28,20},{1,9},{5... | collective-permute-start | bytes 294920 | tf_op jit(solution)/shard_map/ppermute | solution.py:26
  49.5 7.5 %collective-permute-start.16 = (f32[192,128]{1,0:T(8,128)S(1)}, f32[192,128]{1,0:T(8,128)S(1)}, u32[]{:S(2)}, u32[]{:S(2)}) collective-permute-start(f32[192,128]{1,0:T(8,128)S(1)} %add.130), channel_id=1, source_target_pairs={{0,16},{4,20},{8,24},{12,28},{16,0},{20,4},{24,8},{28,12},{1,17},{... | collective-permute-start | bytes 294920 | tf_op jit(solution)/shard_map/ppermute | solution.py:26
  53.7 10.1 %collective-permute-start.10 = (f32[2,64,384]{2,1,0:T(8,128)S(1)}, f32[2,64,384]{2,1,0:T(8,128)S(1)}, u32[]{:S(2)}, u32[]{:S(2)}) collective-permute-start(f32[2,64,384]{2,1,0:T(8,128)S(1)} %get-tuple-element.41), channel_id=1, source_target_pairs={{0,4},{4,0},{8,12},{12,8},{16,20},{20,16},{24,28},{28,24},{1,5},{5... | collective-permute-start | bytes 589832 | tf_op jit(solution)/shard_map/ppermute | solution.py:26
  57.1 6.7 %collective-permute-start.17 = (f32[2,64,128]{2,1,0:T(8,128)S(1)}, f32[2,64,128]{2,1,0:T(8,128)S(1)}, u32[]{:S(2)}, u32[]{:S(2)}) collective-permute-start(f32[2,64,128]{2,1,0:T(8,128)S(1)} %bitcast_add_fusion.3), channel_id=1, source_target_pairs={{0,4},{1,5},{2,6},{3,7},{4,0},{5,1},{6,2},{7,3},{8,12},{9,13},{10,... | collective-permute-start | bytes 196616 | tf_op jit(solution)/shard_map/ppermute | solution.py:37
  57.8 6.0 %collective-permute-start.18 = (f32[2,64,128]{2,1,0:T(8,128)S(1)}, f32[2,64,128]{2,1,0:T(8,128)S(1)}, u32[]{:S(2)}, u32[]{:S(2)}) collective-permute-start(f32[2,64,128]{2,1,0:T(8,128)S(1)} %bitcast_add_fusion.3), channel_id=1, source_target_pairs={{0,2},{1,3},{2,0},{3,1},{4,6},{5,7},{6,4},{7,5},{8,10},{9,11},{10,... | collective-permute-start | bytes 196616 | tf_op jit(solution)/shard_map/ppermute | solution.py:37
  57.8 6.0 %collective-permute-start.19 = (f32[2,64,128]{2,1,0:T(8,128)S(1)}, f32[2,64,128]{2,1,0:T(8,128)S(1)}, u32[]{:S(2)}, u32[]{:S(2)}) collective-permute-start(f32[2,64,128]{2,1,0:T(8,128)S(1)} %bitcast_add_fusion.3), channel_id=1, source_target_pairs={{0,6},{1,7},{2,4},{3,5},{4,2},{5,3},{6,0},{7,1},{8,14},{9,15},{10,... | collective-permute-start | bytes 196616 | tf_op jit(solution)/shard_map/ppermute | solution.py:37
  63.9 1.6 %collective-permute-start.20 = (f32[2,2,2,64,128]{4,3,2,1,0:T(8,128)S(1)}, f32[2,2,2,64,128]{4,3,2,1,0:T(8,128)S(1)}, u32[]{:S(2)}, u32[]{:S(2)}) collective-permute-start(f32[2,2,2,64,128]{4,3,2,1,0:T(8,128)S(1)} %pad_maximum_fusion.4), channel_id=1, source_target_pairs={{0,1},{1,0},{2,3},{3,2},{4,5},{5,4},{6,7},{7,6},{8,9},{9,8},{10,11... | collective-permute-start | bytes 786440 | tf_op jit(solution)/shard_map/ppermute | solution.py:26
  69.6 1.8 %collective-permute-start.21 = (f32[2,2,192,128]{3,2,1,0:T(8,128)S(1)}, f32[2,2,192,128]{3,2,1,0:T(8,128)S(1)}, u32[]{:S(2)}, u32[]{:S(2)}) collective-permute-start(f32[2,2,192,128]{3,2,1,0:T(8,128)S(1)} %get-tuple-element.49), channel_id=1, source_target_pairs={{0,1},{1,0},{2,3},{3,2},{4,5},{5,4},{6,7},{7,6},{8,9},{9,8},{10,11... | collective-permute-start | bytes 1179656 | tf_op jit(solution)/shard_map/ppermute | solution.py:26
  71.5 4.9 %collective-permute-start.25 = (f32[192,128]{1,0:T(8,128)S(1)}, f32[192,128]{1,0:T(8,128)S(1)}, u32[]{:S(2)}, u32[]{:S(2)}) collective-permute-start(f32[192,128]{1,0:T(8,128)S(1)} %get-tuple-element.64), channel_id=1, source_target_pairs={{0,4},{1,5},{2,6},{3,7},{4,0},{5,1},{6,2},{7,3},{8,12},{9,13},{10,... | collective-permute-start | bytes 294920 | tf_op jit(solution)/shard_map/ppermute | solution.py:37
  72.5 5.3 %collective-permute-start.26 = (f32[192,128]{1,0:T(8,128)S(1)}, f32[192,128]{1,0:T(8,128)S(1)}, u32[]{:S(2)}, u32[]{:S(2)}) collective-permute-start(f32[192,128]{1,0:T(8,128)S(1)} %get-tuple-element.66), channel_id=1, source_target_pairs={{0,2},{1,3},{2,0},{3,1},{4,6},{5,7},{6,4},{7,5},{8,10},{9,11},{10,... | collective-permute-start | bytes 294920 | tf_op jit(solution)/shard_map/ppermute | solution.py:37
  74.0 5.7 %collective-permute-start.27 = (f32[192,128]{1,0:T(8,128)S(1)}, f32[192,128]{1,0:T(8,128)S(1)}, u32[]{:S(2)}, u32[]{:S(2)}) collective-permute-start(f32[192,128]{1,0:T(8,128)S(1)} %get-tuple-element.65), channel_id=1, source_target_pairs={{0,6},{1,7},{2,4},{3,5},{4,2},{5,3},{6,0},{7,1},{8,14},{9,15},{10,... | collective-permute-start | bytes 294920 | tf_op jit(solution)/shard_map/ppermute | solution.py:37
  75.1 8.3 %collective-permute-start.22 = (f32[128,384]{1,0:T(8,128)S(1)}, f32[128,384]{1,0:T(8,128)S(1)}, u32[]{:S(2)}, u32[]{:S(2)}) collective-permute-start(f32[128,384]{1,0:T(8,128)S(1)} %slice.117), channel_id=1, source_target_pairs={{0,4},{4,0},{8,12},{12,8},{16,20},{20,16},{24,28},{28,24},{1,5},{5... | collective-permute-start | bytes 589832 | tf_op jit(solution)/shard_map/ppermute | solution.py:26
  79.8 6.6 %collective-permute-start.28 = (f32[192,128]{1,0:T(8,128)S(1)}, f32[192,128]{1,0:T(8,128)S(1)}, u32[]{:S(2)}, u32[]{:S(2)}) collective-permute-start(f32[192,128]{1,0:T(8,128)S(1)} %fusion.8), channel_id=1, source_target_pairs={{0,16},{4,20},{8,24},{12,28},{16,0},{20,4},{24,8},{28,12},{1,17},{... | collective-permute-start | bytes 294920 | tf_op jit(solution)/shard_map/ppermute | solution.py:26
  83.4 7.8 %collective-permute-start.23 = (f32[128,384]{1,0:T(8,128)S(1)}, f32[128,384]{1,0:T(8,128)S(1)}, u32[]{:S(2)}, u32[]{:S(2)}) collective-permute-start(f32[128,384]{1,0:T(8,128)S(1)} %multiply_add_fusion), channel_id=1, source_target_pairs={{0,8},{4,12},{8,16},{12,20},{16,24},{20,28},{1,9},{5,13},{9,17},{1... | collective-permute-start | bytes 589832 | tf_op jit(solution)/shard_map/ppermute | solution.py:22
  86.5 4.7 %collective-permute-start.29 = (f32[192,128]{1,0:T(8,128)S(1)}, f32[192,128]{1,0:T(8,128)S(1)}, u32[]{:S(2)}, u32[]{:S(2)}) collective-permute-start(f32[192,128]{1,0:T(8,128)S(1)} %add.144), channel_id=1, source_target_pairs={{0,8},{4,12},{8,0},{12,4},{16,24},{20,28},{24,16},{28,20},{1,9},{5... | collective-permute-start | bytes 294920 | tf_op jit(solution)/shard_map/ppermute | solution.py:26
  91.3 4.3 %collective-permute-start.30 = (f32[2,64,128]{2,1,0:T(8,128)S(1)}, f32[2,64,128]{2,1,0:T(8,128)S(1)}, u32[]{:S(2)}, u32[]{:S(2)}) collective-permute-start(f32[2,64,128]{2,1,0:T(8,128)S(1)} %bitcast_add_fusion.1), channel_id=1, source_target_pairs={{0,4},{1,5},{2,6},{3,7},{4,0},{5,1},{6,2},{7,3},{8,12},{9,13},{10,... | collective-permute-start | bytes 196616 | tf_op jit(solution)/shard_map/ppermute | solution.py:37
  92.4 3.9 %collective-permute-start.24 = (f32[128,128]{1,0:T(8,128)S(1)}, f32[128,128]{1,0:T(8,128)S(1)}, u32[]{:S(2)}, u32[]{:S(2)}) collective-permute-start(f32[128,128]{1,0:T(8,128)S(1)} %slice.149), channel_id=1, source_target_pairs={{0,1},{1,2},{2,3},{4,5},{5,6},{6,7},{8,9},{9,10},{10,11},{12,13},{... | collective-permute-start | bytes 196616 | tf_op jit(solution)/shard_map/ppermute | solution.py:22
  (3 other events, 2.7 us)

commit v5 on v3

--- a/solution.py
+++ b/solution.py
@@ -363,13 +363,17 @@
         )(entries, me, first, third, probes, inner, outer, a, b)
         return first, third, passed, entries
 
-    def last_update(tile, probes, terms, entries):
-        arrived = swapped(terms[1][:data_rows], "scan", 1)
-        third = terms[2][:data_rows] + arrived * even
-        first = terms[0][:data_rows] + arrived * odd + shifted(third, "scan", 2)
-        return first
-
-    def last_part(tile, probes, first, entries):
+    def with_margin(term, margin):
+        return jnp.concatenate([term[:, :length] + margin, term[:, length:band_cols]], axis=1)
+
+    def last_update(terms):
+        terms = [term[:data_rows] for term in terms]
+        margin = shifted(jnp.concatenate([term[:, band_cols:] for term in terms]), "mode", 1)
+        terms = [with_margin(term, margin[i * data_rows : (i + 1) * data_rows]) for i, term in enumerate(terms)]
+        arrived = swapped(terms[1], "scan", 1)
+        return terms[0] + arrived * odd, terms[2] + arrived * even
+
+    def last_part(tile, probes, terms, entries):
         weight = call(
             functools.partial(last_kernel, (scans, modes)),
             sds(tile_rows, band_cols),
@@ -378,8 +382,6 @@
             flops=2**20,
             moved=2**20,
         )(entries, me, probes)
-        margin = shifted(first[:, band_cols:], "mode", 1)
-        terms = jnp.concatenate([first[:, :length] + margin, first[:, length:band_cols]], axis=1)
         return tile[:, :, :band_cols] + terms.reshape(2, tile_rows, band_cols) / weight
 
     probes = as_halves(probe)
@@ -425,10 +427,9 @@
             pass
         if not last:
             first, third, passed, entries = inner_update(first, third, probes, *joined)
-            own = after(own, passed)
         else:
-            inner = last_update(first, probes, terms[:3], entries)
-            own = after(own, inner)
+            inner, outer = last_update(terms)
+            inner = inner + shifted(outer, "scan", 2)
         probe = probes[0, 0] + own[: 2 * half].reshape(2, half, length) / (own[2 * half :] + 1.0)
         if not last:
             second = swapped(passed, "scan", 1)

time: 99.5 us -> 97.7 us (0.982); the launches traced: 98.1 us -> 97.4 us
  starting transfers between devices: 43.4 us -> 41.9 us
  waiting for transfers between devices: 33.7 us -> 34.8 us
    ppermute x12, waiting for transfers between devices: 16.8 us -> 18.6 us  [swapped(): lax.ppermute(value, axis, [(i, i ^ bit) for i in range(lax.axis_size(axis...]
    ppermute x12, starting transfers between devices: 19 us -> 17.7 us  [swapped(): lax.ppermute(value, axis, [(i, i ^ bit) for i in range(lax.axis_size(axis...]
    ppermute x10, waiting for transfers between devices: 12.7 us -> 11.4 us  [across(): lax.ppermute(value, ('scan', 'mode'), [(i, i ^ other) for i in range(scan...]
  transfers between devices with their start and end apart: 31 -> 31, of which waited for: 18 -> 18; matrix products, arithmetic and copies ran while one was open for 3% -> 3% of each run, Pallas kernels for 6% -> 5%
where the time goes in v5:
time: 97.7 us; the launch traced here: 97.4 us
  starting transfers between devices  41.9 us (43%)
  waiting for transfers between devices  34.8 us (36%)
  Pallas kernels  13.5 us (14%)
  local copies, waits for them, and re-layouts  3.72 us (4%)
  between operations  1.81 us (2%)
  other arithmetic  1.68 us (2%)
    ppermute x12, waiting for transfers between devices, swapped(): lax.ppermute(value, axis, [(i, i ^ bit) for i in range(lax.axis_size(axis...  18.6 us
    ppermute x12, starting transfers between devices, swapped(): lax.ppermute(value, axis, [(i, i ^ bit) for i in range(lax.axis_size(axis...  17.7 us
    ppermute x10, starting transfers between devices, across(): lax.ppermute(value, ('scan', 'mode'), [(i, i ^ other) for i in range(scan...  13.2 us
    ppermute x10, waiting for transfers between devices, across(): lax.ppermute(value, ('scan', 'mode'), [(i, i ^ other) for i in range(scan...  11.4 us
    pallas_call x2, Pallas kernels, local(): call(wave_kernel, (*[sds(modes // 2, 2, 3 * half, length)] * 2, *[sds(row...  8.17 us
    ppermute x5, starting transfers between devices, shifted(): lax.ppermute(value, axis, [(source, source + steps) for source in range(i...  7.55 us
    ppermute x5, waiting for transfers between devices, shifted(): lax.ppermute(value, axis, [(source, source + steps) for source in range(i...  4.86 us
    ppermute x4, starting transfers between devices, paired(): lax.ppermute(value, axis, [(i, i + step) for i in lower] + [(i + step, i)...  3.34 us
  transfers between devices with their start and end apart: 31, of which 18 were waited for; matrix products, arithmetic and copies ran while one was open for 3% of the time, Pallas kernels for 5%

profile of v5, /device:TPU:0, one launch (start us, length us, event | category | flops | bytes accessed | tf_op | source)
XLA Modules:
  0.0 97.4 jit_solution(10216847707231145806)
XLA Ops:
  0.6 1.3 %collective-permute-start = (f32[2,64,256]{2,1,0:T(8,128)}, f32[2,64,256]{2,1,0:T(8,128)S(1)}, u32[]{:S(2)}, u32[]{:S(2)}) collective-permute-start(f32[2,64,256]{2,1,0:T(8,128)} %param.6), channel_id=1, source_target_pairs={{4,0},{8,4},{12,8},{16,12},{20,16},{24,20},{28,24},{5,1},{9,5},{13... | collective-permute-start | bytes 393224 | tf_op jit(solution)/shard_map/ppermute | solution.py:22
  1.9 1.3 %collective-permute-start.1 = (f32[2,64,256]{2,1,0:T(8,128)}, f32[2,64,256]{2,1,0:T(8,128)S(1)}, u32[]{:S(2)}, u32[]{:S(2)}) collective-permute-start(f32[2,64,256]{2,1,0:T(8,128)} %param.6), channel_id=1, source_target_pairs={{8,0},{12,4},{16,8},{20,12},{24,16},{28,20},{9,1},{13,5},{17,9},{2... | collective-permute-start | bytes 393224 | tf_op jit(solution)/shard_map/ppermute | solution.py:22
  4.2 3.0 %collective-permute-start.3 = (f32[1,2,2,64,128]{4,3,2,1,0:T(8,128)S(1)}, f32[1,2,2,64,128]{4,3,2,1,0:T(8,128)S(1)}, u32[]{:S(2)}, u32[]{:S(2)}) collective-permute-start(f32[1,2,2,64,128]{4,3,2,1,0:T(8,128)S(1)} %reverse_select_fusion.1), channel_id=1, source_target_pairs={{0,2},{1,3},{2,0},{3,1},{4,6},{5,7},{6,4},{7,5},{8,10},{9,11},{10,... | collective-permute-start | bytes 393224 | tf_op jit(solution)/shard_map/ppermute | solution.py:26
  9.1 1.6 %collective-permute-done.3 = f32[1,2,2,64,128]{4,3,2,1,0:T(8,128)S(1)} collective-permute-done((f32[1,2,2,64,128]{4,3,2,1,0:T(8,128)S(1)}, f32[1,2,2,64,128]{4,3,2,1,0:T(8,128)S(1)}, u32[]{:S(2)}, u32[]{:S(2)}) %collective-permute-start.3) | collective-permute-done | bytes 131104 | tf_op jit(solution)/shard_map/ppermute | solution.py:26
  10.8 2.4 %collective-permute-done.1 = f32[2,64,256]{2,1,0:T(8,128)S(1)} collective-permute-done((f32[2,64,256]{2,1,0:T(8,128)}, f32[2,64,256]{2,1,0:T(8,128)S(1)}, u32[]{:S(2)}, u32[]{:S(2)}) %collective-permute-start.1) | collective-permute-done | bytes 131104 | tf_op jit(solution)/shard_map/ppermute | solution.py:22
  13.2 1.3 %collective-permute-start.2 = (f32[2,192,128]{2,1,0:T(8,128)S(1)}, f32[2,192,128]{2,1,0:T(8,128)S(1)}, u32[]{:S(2)}, u32[]{:S(2)}) collective-permute-start(f32[2,192,128]{2,1,0:T(8,128)S(1)} %slice.165), channel_id=1, source_target_pairs={{1,0},{2,1},{3,2},{5,4},{6,5},{7,6},{9,8},{10,9},{11,10},{13,12},{... | collective-permute-start | bytes 589832 | tf_op jit(solution)/shard_map/ppermute | solution.py:22
  14.7 1.9 %collective-permute-done.2 = f32[2,192,128]{2,1,0:T(8,128)S(1)} collective-permute-done((f32[2,192,128]{2,1,0:T(8,128)S(1)}, f32[2,192,128]{2,1,0:T(8,128)S(1)}, u32[]{:S(2)}, u32[]{:S(2)}) %collective-permute-start.2) | collective-permute-done | bytes 196640 | tf_op jit(solution)/shard_map/ppermute | solution.py:22
  18.4 4.1 %shard_map.78 = (f32[2,2,192,128]{3,2,1,0:T(8,128)S(1)}, f32[2,2,192,128]{3,2,1,0:T(8,128)S(1)}, f32[136,384]{1,0:T(8,128)S(1)}, f32[136,384]{1,0:T(8,128)S(1)}, f32[136,384]{1,0:T(8,128)S(1)}) custom-call(s32[6]{0:T(128)S(1)} %reshape.96.place, s32[2]{0:T(128)S(1)} %pad_add_fusion.2.me, f32[2,2,128,128]{3,2,1,0:T(8,128)S(1)} %get-tuple-element.29.patch, ...), custom_call_target="tpu_custom_call" | custom-call | flops 1610612736 | bytes 4194304 | tf_op jit(solution)/shard_map/pallas_call | solution.py:406
  22.6 3.9 %collective-permute-start.11 = (f32[2,2,192,128]{3,2,1,0:T(8,128)S(1)}, f32[2,2,192,128]{3,2,1,0:T(8,128)S(1)}, u32[]{:S(2)}, u32[]{:S(2)}) collective-permute-start(f32[2,2,192,128]{3,2,1,0:T(8,128)S(1)} %get-tuple-element.45), channel_id=1, source_target_pairs={{0,1},{1,0},{2,3},{3,2},{4,5},{5,4},{6,7},{7,6},{8,9},{9,8},{10,11... | collective-permute-start | bytes 1179656 | tf_op jit(solution)/shard_map/ppermute | solution.py:26
  26.5 1.9 %collective-permute-done.5 = f32[136,384]{1,0:T(8,128)S(1)} collective-permute-done((f32[136,384]{1,0:T(8,128)S(1)}, f32[136,384]{1,0:T(8,128)S(1)}, u32[]{:S(2)}, u32[]{:S(2)}) %collective-permute-start.5) | collective-permute-done | bytes 208928 | tf_op jit(solution)/shard_map/ppermute | solution.py:26
  28.5 1.9 %collective-permute-start.6 = (f32[136,384]{1,0:T(8,128)S(1)}, f32[136,384]{1,0:T(8,128)S(1)}, u32[]{:S(2)}, u32[]{:S(2)}) collective-permute-start(f32[136,384]{1,0:T(8,128)S(1)} %get-tuple-element.79), channel_id=1, source_target_pairs={{0,8},{4,12},{16,24},{20,28},{8,0},{12,4},{24,16},{28,20},{1,9},{5... | collective-permute-start | bytes 626696 | tf_op jit(solution)/shard_map/ppermute | solution.py:31
  31.9 3.9 %collective-permute-start.13 = (f32[192,128]{1,0:T(8,128)S(1)}, f32[192,128]{1,0:T(8,128)S(1)}, u32[]{:S(2)}, u32[]{:S(2)}) collective-permute-start(f32[192,128]{1,0:T(8,128)S(1)} %get-tuple-element.67), channel_id=1, source_target_pairs={{0,2},{1,3},{2,0},{3,1},{4,6},{5,7},{6,4},{7,5},{8,10},{9,11},{10,... | collective-permute-start | bytes 294920 | tf_op jit(solution)/shard_map/ppermute | solution.py:37
  38.1 1.3 %collective-permute-done.13 = f32[192,128]{1,0:T(8,128)S(1)} collective-permute-done((f32[192,128]{1,0:T(8,128)S(1)}, f32[192,128]{1,0:T(8,128)S(1)}, u32[]{:S(2)}, u32[]{:S(2)}) %collective-permute-start.13) | collective-permute-done | bytes 98336 | tf_op jit(solution)/shard_map/ppermute | solution.py:37
  39.3 2.7 %collective-permute-done.14 = f32[192,128]{1,0:T(8,128)S(1)} collective-permute-done((f32[192,128]{1,0:T(8,128)S(1)}, f32[192,128]{1,0:T(8,128)S(1)}, u32[]{:S(2)}, u32[]{:S(2)}) %collective-permute-start.14) | collective-permute-done | bytes 98336 | tf_op jit(solution)/shard_map/ppermute | solution.py:37
  42.0 4.6 %collective-permute-start.15 = (f32[192,128]{1,0:T(8,128)S(1)}, f32[192,128]{1,0:T(8,128)S(1)}, u32[]{:S(2)}, u32[]{:S(2)}) collective-permute-start(f32[192,128]{1,0:T(8,128)S(1)} %fusion.7), channel_id=1, source_target_pairs={{0,8},{4,12},{8,0},{12,4},{16,24},{20,28},{24,16},{28,20},{1,9},{5... | collective-permute-start | bytes 294920 | tf_op jit(solution)/shard_map/ppermute | solution.py:26
  46.6 2.8 %collective-permute-done.15 = f32[192,128]{1,0:T(8,128)S(1)} collective-permute-done((f32[192,128]{1,0:T(8,128)S(1)}, f32[192,128]{1,0:T(8,128)S(1)}, u32[]{:S(2)}, u32[]{:S(2)}) %collective-permute-start.15) | collective-permute-done | bytes 98336 | tf_op jit(solution)/shard_map/ppermute | solution.py:26
  49.4 2.1 %collective-permute-start.16 = (f32[192,128]{1,0:T(8,128)S(1)}, f32[192,128]{1,0:T(8,128)S(1)}, u32[]{:S(2)}, u32[]{:S(2)}) collective-permute-start(f32[192,128]{1,0:T(8,128)S(1)} %add.136), channel_id=1, source_target_pairs={{0,16},{4,20},{8,24},{12,28},{16,0},{20,4},{24,8},{28,12},{1,17},{... | collective-permute-start | bytes 294920 | tf_op jit(solution)/shard_map/ppermute | solution.py:26
  51.6 2.0 %shard_map.80 = (f32[2,64,384]{2,1,0:T(8,128)S(1)}, f32[2,64,384]{2,1,0:T(8,128)S(1)}, f32[2,64,384]{2,1,0:T(8,128)S(1)}) custom-call(s32[1024]{0:T(1024)S(1)} %fusion.11.table, s32[2]{0:T(128)S(1)} %pad_add_fusion.2.me, f32[2,64,384]{2,1,0:T(8,128)S(1)} %get-tuple-element.61.first, f32[2,64,384]{2,1,0:T(8,128)S(1)} %get-tuple-element.59.third, ...), custom_call_target="tpu_custom_call" | custom-call | flops 1048576 | bytes 1048576 | tf_op jit(solution)/shard_map/pallas_call | solution.py:356
  53.6 1.0 %collective-permute-start.10 = (f32[2,64,384]{2,1,0:T(8,128)S(1)}, f32[2,64,384]{2,1,0:T(8,128)S(1)}, u32[]{:S(2)}, u32[]{:S(2)}) collective-permute-start(f32[2,64,384]{2,1,0:T(8,128)S(1)} %get-tuple-element.40), channel_id=1, source_target_pairs={{0,4},{4,0},{8,12},{12,8},{16,20},{20,16},{24,28},{28,24},{1,5},{5... | collective-permute-start | bytes 589832 | tf_op jit(solution)/shard_map/ppermute | solution.py:26
  54.7 2.3 %collective-permute-done.16 = f32[192,128]{1,0:T(8,128)S(1)} collective-permute-done((f32[192,128]{1,0:T(8,128)S(1)}, f32[192,128]{1,0:T(8,128)S(1)}, u32[]{:S(2)}, u32[]{:S(2)}) %collective-permute-start.16) | collective-permute-done | bytes 98336 | tf_op jit(solution)/shard_map/ppermute | solution.py:26
  57.8 2.8 %collective-permute-start.19 = (f32[2,64,128]{2,1,0:T(8,128)S(1)}, f32[2,64,128]{2,1,0:T(8,128)S(1)}, u32[]{:S(2)}, u32[]{:S(2)}) collective-permute-start(f32[2,64,128]{2,1,0:T(8,128)S(1)} %bitcast_add_fusion.3), channel_id=1, source_target_pairs={{0,6},{1,7},{2,4},{3,5},{4,2},{5,3},{6,0},{7,1},{8,14},{9,15},{10,... | collective-permute-start | bytes 196616 | tf_op jit(solution)/shard_map/ppermute | solution.py:37
  60.6 2.2 %collective-permute-done.17 = f32[2,64,128]{2,1,0:T(8,128)S(1)} collective-permute-done((f32[2,64,128]{2,1,0:T(8,128)S(1)}, f32[2,64,128]{2,1,0:T(8,128)S(1)}, u32[]{:S(2)}, u32[]{:S(2)}) %collective-permute-start.17) | collective-permute-done | bytes 65568 | tf_op jit(solution)/shard_map/ppermute | solution.py:37
  65.2 4.1 %shard_map.82 = (f32[2,2,192,128]{3,2,1,0:T(8,128)S(1)}, f32[2,2,192,128]{3,2,1,0:T(8,128)S(1)}, f32[136,384]{1,0:T(8,128)S(1)}, f32[136,384]{1,0:T(8,128)S(1)}, f32[136,384]{1,0:T(8,128)S(1)}) custom-call(s32[6]{0:T(128)S(1)} %reshape.96.place, s32[2]{0:T(128)S(1)} %pad_add_fusion.2.me, f32[2,2,128,128]{3,2,1,0:T(8,128)S(1)} %get-tuple-element.42.patch, ...), custom_call_target="tpu_custom_call" | custom-call | flops 1610612736 | bytes 4194304 | tf_op jit(solution)/shard_map/pallas_call | solution.py:406
  69.5 1.6 %collective-permute-done.21 = f32[2,2,192,128]{3,2,1,0:T(8,128)S(1)} collective-permute-done((f32[2,2,192,128]{3,2,1,0:T(8,128)S(1)}, f32[2,2,192,128]{3,2,1,0:T(8,128)S(1)}, u32[]{:S(2)}, u32[]{:S(2)}) %collective-permute-start.21) | collective-permute-done | bytes 393248 | tf_op jit(solution)/shard_map/ppermute | solution.py:26
  72.2 1.8 %collective-permute-start.26 = (f32[192,128]{1,0:T(8,128)S(1)}, f32[192,128]{1,0:T(8,128)S(1)}, u32[]{:S(2)}, u32[]{:S(2)}) collective-permute-start(f32[192,128]{1,0:T(8,128)S(1)} %get-tuple-element.64), channel_id=1, source_target_pairs={{0,2},{1,3},{2,0},{3,1},{4,6},{5,7},{6,4},{7,5},{8,10},{9,11},{10,... | collective-permute-start | bytes 294920 | tf_op jit(solution)/shard_map/ppermute | solution.py:37
  74.8 1.3 %collective-permute-start.22 = (f32[384,128]{1,0:T(8,128)S(1)}, f32[384,128]{1,0:T(8,128)S(1)}, u32[]{:S(2)}, u32[]{:S(2)}) collective-permute-start(f32[384,128]{1,0:T(8,128)S(1)} %pad_maximum_fusion.5), channel_id=1, source_target_pairs={{0,1},{1,2},{2,3},{4,5},{5,6},{6,7},{8,9},{9,10},{10,11},{12,13},{... | collective-permute-start | bytes 589832 | tf_op jit(solution)/shard_map/ppermute | solution.py:22
  76.1 1.3 %collective-permute-done.26 = f32[192,128]{1,0:T(8,128)S(1)} collective-permute-done((f32[192,128]{1,0:T(8,128)S(1)}, f32[192,128]{1,0:T(8,128)S(1)}, u32[]{:S(2)}, u32[]{:S(2)}) %collective-permute-start.26) | collective-permute-done | bytes 98336 | tf_op jit(solution)/shard_map/ppermute | solution.py:37
  77.4 2.1 %collective-permute-done.27 = f32[192,128]{1,0:T(8,128)S(1)} collective-permute-done((f32[192,128]{1,0:T(8,128)S(1)}, f32[192,128]{1,0:T(8,128)S(1)}, u32[]{:S(2)}, u32[]{:S(2)}) %collective-permute-start.27) | collective-permute-done | bytes 98336 | tf_op jit(solution)/shard_map/ppermute | solution.py:37
  81.3 3.0 %collective-permute-done.28 = f32[192,128]{1,0:T(8,128)S(1)} collective-permute-done((f32[192,128]{1,0:T(8,128)S(1)}, f32[192,128]{1,0:T(8,128)S(1)}, u32[]{:S(2)}, u32[]{:S(2)}) %collective-permute-start.28) | collective-permute-done | bytes 98336 | tf_op jit(solution)/shard_map/ppermute | solution.py:26
  86.3 4.6 %collective-permute-done.29 = f32[192,128]{1,0:T(8,128)S(1)} collective-permute-done((f32[192,128]{1,0:T(8,128)S(1)}, f32[192,128]{1,0:T(8,128)S(1)}, u32[]{:S(2)}, u32[]{:S(2)}) %collective-permute-start.29) | collective-permute-done | bytes 98336 | tf_op jit(solution)/shard_map/ppermute | solution.py:26
  91.8 2.4 %collective-permute-start.24 = (f32[128,256]{1,0:T(8,128)S(1)}, f32[128,256]{1,0:T(8,128)S(1)}, u32[]{:S(2)}, u32[]{:S(2)}) collective-permute-start(f32[128,256]{1,0:T(8,128)S(1)} %maximum_add_fusion.1), channel_id=1, source_target_pairs={{0,8},{4,12},{8,16},{12,20},{16,24},{20,28},{1,9},{5,13},{9,17},{1... | collective-permute-start | bytes 393224 | tf_op jit(solution)/shard_map/ppermute | solution.py:22
  94.2 1.2 %collective-permute-done.30 = f32[2,64,128]{2,1,0:T(8,128)S(1)} collective-permute-done((f32[2,64,128]{2,1,0:T(8,128)S(1)}, f32[2,64,128]{2,1,0:T(8,128)S(1)}, u32[]{:S(2)}, u32[]{:S(2)}) %collective-permute-start.30) | collective-permute-done | bytes 65568 | tf_op jit(solution)/shard_map/ppermute | solution.py:37
  (110 shorter events, 20.0 us)
Async XLA Ops:
  0.6 10.2 %collective-permute-start = (f32[2,64,256]{2,1,0:T(8,128)}, f32[2,64,256]{2,1,0:T(8,128)S(1)}, u32[]{:S(2)}, u32[]{:S(2)}) collective-permute-start(f32[2,64,256]{2,1,0:T(8,128)} %param.6), channel_id=1, source_target_pairs={{4,0},{8,4},{12,8},{16,12},{20,16},{24,20},{28,24},{5,1},{9,5},{13... | collective-permute-start | bytes 393224 | tf_op jit(solution)/shard_map/ppermute | solution.py:22
  1.9 11.3 %collective-permute-start.1 = (f32[2,64,256]{2,1,0:T(8,128)}, f32[2,64,256]{2,1,0:T(8,128)S(1)}, u32[]{:S(2)}, u32[]{:S(2)}) collective-permute-start(f32[2,64,256]{2,1,0:T(8,128)} %param.6), channel_id=1, source_target_pairs={{8,0},{12,4},{16,8},{20,12},{24,16},{28,20},{9,1},{13,5},{17,9},{2... | collective-permute-start | bytes 393224 | tf_op jit(solution)/shard_map/ppermute | solution.py:22
  4.2 4.9 %copy-start.2 = (f32[2,64,256]{2,1,0:T(8,128)S(1)}, f32[2,64,256]{2,1,0:T(8,128)}, u32[]{:S(2)}) copy-start(f32[2,64,256]{2,1,0:T(8,128)} %param.6) | copy-start | bytes 393220
  4.2 6.5 %collective-permute-start.3 = (f32[1,2,2,64,128]{4,3,2,1,0:T(8,128)S(1)}, f32[1,2,2,64,128]{4,3,2,1,0:T(8,128)S(1)}, u32[]{:S(2)}, u32[]{:S(2)}) collective-permute-start(f32[1,2,2,64,128]{4,3,2,1,0:T(8,128)S(1)} %reverse_select_fusion.1), channel_id=1, source_target_pairs={{0,2},{1,3},{2,0},{3,1},{4,6},{5,7},{6,4},{7,5},{8,10},{9,11},{10,... | collective-permute-start | bytes 393224 | tf_op jit(solution)/shard_map/ppermute | solution.py:26
  10.7 6.7 %collective-permute-start.4 = (f32[2,2,2,64,128]{4,3,2,1,0:T(8,128)S(1)}, f32[2,2,2,64,128]{4,3,2,1,0:T(8,128)S(1)}, u32[]{:S(2)}, u32[]{:S(2)}) collective-permute-start(f32[2,2,2,64,128]{4,3,2,1,0:T(8,128)S(1)} %pad_maximum_fusion.3), channel_id=1, source_target_pairs={{0,1},{1,0},{2,3},{3,2},{4,5},{5,4},{6,7},{7,6},{8,9},{9,8},{10,11... | collective-permute-start | bytes 786440 | tf_op jit(solution)/shard_map/ppermute | solution.py:26
  13.2 3.3 %collective-permute-start.2 = (f32[2,192,128]{2,1,0:T(8,128)S(1)}, f32[2,192,128]{2,1,0:T(8,128)S(1)}, u32[]{:S(2)}, u32[]{:S(2)}) collective-permute-start(f32[2,192,128]{2,1,0:T(8,128)S(1)} %slice.165), channel_id=1, source_target_pairs={{1,0},{2,1},{3,2},{5,4},{6,5},{7,6},{9,8},{10,9},{11,10},{13,12},{... | collective-permute-start | bytes 589832 | tf_op jit(solution)/shard_map/ppermute | solution.py:22
  22.5 5.9 %collective-permute-start.5 = (f32[136,384]{1,0:T(8,128)S(1)}, f32[136,384]{1,0:T(8,128)S(1)}, u32[]{:S(2)}, u32[]{:S(2)}) collective-permute-start(f32[136,384]{1,0:T(8,128)S(1)} %get-tuple-element.33), channel_id=1, source_target_pairs={{0,4},{4,0},{8,12},{12,8},{16,20},{20,16},{24,28},{28,24},{1,5},{5... | collective-permute-start | bytes 626696 | tf_op jit(solution)/shard_map/ppermute | solution.py:26
  22.6 8.5 %collective-permute-start.11 = (f32[2,2,192,128]{3,2,1,0:T(8,128)S(1)}, f32[2,2,192,128]{3,2,1,0:T(8,128)S(1)}, u32[]{:S(2)}, u32[]{:S(2)}) collective-permute-start(f32[2,2,192,128]{3,2,1,0:T(8,128)S(1)} %get-tuple-element.45), channel_id=1, source_target_pairs={{0,1},{1,0},{2,3},{3,2},{4,5},{5,4},{6,7},{7,6},{8,9},{9,8},{10,11... | collective-permute-start | bytes 1179656 | tf_op jit(solution)/shard_map/ppermute | solution.py:26
  28.5 8.1 %collective-permute-start.6 = (f32[136,384]{1,0:T(8,128)S(1)}, f32[136,384]{1,0:T(8,128)S(1)}, u32[]{:S(2)}, u32[]{:S(2)}) collective-permute-start(f32[136,384]{1,0:T(8,128)S(1)} %get-tuple-element.79), channel_id=1, source_target_pairs={{0,8},{4,12},{16,24},{20,28},{8,0},{12,4},{24,16},{28,20},{1,9},{5... | collective-permute-start | bytes 626696 | tf_op jit(solution)/shard_map/ppermute | solution.py:31
  30.4 6.2 %collective-permute-start.7 = (f32[136,384]{1,0:T(8,128)S(1)}, f32[136,384]{1,0:T(8,128)S(1)}, u32[]{:S(2)}, u32[]{:S(2)}) collective-permute-start(f32[136,384]{1,0:T(8,128)S(1)} %get-tuple-element.78), channel_id=1, source_target_pairs={{8,16},{12,20},{16,8},{20,12},{9,17},{13,21},{17,9},{21,13},{10,18... | collective-permute-start | bytes 626696 | tf_op jit(solution)/shard_map/ppermute | solution.py:31
  31.2 6.8 %collective-permute-start.12 = (f32[192,128]{1,0:T(8,128)S(1)}, f32[192,128]{1,0:T(8,128)S(1)}, u32[]{:S(2)}, u32[]{:S(2)}) collective-permute-start(f32[192,128]{1,0:T(8,128)S(1)} %get-tuple-element.65), channel_id=1, source_target_pairs={{0,4},{1,5},{2,6},{3,7},{4,0},{5,1},{6,2},{7,3},{8,12},{9,13},{10,... | collective-permute-start | bytes 294920 | tf_op jit(solution)/shard_map/ppermute | solution.py:37
  31.9 7.4 %collective-permute-start.13 = (f32[192,128]{1,0:T(8,128)S(1)}, f32[192,128]{1,0:T(8,128)S(1)}, u32[]{:S(2)}, u32[]{:S(2)}) collective-permute-start(f32[192,128]{1,0:T(8,128)S(1)} %get-tuple-element.67), channel_id=1, source_target_pairs={{0,2},{1,3},{2,0},{3,1},{4,6},{5,7},{6,4},{7,5},{8,10},{9,11},{10,... | collective-permute-start | bytes 294920 | tf_op jit(solution)/shard_map/ppermute | solution.py:37
  35.8 6.2 %collective-permute-start.14 = (f32[192,128]{1,0:T(8,128)S(1)}, f32[192,128]{1,0:T(8,128)S(1)}, u32[]{:S(2)}, u32[]{:S(2)}) collective-permute-start(f32[192,128]{1,0:T(8,128)S(1)} %get-tuple-element.66), channel_id=1, source_target_pairs={{0,6},{1,7},{2,4},{3,5},{4,2},{5,3},{6,0},{7,1},{8,14},{9,15},{10,... | collective-permute-start | bytes 294920 | tf_op jit(solution)/shard_map/ppermute | solution.py:37
  37.3 14.3 %collective-permute-start.8 = (f32[264,128]{1,0:T(8,128)S(1)}, f32[264,128]{1,0:T(8,128)S(1)}, u32[]{:S(2)}, u32[]{:S(2)}) collective-permute-start(f32[264,128]{1,0:T(8,128)S(1)} %get-tuple-element.35), channel_id=1, source_target_pairs={{0,1},{2,3},{1,0},{3,2},{4,5},{6,7},{5,4},{7,6},{8,9},{10,11},{9,8... | collective-permute-start | bytes 405512 | tf_op jit(solution)/shard_map/ppermute | solution.py:31
  37.4 14.2 %collective-permute-start.9 = (f32[264,128]{1,0:T(8,128)S(1)}, f32[264,128]{1,0:T(8,128)S(1)}, u32[]{:S(2)}, u32[]{:S(2)}) collective-permute-start(f32[264,128]{1,0:T(8,128)S(1)} %get-tuple-element.36), channel_id=1, source_target_pairs={{1,2},{2,1},{5,6},{6,5},{9,10},{10,9},{13,14},{14,13},{17,18},{18,... | collective-permute-start | bytes 405512 | tf_op jit(solution)/shard_map/ppermute | solution.py:31
  42.0 7.4 %collective-permute-start.15 = (f32[192,128]{1,0:T(8,128)S(1)}, f32[192,128]{1,0:T(8,128)S(1)}, u32[]{:S(2)}, u32[]{:S(2)}) collective-permute-start(f32[192,128]{1,0:T(8,128)S(1)} %fusion.7), channel_id=1, source_target_pairs={{0,8},{4,12},{8,0},{12,4},{16,24},{20,28},{24,16},{28,20},{1,9},{5... | collective-permute-start | bytes 294920 | tf_op jit(solution)/shard_map/ppermute | solution.py:26
  49.4 7.5 %collective-permute-start.16 = (f32[192,128]{1,0:T(8,128)S(1)}, f32[192,128]{1,0:T(8,128)S(1)}, u32[]{:S(2)}, u32[]{:S(2)}) collective-permute-start(f32[192,128]{1,0:T(8,128)S(1)} %add.136), channel_id=1, source_target_pairs={{0,16},{4,20},{8,24},{12,28},{16,0},{20,4},{24,8},{28,12},{1,17},{... | collective-permute-start | bytes 294920 | tf_op jit(solution)/shard_map/ppermute | solution.py:26
  53.6 10.0 %collective-permute-start.10 = (f32[2,64,384]{2,1,0:T(8,128)S(1)}, f32[2,64,384]{2,1,0:T(8,128)S(1)}, u32[]{:S(2)}, u32[]{:S(2)}) collective-permute-start(f32[2,64,384]{2,1,0:T(8,128)S(1)} %get-tuple-element.40), channel_id=1, source_target_pairs={{0,4},{4,0},{8,12},{12,8},{16,20},{20,16},{24,28},{28,24},{1,5},{5... | collective-permute-start | bytes 589832 | tf_op jit(solution)/shard_map/ppermute | solution.py:26
  57.1 5.7 %collective-permute-start.17 = (f32[2,64,128]{2,1,0:T(8,128)S(1)}, f32[2,64,128]{2,1,0:T(8,128)S(1)}, u32[]{:S(2)}, u32[]{:S(2)}) collective-permute-start(f32[2,64,128]{2,1,0:T(8,128)S(1)} %bitcast_add_fusion.3), channel_id=1, source_target_pairs={{0,4},{1,5},{2,6},{3,7},{4,0},{5,1},{6,2},{7,3},{8,12},{9,13},{10,... | collective-permute-start | bytes 196616 | tf_op jit(solution)/shard_map/ppermute | solution.py:37
  57.8 5.0 %collective-permute-start.18 = (f32[2,64,128]{2,1,0:T(8,128)S(1)}, f32[2,64,128]{2,1,0:T(8,128)S(1)}, u32[]{:S(2)}, u32[]{:S(2)}) collective-permute-start(f32[2,64,128]{2,1,0:T(8,128)S(1)} %bitcast_add_fusion.3), channel_id=1, source_target_pairs={{0,2},{1,3},{2,0},{3,1},{4,6},{5,7},{6,4},{7,5},{8,10},{9,11},{10,... | collective-permute-start | bytes 196616 | tf_op jit(solution)/shard_map/ppermute | solution.py:37
  57.8 5.7 %collective-permute-start.19 = (f32[2,64,128]{2,1,0:T(8,128)S(1)}, f32[2,64,128]{2,1,0:T(8,128)S(1)}, u32[]{:S(2)}, u32[]{:S(2)}) collective-permute-start(f32[2,64,128]{2,1,0:T(8,128)S(1)} %bitcast_add_fusion.3), channel_id=1, source_target_pairs={{0,6},{1,7},{2,4},{3,5},{4,2},{5,3},{6,0},{7,1},{8,14},{9,15},{10,... | collective-permute-start | bytes 196616 | tf_op jit(solution)/shard_map/ppermute | solution.py:37
  63.6 1.6 %collective-permute-start.20 = (f32[2,2,2,64,128]{4,3,2,1,0:T(8,128)S(1)}, f32[2,2,2,64,128]{4,3,2,1,0:T(8,128)S(1)}, u32[]{:S(2)}, u32[]{:S(2)}) collective-permute-start(f32[2,2,2,64,128]{4,3,2,1,0:T(8,128)S(1)} %pad_maximum_fusion.4), channel_id=1, source_target_pairs={{0,1},{1,0},{2,3},{3,2},{4,5},{5,4},{6,7},{7,6},{8,9},{9,8},{10,11... | collective-permute-start | bytes 786440 | tf_op jit(solution)/shard_map/ppermute | solution.py:26
  69.3 1.8 %collective-permute-start.21 = (f32[2,2,192,128]{3,2,1,0:T(8,128)S(1)}, f32[2,2,192,128]{3,2,1,0:T(8,128)S(1)}, u32[]{:S(2)}, u32[]{:S(2)}) collective-permute-start(f32[2,2,192,128]{3,2,1,0:T(8,128)S(1)} %get-tuple-element.48), channel_id=1, source_target_pairs={{0,1},{1,0},{2,3},{3,2},{4,5},{5,4},{6,7},{7,6},{8,9},{9,8},{10,11... | collective-permute-start | bytes 1179656 | tf_op jit(solution)/shard_map/ppermute | solution.py:26
  71.2 4.9 %collective-permute-start.25 = (f32[192,128]{1,0:T(8,128)S(1)}, f32[192,128]{1,0:T(8,128)S(1)}, u32[]{:S(2)}, u32[]{:S(2)}) collective-permute-start(f32[192,128]{1,0:T(8,128)S(1)} %get-tuple-element.62), channel_id=1, source_target_pairs={{0,4},{1,5},{2,6},{3,7},{4,0},{5,1},{6,2},{7,3},{8,12},{9,13},{10,... | collective-permute-start | bytes 294920 | tf_op jit(solution)/shard_map/ppermute | solution.py:37
  72.2 5.2 %collective-permute-start.26 = (f32[192,128]{1,0:T(8,128)S(1)}, f32[192,128]{1,0:T(8,128)S(1)}, u32[]{:S(2)}, u32[]{:S(2)}) collective-permute-start(f32[192,128]{1,0:T(8,128)S(1)} %get-tuple-element.64), channel_id=1, source_target_pairs={{0,2},{1,3},{2,0},{3,1},{4,6},{5,7},{6,4},{7,5},{8,10},{9,11},{10,... | collective-permute-start | bytes 294920 | tf_op jit(solution)/shard_map/ppermute | solution.py:37
  74.0 5.5 %collective-permute-start.27 = (f32[192,128]{1,0:T(8,128)S(1)}, f32[192,128]{1,0:T(8,128)S(1)}, u32[]{:S(2)}, u32[]{:S(2)}) collective-permute-start(f32[192,128]{1,0:T(8,128)S(1)} %get-tuple-element.63), channel_id=1, source_target_pairs={{0,6},{1,7},{2,4},{3,5},{4,2},{5,3},{6,0},{7,1},{8,14},{9,15},{10,... | collective-permute-start | bytes 294920 | tf_op jit(solution)/shard_map/ppermute | solution.py:37
  74.8 10.4 %collective-permute-start.22 = (f32[384,128]{1,0:T(8,128)S(1)}, f32[384,128]{1,0:T(8,128)S(1)}, u32[]{:S(2)}, u32[]{:S(2)}) collective-permute-start(f32[384,128]{1,0:T(8,128)S(1)} %pad_maximum_fusion.5), channel_id=1, source_target_pairs={{0,1},{1,2},{2,3},{4,5},{5,6},{6,7},{8,9},{9,10},{10,11},{12,13},{... | collective-permute-start | bytes 589832 | tf_op jit(solution)/shard_map/ppermute | solution.py:22
  79.6 4.7 %collective-permute-start.28 = (f32[192,128]{1,0:T(8,128)S(1)}, f32[192,128]{1,0:T(8,128)S(1)}, u32[]{:S(2)}, u32[]{:S(2)}) collective-permute-start(f32[192,128]{1,0:T(8,128)S(1)} %fusion.9), channel_id=1, source_target_pairs={{0,8},{4,12},{8,0},{12,4},{16,24},{20,28},{24,16},{28,20},{1,9},{5... | collective-permute-start | bytes 294920 | tf_op jit(solution)/shard_map/ppermute | solution.py:26
  84.3 6.6 %collective-permute-start.29 = (f32[192,128]{1,0:T(8,128)S(1)}, f32[192,128]{1,0:T(8,128)S(1)}, u32[]{:S(2)}, u32[]{:S(2)}) collective-permute-start(f32[192,128]{1,0:T(8,128)S(1)} %add.152), channel_id=1, source_target_pairs={{0,16},{4,20},{8,24},{12,28},{16,0},{20,4},{24,8},{28,12},{1,17},{... | collective-permute-start | bytes 294920 | tf_op jit(solution)/shard_map/ppermute | solution.py:26
  85.3 6.5 %collective-permute-start.23 = (f32[128,256]{1,0:T(8,128)S(1)}, f32[128,256]{1,0:T(8,128)S(1)}, u32[]{:S(2)}, u32[]{:S(2)}) collective-permute-start(f32[128,256]{1,0:T(8,128)S(1)} %pad_maximum_fusion.6), channel_id=1, source_target_pairs={{0,4},{4,0},{8,12},{12,8},{16,20},{20,16},{24,28},{28,24},{1,5},{5... | collective-permute-start | bytes 393224 | tf_op jit(solution)/shard_map/ppermute | solution.py:26
  91.0 4.3 %collective-permute-start.30 = (f32[2,64,128]{2,1,0:T(8,128)S(1)}, f32[2,64,128]{2,1,0:T(8,128)S(1)}, u32[]{:S(2)}, u32[]{:S(2)}) collective-permute-start(f32[2,64,128]{2,1,0:T(8,128)S(1)} %bitcast_add_fusion.1), channel_id=1, source_target_pairs={{0,4},{1,5},{2,6},{3,7},{4,0},{5,1},{6,2},{7,3},{8,12},{9,13},{10,... | collective-permute-start | bytes 196616 | tf_op jit(solution)/shard_map/ppermute | solution.py:37
  91.8 4.9 %collective-permute-start.24 = (f32[128,256]{1,0:T(8,128)S(1)}, f32[128,256]{1,0:T(8,128)S(1)}, u32[]{:S(2)}, u32[]{:S(2)}) collective-permute-start(f32[128,256]{1,0:T(8,128)S(1)} %maximum_add_fusion.1), channel_id=1, source_target_pairs={{0,8},{4,12},{8,16},{12,20},{16,24},{20,28},{1,9},{5,13},{9,17},{1... | collective-permute-start | bytes 393224 | tf_op jit(solution)/shard_map/ppermute | solution.py:22
  (3 other events, 2.7 us)

commit v6 on v5

--- a/solution.py
+++ b/solution.py
@@ -339,8 +339,8 @@
         inner = terms[0][:data_rows] + arrived[:data_rows] * odd
         outer = terms[2][:data_rows] + arrived[:data_rows] * even
         entries = terms[0][data_rows:] + arrived[data_rows:]
+        b = paired(jnp.concatenate([inner * lower + outer * (1.0 - lower), entries]), "scan", 2, 1)
         a = paired(jnp.concatenate([outer * lower + inner * (1.0 - lower), entries]), "scan", 2, 0)
-        b = paired(jnp.concatenate([inner * lower + outer * (1.0 - lower), entries]), "scan", 2, 1)
         rows = 2 * data_rows + table_rows
         return call(
             functools.partial(join_kernel, band_cols),
@@ -351,7 +351,8 @@
         )(me, inner, outer, entries[:, LANES : 2 * LANES], a, b)
 
     def inner_update(first, third, probes, inner, outer, for_a, for_b):
-        a, b = paired(for_a, "mode", 1, 0), paired(for_b, "mode", 1, 1)
+        b = paired(for_b, "mode", 1, 1)
+        a = paired(for_a, "mode", 1, 0)
         entries = (for_a + a + b)[2 * data_rows :].astype(jnp.int32).reshape(-1)
         first, third, passed = call(
             functools.partial(inner_kernel, (scans, modes), band_cols),

time: 97.7 us -> 97.7 us (level)
  transfers between devices with their start and end apart: 31 -> 31, of which waited for: 18 -> 17; matrix products, arithmetic and copies ran while one was open for 3% -> 3% of each run, Pallas kernels for 5% -> 6%
where the time goes in v6:
time: 97.7 us; the launch traced here: 97.4 us
  starting transfers between devices  41.8 us (43%)
  waiting for transfers between devices  34.7 us (36%)
  Pallas kernels  13.7 us (14%)
  local copies, waits for them, and re-layouts  3.72 us (4%)
  between operations  1.83 us (2%)
  other arithmetic  1.68 us (2%)
    ppermute x12, waiting for transfers between devices, swapped(): lax.ppermute(value, axis, [(i, i ^ bit) for i in range(lax.axis_size(axis...  18.4 us
    ppermute x12, starting transfers between devices, swapped(): lax.ppermute(value, axis, [(i, i ^ bit) for i in range(lax.axis_size(axis...  17.7 us
    ppermute x10, starting transfers between devices, across(): lax.ppermute(value, ('scan', 'mode'), [(i, i ^ other) for i in range(scan...  13.2 us
    ppermute x10, waiting for transfers between devices, across(): lax.ppermute(value, ('scan', 'mode'), [(i, i ^ other) for i in range(scan...  11.5 us
    pallas_call x2, Pallas kernels, local(): call(wave_kernel, (*[sds(modes // 2, 2, 3 * half, length)] * 2, *[sds(row...  8.17 us
    ppermute x5, starting transfers between devices, shifted(): lax.ppermute(value, axis, [(source, source + steps) for source in range(i...  7.53 us
    ppermute x5, waiting for transfers between devices, shifted(): lax.ppermute(value, axis, [(source, source + steps) for source in range(i...  4.81 us
    ppermute x4, starting transfers between devices, paired(): lax.ppermute(value, axis, [(i, i + step) for i in lower] + [(i + step, i)...  3.35 us
  transfers between devices with their start and end apart: 31, of which 17 were waited for; matrix products, arithmetic and copies ran while one was open for 3% of the time, Pallas kernels for 6%

profile of v6, /device:TPU:0, one launch (start us, length us, event | category | flops | bytes accessed | tf_op | source)
XLA Modules:
  0.0 97.4 jit_solution(10216847707231145806)
XLA Ops:
  0.6 1.3 %collective-permute-start = (f32[2,64,256]{2,1,0:T(8,128)}, f32[2,64,256]{2,1,0:T(8,128)S(1)}, u32[]{:S(2)}, u32[]{:S(2)}) collective-permute-start(f32[2,64,256]{2,1,0:T(8,128)} %param.6), channel_id=1, source_target_pairs={{4,0},{8,4},{12,8},{16,12},{20,16},{24,20},{28,24},{5,1},{9,5},{13... | collective-permute-start | bytes 393224 | tf_op jit(solution)/shard_map/ppermute | solution.py:22
  1.9 1.3 %collective-permute-start.1 = (f32[2,64,256]{2,1,0:T(8,128)}, f32[2,64,256]{2,1,0:T(8,128)S(1)}, u32[]{:S(2)}, u32[]{:S(2)}) collective-permute-start(f32[2,64,256]{2,1,0:T(8,128)} %param.6), channel_id=1, source_target_pairs={{8,0},{12,4},{16,8},{20,12},{24,16},{28,20},{9,1},{13,5},{17,9},{2... | collective-permute-start | bytes 393224 | tf_op jit(solution)/shard_map/ppermute | solution.py:22
  4.2 3.0 %collective-permute-start.3 = (f32[1,2,2,64,128]{4,3,2,1,0:T(8,128)S(1)}, f32[1,2,2,64,128]{4,3,2,1,0:T(8,128)S(1)}, u32[]{:S(2)}, u32[]{:S(2)}) collective-permute-start(f32[1,2,2,64,128]{4,3,2,1,0:T(8,128)S(1)} %reverse_select_fusion.1), channel_id=1, source_target_pairs={{0,2},{1,3},{2,0},{3,1},{4,6},{5,7},{6,4},{7,5},{8,10},{9,11},{10,... | collective-permute-start | bytes 393224 | tf_op jit(solution)/shard_map/ppermute | solution.py:26
  9.1 1.6 %collective-permute-done.3 = f32[1,2,2,64,128]{4,3,2,1,0:T(8,128)S(1)} collective-permute-done((f32[1,2,2,64,128]{4,3,2,1,0:T(8,128)S(1)}, f32[1,2,2,64,128]{4,3,2,1,0:T(8,128)S(1)}, u32[]{:S(2)}, u32[]{:S(2)}) %collective-permute-start.3) | collective-permute-done | bytes 131104 | tf_op jit(solution)/shard_map/ppermute | solution.py:26
  10.8 2.4 %collective-permute-done.1 = f32[2,64,256]{2,1,0:T(8,128)S(1)} collective-permute-done((f32[2,64,256]{2,1,0:T(8,128)}, f32[2,64,256]{2,1,0:T(8,128)S(1)}, u32[]{:S(2)}, u32[]{:S(2)}) %collective-permute-start.1) | collective-permute-done | bytes 131104 | tf_op jit(solution)/shard_map/ppermute | solution.py:22
  13.2 1.3 %collective-permute-start.2 = (f32[2,192,128]{2,1,0:T(8,128)S(1)}, f32[2,192,128]{2,1,0:T(8,128)S(1)}, u32[]{:S(2)}, u32[]{:S(2)}) collective-permute-start(f32[2,192,128]{2,1,0:T(8,128)S(1)} %slice.165), channel_id=1, source_target_pairs={{1,0},{2,1},{3,2},{5,4},{6,5},{7,6},{9,8},{10,9},{11,10},{13,12},{... | collective-permute-start | bytes 589832 | tf_op jit(solution)/shard_map/ppermute | solution.py:22
  14.7 1.9 %collective-permute-done.2 = f32[2,192,128]{2,1,0:T(8,128)S(1)} collective-permute-done((f32[2,192,128]{2,1,0:T(8,128)S(1)}, f32[2,192,128]{2,1,0:T(8,128)S(1)}, u32[]{:S(2)}, u32[]{:S(2)}) %collective-permute-start.2) | collective-permute-done | bytes 196640 | tf_op jit(solution)/shard_map/ppermute | solution.py:22
  18.4 4.1 %shard_map.78 = (f32[2,2,192,128]{3,2,1,0:T(8,128)S(1)}, f32[2,2,192,128]{3,2,1,0:T(8,128)S(1)}, f32[136,384]{1,0:T(8,128)S(1)}, f32[136,384]{1,0:T(8,128)S(1)}, f32[136,384]{1,0:T(8,128)S(1)}) custom-call(s32[6]{0:T(128)S(1)} %reshape.96.place, s32[2]{0:T(128)S(1)} %pad_add_fusion.2.me, f32[2,2,128,128]{3,2,1,0:T(8,128)S(1)} %get-tuple-element.29.patch, ...), custom_call_target="tpu_custom_call" | custom-call | flops 1610612736 | bytes 4194304 | tf_op jit(solution)/shard_map/pallas_call | solution.py:407
  22.6 3.9 %collective-permute-start.11 = (f32[2,2,192,128]{3,2,1,0:T(8,128)S(1)}, f32[2,2,192,128]{3,2,1,0:T(8,128)S(1)}, u32[]{:S(2)}, u32[]{:S(2)}) collective-permute-start(f32[2,2,192,128]{3,2,1,0:T(8,128)S(1)} %get-tuple-element.45), channel_id=1, source_target_pairs={{0,1},{1,0},{2,3},{3,2},{4,5},{5,4},{6,7},{7,6},{8,9},{9,8},{10,11... | collective-permute-start | bytes 1179656 | tf_op jit(solution)/shard_map/ppermute | solution.py:26
  26.5 1.9 %collective-permute-done.5 = f32[136,384]{1,0:T(8,128)S(1)} collective-permute-done((f32[136,384]{1,0:T(8,128)S(1)}, f32[136,384]{1,0:T(8,128)S(1)}, u32[]{:S(2)}, u32[]{:S(2)}) %collective-permute-start.5) | collective-permute-done | bytes 208928 | tf_op jit(solution)/shard_map/ppermute | solution.py:26
  28.5 1.9 %collective-permute-start.6 = (f32[136,384]{1,0:T(8,128)S(1)}, f32[136,384]{1,0:T(8,128)S(1)}, u32[]{:S(2)}, u32[]{:S(2)}) collective-permute-start(f32[136,384]{1,0:T(8,128)S(1)} %get-tuple-element.79), channel_id=1, source_target_pairs={{0,8},{4,12},{16,24},{20,28},{8,0},{12,4},{24,16},{28,20},{1,9},{5... | collective-permute-start | bytes 626696 | tf_op jit(solution)/shard_map/ppermute | solution.py:31
  31.9 3.9 %collective-permute-start.13 = (f32[192,128]{1,0:T(8,128)S(1)}, f32[192,128]{1,0:T(8,128)S(1)}, u32[]{:S(2)}, u32[]{:S(2)}) collective-permute-start(f32[192,128]{1,0:T(8,128)S(1)} %get-tuple-element.67), channel_id=1, source_target_pairs={{0,2},{1,3},{2,0},{3,1},{4,6},{5,7},{6,4},{7,5},{8,10},{9,11},{10,... | collective-permute-start | bytes 294920 | tf_op jit(solution)/shard_map/ppermute | solution.py:37
  38.1 1.3 %collective-permute-done.13 = f32[192,128]{1,0:T(8,128)S(1)} collective-permute-done((f32[192,128]{1,0:T(8,128)S(1)}, f32[192,128]{1,0:T(8,128)S(1)}, u32[]{:S(2)}, u32[]{:S(2)}) %collective-permute-start.13) | collective-permute-done | bytes 98336 | tf_op jit(solution)/shard_map/ppermute | solution.py:37
  39.3 2.7 %collective-permute-done.14 = f32[192,128]{1,0:T(8,128)S(1)} collective-permute-done((f32[192,128]{1,0:T(8,128)S(1)}, f32[192,128]{1,0:T(8,128)S(1)}, u32[]{:S(2)}, u32[]{:S(2)}) %collective-permute-start.14) | collective-permute-done | bytes 98336 | tf_op jit(solution)/shard_map/ppermute | solution.py:37
  42.0 4.6 %collective-permute-start.15 = (f32[192,128]{1,0:T(8,128)S(1)}, f32[192,128]{1,0:T(8,128)S(1)}, u32[]{:S(2)}, u32[]{:S(2)}) collective-permute-start(f32[192,128]{1,0:T(8,128)S(1)} %fusion.7), channel_id=1, source_target_pairs={{0,8},{4,12},{8,0},{12,4},{16,24},{20,28},{24,16},{28,20},{1,9},{5... | collective-permute-start | bytes 294920 | tf_op jit(solution)/shard_map/ppermute | solution.py:26
  46.6 2.8 %collective-permute-done.15 = f32[192,128]{1,0:T(8,128)S(1)} collective-permute-done((f32[192,128]{1,0:T(8,128)S(1)}, f32[192,128]{1,0:T(8,128)S(1)}, u32[]{:S(2)}, u32[]{:S(2)}) %collective-permute-start.15) | collective-permute-done | bytes 98336 | tf_op jit(solution)/shard_map/ppermute | solution.py:26
  49.4 2.1 %collective-permute-start.16 = (f32[192,128]{1,0:T(8,128)S(1)}, f32[192,128]{1,0:T(8,128)S(1)}, u32[]{:S(2)}, u32[]{:S(2)}) collective-permute-start(f32[192,128]{1,0:T(8,128)S(1)} %add.136), channel_id=1, source_target_pairs={{0,16},{4,20},{8,24},{12,28},{16,0},{20,4},{24,8},{28,12},{1,17},{... | collective-permute-start | bytes 294920 | tf_op jit(solution)/shard_map/ppermute | solution.py:26
  51.6 2.1 %shard_map.80 = (f32[2,64,384]{2,1,0:T(8,128)S(1)}, f32[2,64,384]{2,1,0:T(8,128)S(1)}, f32[2,64,384]{2,1,0:T(8,128)S(1)}) custom-call(s32[1024]{0:T(1024)S(1)} %fusion.11.table, s32[2]{0:T(128)S(1)} %pad_add_fusion.2.me, f32[2,64,384]{2,1,0:T(8,128)S(1)} %get-tuple-element.61.first, f32[2,64,384]{2,1,0:T(8,128)S(1)} %get-tuple-element.59.third, ...), custom_call_target="tpu_custom_call" | custom-call | flops 1048576 | bytes 1048576 | tf_op jit(solution)/shard_map/pallas_call | solution.py:357
  53.7 1.2 %collective-permute-start.10 = (f32[2,64,384]{2,1,0:T(8,128)S(1)}, f32[2,64,384]{2,1,0:T(8,128)S(1)}, u32[]{:S(2)}, u32[]{:S(2)}) collective-permute-start(f32[2,64,384]{2,1,0:T(8,128)S(1)} %get-tuple-element.40), channel_id=1, source_target_pairs={{0,4},{4,0},{8,12},{12,8},{16,20},{20,16},{24,28},{28,24},{1,5},{5... | collective-permute-start | bytes 589832 | tf_op jit(solution)/shard_map/ppermute | solution.py:26
  54.9 2.1 %collective-permute-done.16 = f32[192,128]{1,0:T(8,128)S(1)} collective-permute-done((f32[192,128]{1,0:T(8,128)S(1)}, f32[192,128]{1,0:T(8,128)S(1)}, u32[]{:S(2)}, u32[]{:S(2)}) %collective-permute-start.16) | collective-permute-done | bytes 98336 | tf_op jit(solution)/shard_map/ppermute | solution.py:26
  57.8 2.8 %collective-permute-start.19 = (f32[2,64,128]{2,1,0:T(8,128)S(1)}, f32[2,64,128]{2,1,0:T(8,128)S(1)}, u32[]{:S(2)}, u32[]{:S(2)}) collective-permute-start(f32[2,64,128]{2,1,0:T(8,128)S(1)} %bitcast_add_fusion.3), channel_id=1, source_target_pairs={{0,6},{1,7},{2,4},{3,5},{4,2},{5,3},{6,0},{7,1},{8,14},{9,15},{10,... | collective-permute-start | bytes 196616 | tf_op jit(solution)/shard_map/ppermute | solution.py:37
  60.6 3.1 %collective-permute-done.17 = f32[2,64,128]{2,1,0:T(8,128)S(1)} collective-permute-done((f32[2,64,128]{2,1,0:T(8,128)S(1)}, f32[2,64,128]{2,1,0:T(8,128)S(1)}, u32[]{:S(2)}, u32[]{:S(2)}) %collective-permute-start.17) | collective-permute-done | bytes 65568 | tf_op jit(solution)/shard_map/ppermute | solution.py:37
  65.4 4.1 %shard_map.82 = (f32[2,2,192,128]{3,2,1,0:T(8,128)S(1)}, f32[2,2,192,128]{3,2,1,0:T(8,128)S(1)}, f32[136,384]{1,0:T(8,128)S(1)}, f32[136,384]{1,0:T(8,128)S(1)}, f32[136,384]{1,0:T(8,128)S(1)}) custom-call(s32[6]{0:T(128)S(1)} %reshape.96.place, s32[2]{0:T(128)S(1)} %pad_add_fusion.2.me, f32[2,2,128,128]{3,2,1,0:T(8,128)S(1)} %get-tuple-element.42.patch, ...), custom_call_target="tpu_custom_call" | custom-call | flops 1610612736 | bytes 4194304 | tf_op jit(solution)/shard_map/pallas_call | solution.py:407
  69.7 1.6 %collective-permute-done.21 = f32[2,2,192,128]{3,2,1,0:T(8,128)S(1)} collective-permute-done((f32[2,2,192,128]{3,2,1,0:T(8,128)S(1)}, f32[2,2,192,128]{3,2,1,0:T(8,128)S(1)}, u32[]{:S(2)}, u32[]{:S(2)}) %collective-permute-start.21) | collective-permute-done | bytes 393248 | tf_op jit(solution)/shard_map/ppermute | solution.py:26
  72.4 1.6 %collective-permute-start.26 = (f32[192,128]{1,0:T(8,128)S(1)}, f32[192,128]{1,0:T(8,128)S(1)}, u32[]{:S(2)}, u32[]{:S(2)}) collective-permute-start(f32[192,128]{1,0:T(8,128)S(1)} %get-tuple-element.64), channel_id=1, source_target_pairs={{0,2},{1,3},{2,0},{3,1},{4,6},{5,7},{6,4},{7,5},{8,10},{9,11},{10,... | collective-permute-start | bytes 294920 | tf_op jit(solution)/shard_map/ppermute | solution.py:37
  75.0 1.3 %collective-permute-start.22 = (f32[384,128]{1,0:T(8,128)S(1)}, f32[384,128]{1,0:T(8,128)S(1)}, u32[]{:S(2)}, u32[]{:S(2)}) collective-permute-start(f32[384,128]{1,0:T(8,128)S(1)} %pad_maximum_fusion.5), channel_id=1, source_target_pairs={{0,1},{1,2},{2,3},{4,5},{5,6},{6,7},{8,9},{9,10},{10,11},{12,13},{... | collective-permute-start | bytes 589832 | tf_op jit(solution)/shard_map/ppermute | solution.py:22
  76.3 1.6 %collective-permute-done.26 = f32[192,128]{1,0:T(8,128)S(1)} collective-permute-done((f32[192,128]{1,0:T(8,128)S(1)}, f32[192,128]{1,0:T(8,128)S(1)}, u32[]{:S(2)}, u32[]{:S(2)}) %collective-permute-start.26) | collective-permute-done | bytes 98336 | tf_op jit(solution)/shard_map/ppermute | solution.py:37
  77.9 1.8 %collective-permute-done.27 = f32[192,128]{1,0:T(8,128)S(1)} collective-permute-done((f32[192,128]{1,0:T(8,128)S(1)}, f32[192,128]{1,0:T(8,128)S(1)}, u32[]{:S(2)}, u32[]{:S(2)}) %collective-permute-start.27) | collective-permute-done | bytes 98336 | tf_op jit(solution)/shard_map/ppermute | solution.py:37
  81.4 3.0 %collective-permute-done.28 = f32[192,128]{1,0:T(8,128)S(1)} collective-permute-done((f32[192,128]{1,0:T(8,128)S(1)}, f32[192,128]{1,0:T(8,128)S(1)}, u32[]{:S(2)}, u32[]{:S(2)}) %collective-permute-start.28) | collective-permute-done | bytes 98336 | tf_op jit(solution)/shard_map/ppermute | solution.py:26
  86.3 4.7 %collective-permute-done.29 = f32[192,128]{1,0:T(8,128)S(1)} collective-permute-done((f32[192,128]{1,0:T(8,128)S(1)}, f32[192,128]{1,0:T(8,128)S(1)}, u32[]{:S(2)}, u32[]{:S(2)}) %collective-permute-start.29) | collective-permute-done | bytes 98336 | tf_op jit(solution)/shard_map/ppermute | solution.py:26
  91.8 2.4 %collective-permute-start.24 = (f32[128,256]{1,0:T(8,128)S(1)}, f32[128,256]{1,0:T(8,128)S(1)}, u32[]{:S(2)}, u32[]{:S(2)}) collective-permute-start(f32[128,256]{1,0:T(8,128)S(1)} %maximum_add_fusion.1), channel_id=1, source_target_pairs={{0,8},{4,12},{8,16},{12,20},{16,24},{20,28},{1,9},{5,13},{9,17},{1... | collective-permute-start | bytes 393224 | tf_op jit(solution)/shard_map/ppermute | solution.py:22
  94.2 1.2 %collective-permute-done.30 = f32[2,64,128]{2,1,0:T(8,128)S(1)} collective-permute-done((f32[2,64,128]{2,1,0:T(8,128)S(1)}, f32[2,64,128]{2,1,0:T(8,128)S(1)}, u32[]{:S(2)}, u32[]{:S(2)}) %collective-permute-start.30) | collective-permute-done | bytes 65568 | tf_op jit(solution)/shard_map/ppermute | solution.py:37
  (110 shorter events, 19.4 us)
Async XLA Ops:
  0.6 10.2 %collective-permute-start = (f32[2,64,256]{2,1,0:T(8,128)}, f32[2,64,256]{2,1,0:T(8,128)S(1)}, u32[]{:S(2)}, u32[]{:S(2)}) collective-permute-start(f32[2,64,256]{2,1,0:T(8,128)} %param.6), channel_id=1, source_target_pairs={{4,0},{8,4},{12,8},{16,12},{20,16},{24,20},{28,24},{5,1},{9,5},{13... | collective-permute-start | bytes 393224 | tf_op jit(solution)/shard_map/ppermute | solution.py:22
  1.9 11.3 %collective-permute-start.1 = (f32[2,64,256]{2,1,0:T(8,128)}, f32[2,64,256]{2,1,0:T(8,128)S(1)}, u32[]{:S(2)}, u32[]{:S(2)}) collective-permute-start(f32[2,64,256]{2,1,0:T(8,128)} %param.6), channel_id=1, source_target_pairs={{8,0},{12,4},{16,8},{20,12},{24,16},{28,20},{9,1},{13,5},{17,9},{2... | collective-permute-start | bytes 393224 | tf_op jit(solution)/shard_map/ppermute | solution.py:22
  4.2 4.9 %copy-start.2 = (f32[2,64,256]{2,1,0:T(8,128)S(1)}, f32[2,64,256]{2,1,0:T(8,128)}, u32[]{:S(2)}) copy-start(f32[2,64,256]{2,1,0:T(8,128)} %param.6) | copy-start | bytes 393220
  4.2 6.5 %collective-permute-start.3 = (f32[1,2,2,64,128]{4,3,2,1,0:T(8,128)S(1)}, f32[1,2,2,64,128]{4,3,2,1,0:T(8,128)S(1)}, u32[]{:S(2)}, u32[]{:S(2)}) collective-permute-start(f32[1,2,2,64,128]{4,3,2,1,0:T(8,128)S(1)} %reverse_select_fusion.1), channel_id=1, source_target_pairs={{0,2},{1,3},{2,0},{3,1},{4,6},{5,7},{6,4},{7,5},{8,10},{9,11},{10,... | collective-permute-start | bytes 393224 | tf_op jit(solution)/shard_map/ppermute | solution.py:26
  10.7 6.7 %collective-permute-start.4 = (f32[2,2,2,64,128]{4,3,2,1,0:T(8,128)S(1)}, f32[2,2,2,64,128]{4,3,2,1,0:T(8,128)S(1)}, u32[]{:S(2)}, u32[]{:S(2)}) collective-permute-start(f32[2,2,2,64,128]{4,3,2,1,0:T(8,128)S(1)} %pad_maximum_fusion.3), channel_id=1, source_target_pairs={{0,1},{1,0},{2,3},{3,2},{4,5},{5,4},{6,7},{7,6},{8,9},{9,8},{10,11... | collective-permute-start | bytes 786440 | tf_op jit(solution)/shard_map/ppermute | solution.py:26
  13.2 3.3 %collective-permute-start.2 = (f32[2,192,128]{2,1,0:T(8,128)S(1)}, f32[2,192,128]{2,1,0:T(8,128)S(1)}, u32[]{:S(2)}, u32[]{:S(2)}) collective-permute-start(f32[2,192,128]{2,1,0:T(8,128)S(1)} %slice.165), channel_id=1, source_target_pairs={{1,0},{2,1},{3,2},{5,4},{6,5},{7,6},{9,8},{10,9},{11,10},{13,12},{... | collective-permute-start | bytes 589832 | tf_op jit(solution)/shard_map/ppermute | solution.py:22
  22.5 5.9 %collective-permute-start.5 = (f32[136,384]{1,0:T(8,128)S(1)}, f32[136,384]{1,0:T(8,128)S(1)}, u32[]{:S(2)}, u32[]{:S(2)}) collective-permute-start(f32[136,384]{1,0:T(8,128)S(1)} %get-tuple-element.33), channel_id=1, source_target_pairs={{0,4},{4,0},{8,12},{12,8},{16,20},{20,16},{24,28},{28,24},{1,5},{5... | collective-permute-start | bytes 626696 | tf_op jit(solution)/shard_map/ppermute | solution.py:26
  22.6 8.5 %collective-permute-start.11 = (f32[2,2,192,128]{3,2,1,0:T(8,128)S(1)}, f32[2,2,192,128]{3,2,1,0:T(8,128)S(1)}, u32[]{:S(2)}, u32[]{:S(2)}) collective-permute-start(f32[2,2,192,128]{3,2,1,0:T(8,128)S(1)} %get-tuple-element.45), channel_id=1, source_target_pairs={{0,1},{1,0},{2,3},{3,2},{4,5},{5,4},{6,7},{7,6},{8,9},{9,8},{10,11... | collective-permute-start | bytes 1179656 | tf_op jit(solution)/shard_map/ppermute | solution.py:26
  28.5 8.1 %collective-permute-start.6 = (f32[136,384]{1,0:T(8,128)S(1)}, f32[136,384]{1,0:T(8,128)S(1)}, u32[]{:S(2)}, u32[]{:S(2)}) collective-permute-start(f32[136,384]{1,0:T(8,128)S(1)} %get-tuple-element.79), channel_id=1, source_target_pairs={{0,8},{4,12},{16,24},{20,28},{8,0},{12,4},{24,16},{28,20},{1,9},{5... | collective-permute-start | bytes 626696 | tf_op jit(solution)/shard_map/ppermute | solution.py:31
  30.4 6.2 %collective-permute-start.7 = (f32[136,384]{1,0:T(8,128)S(1)}, f32[136,384]{1,0:T(8,128)S(1)}, u32[]{:S(2)}, u32[]{:S(2)}) collective-permute-start(f32[136,384]{1,0:T(8,128)S(1)} %get-tuple-element.78), channel_id=1, source_target_pairs={{8,16},{12,20},{16,8},{20,12},{9,17},{13,21},{17,9},{21,13},{10,18... | collective-permute-start | bytes 626696 | tf_op jit(solution)/shard_map/ppermute | solution.py:31
  31.2 6.8 %collective-permute-start.12 = (f32[192,128]{1,0:T(8,128)S(1)}, f32[192,128]{1,0:T(8,128)S(1)}, u32[]{:S(2)}, u32[]{:S(2)}) collective-permute-start(f32[192,128]{1,0:T(8,128)S(1)} %get-tuple-element.65), channel_id=1, source_target_pairs={{0,4},{1,5},{2,6},{3,7},{4,0},{5,1},{6,2},{7,3},{8,12},{9,13},{10,... | collective-permute-start | bytes 294920 | tf_op jit(solution)/shard_map/ppermute | solution.py:37
  31.9 7.4 %collective-permute-start.13 = (f32[192,128]{1,0:T(8,128)S(1)}, f32[192,128]{1,0:T(8,128)S(1)}, u32[]{:S(2)}, u32[]{:S(2)}) collective-permute-start(f32[192,128]{1,0:T(8,128)S(1)} %get-tuple-element.67), channel_id=1, source_target_pairs={{0,2},{1,3},{2,0},{3,1},{4,6},{5,7},{6,4},{7,5},{8,10},{9,11},{10,... | collective-permute-start | bytes 294920 | tf_op jit(solution)/shard_map/ppermute | solution.py:37
  35.8 6.2 %collective-permute-start.14 = (f32[192,128]{1,0:T(8,128)S(1)}, f32[192,128]{1,0:T(8,128)S(1)}, u32[]{:S(2)}, u32[]{:S(2)}) collective-permute-start(f32[192,128]{1,0:T(8,128)S(1)} %get-tuple-element.66), channel_id=1, source_target_pairs={{0,6},{1,7},{2,4},{3,5},{4,2},{5,3},{6,0},{7,1},{8,14},{9,15},{10,... | collective-permute-start | bytes 294920 | tf_op jit(solution)/shard_map/ppermute | solution.py:37
  37.3 14.3 %collective-permute-start.8 = (f32[264,128]{1,0:T(8,128)S(1)}, f32[264,128]{1,0:T(8,128)S(1)}, u32[]{:S(2)}, u32[]{:S(2)}) collective-permute-start(f32[264,128]{1,0:T(8,128)S(1)} %get-tuple-element.35), channel_id=1, source_target_pairs={{0,1},{2,3},{1,0},{3,2},{4,5},{6,7},{5,4},{7,6},{8,9},{10,11},{9,8... | collective-permute-start | bytes 405512 | tf_op jit(solution)/shard_map/ppermute | solution.py:31
  37.4 14.2 %collective-permute-start.9 = (f32[264,128]{1,0:T(8,128)S(1)}, f32[264,128]{1,0:T(8,128)S(1)}, u32[]{:S(2)}, u32[]{:S(2)}) collective-permute-start(f32[264,128]{1,0:T(8,128)S(1)} %get-tuple-element.36), channel_id=1, source_target_pairs={{1,2},{2,1},{5,6},{6,5},{9,10},{10,9},{13,14},{14,13},{17,18},{18,... | collective-permute-start | bytes 405512 | tf_op jit(solution)/shard_map/ppermute | solution.py:31
  42.0 7.4 %collective-permute-start.15 = (f32[192,128]{1,0:T(8,128)S(1)}, f32[192,128]{1,0:T(8,128)S(1)}, u32[]{:S(2)}, u32[]{:S(2)}) collective-permute-start(f32[192,128]{1,0:T(8,128)S(1)} %fusion.7), channel_id=1, source_target_pairs={{0,8},{4,12},{8,0},{12,4},{16,24},{20,28},{24,16},{28,20},{1,9},{5... | collective-permute-start | bytes 294920 | tf_op jit(solution)/shard_map/ppermute | solution.py:26
  49.4 7.5 %collective-permute-start.16 = (f32[192,128]{1,0:T(8,128)S(1)}, f32[192,128]{1,0:T(8,128)S(1)}, u32[]{:S(2)}, u32[]{:S(2)}) collective-permute-start(f32[192,128]{1,0:T(8,128)S(1)} %add.136), channel_id=1, source_target_pairs={{0,16},{4,20},{8,24},{12,28},{16,0},{20,4},{24,8},{28,12},{1,17},{... | collective-permute-start | bytes 294920 | tf_op jit(solution)/shard_map/ppermute | solution.py:26
  53.7 10.0 %collective-permute-start.10 = (f32[2,64,384]{2,1,0:T(8,128)S(1)}, f32[2,64,384]{2,1,0:T(8,128)S(1)}, u32[]{:S(2)}, u32[]{:S(2)}) collective-permute-start(f32[2,64,384]{2,1,0:T(8,128)S(1)} %get-tuple-element.40), channel_id=1, source_target_pairs={{0,4},{4,0},{8,12},{12,8},{16,20},{20,16},{24,28},{28,24},{1,5},{5... | collective-permute-start | bytes 589832 | tf_op jit(solution)/shard_map/ppermute | solution.py:26
  57.1 6.6 %collective-permute-start.17 = (f32[2,64,128]{2,1,0:T(8,128)S(1)}, f32[2,64,128]{2,1,0:T(8,128)S(1)}, u32[]{:S(2)}, u32[]{:S(2)}) collective-permute-start(f32[2,64,128]{2,1,0:T(8,128)S(1)} %bitcast_add_fusion.3), channel_id=1, source_target_pairs={{0,4},{1,5},{2,6},{3,7},{4,0},{5,1},{6,2},{7,3},{8,12},{9,13},{10,... | collective-permute-start | bytes 196616 | tf_op jit(solution)/shard_map/ppermute | solution.py:37
  57.8 5.9 %collective-permute-start.18 = (f32[2,64,128]{2,1,0:T(8,128)S(1)}, f32[2,64,128]{2,1,0:T(8,128)S(1)}, u32[]{:S(2)}, u32[]{:S(2)}) collective-permute-start(f32[2,64,128]{2,1,0:T(8,128)S(1)} %bitcast_add_fusion.3), channel_id=1, source_target_pairs={{0,2},{1,3},{2,0},{3,1},{4,6},{5,7},{6,4},{7,5},{8,10},{9,11},{10,... | collective-permute-start | bytes 196616 | tf_op jit(solution)/shard_map/ppermute | solution.py:37
  57.8 5.9 %collective-permute-start.19 = (f32[2,64,128]{2,1,0:T(8,128)S(1)}, f32[2,64,128]{2,1,0:T(8,128)S(1)}, u32[]{:S(2)}, u32[]{:S(2)}) collective-permute-start(f32[2,64,128]{2,1,0:T(8,128)S(1)} %bitcast_add_fusion.3), channel_id=1, source_target_pairs={{0,6},{1,7},{2,4},{3,5},{4,2},{5,3},{6,0},{7,1},{8,14},{9,15},{10,... | collective-permute-start | bytes 196616 | tf_op jit(solution)/shard_map/ppermute | solution.py:37
  63.8 1.6 %collective-permute-start.20 = (f32[2,2,2,64,128]{4,3,2,1,0:T(8,128)S(1)}, f32[2,2,2,64,128]{4,3,2,1,0:T(8,128)S(1)}, u32[]{:S(2)}, u32[]{:S(2)}) collective-permute-start(f32[2,2,2,64,128]{4,3,2,1,0:T(8,128)S(1)} %pad_maximum_fusion.4), channel_id=1, source_target_pairs={{0,1},{1,0},{2,3},{3,2},{4,5},{5,4},{6,7},{7,6},{8,9},{9,8},{10,11... | collective-permute-start | bytes 786440 | tf_op jit(solution)/shard_map/ppermute | solution.py:26
  69.5 1.8 %collective-permute-start.21 = (f32[2,2,192,128]{3,2,1,0:T(8,128)S(1)}, f32[2,2,192,128]{3,2,1,0:T(8,128)S(1)}, u32[]{:S(2)}, u32[]{:S(2)}) collective-permute-start(f32[2,2,192,128]{3,2,1,0:T(8,128)S(1)} %get-tuple-element.48), channel_id=1, source_target_pairs={{0,1},{1,0},{2,3},{3,2},{4,5},{5,4},{6,7},{7,6},{8,9},{9,8},{10,11... | collective-permute-start | bytes 1179656 | tf_op jit(solution)/shard_map/ppermute | solution.py:26
  71.4 4.9 %collective-permute-start.25 = (f32[192,128]{1,0:T(8,128)S(1)}, f32[192,128]{1,0:T(8,128)S(1)}, u32[]{:S(2)}, u32[]{:S(2)}) collective-permute-start(f32[192,128]{1,0:T(8,128)S(1)} %get-tuple-element.62), channel_id=1, source_target_pairs={{0,4},{1,5},{2,6},{3,7},{4,0},{5,1},{6,2},{7,3},{8,12},{9,13},{10,... | collective-permute-start | bytes 294920 | tf_op jit(solution)/shard_map/ppermute | solution.py:37
  72.4 5.4 %collective-permute-start.26 = (f32[192,128]{1,0:T(8,128)S(1)}, f32[192,128]{1,0:T(8,128)S(1)}, u32[]{:S(2)}, u32[]{:S(2)}) collective-permute-start(f32[192,128]{1,0:T(8,128)S(1)} %get-tuple-element.64), channel_id=1, source_target_pairs={{0,2},{1,3},{2,0},{3,1},{4,6},{5,7},{6,4},{7,5},{8,10},{9,11},{10,... | collective-permute-start | bytes 294920 | tf_op jit(solution)/shard_map/ppermute | solution.py:37
  74.0 5.6 %collective-permute-start.27 = (f32[192,128]{1,0:T(8,128)S(1)}, f32[192,128]{1,0:T(8,128)S(1)}, u32[]{:S(2)}, u32[]{:S(2)}) collective-permute-start(f32[192,128]{1,0:T(8,128)S(1)} %get-tuple-element.63), channel_id=1, source_target_pairs={{0,6},{1,7},{2,4},{3,5},{4,2},{5,3},{6,0},{7,1},{8,14},{9,15},{10,... | collective-permute-start | bytes 294920 | tf_op jit(solution)/shard_map/ppermute | solution.py:37
  75.0 10.2 %collective-permute-start.22 = (f32[384,128]{1,0:T(8,128)S(1)}, f32[384,128]{1,0:T(8,128)S(1)}, u32[]{:S(2)}, u32[]{:S(2)}) collective-permute-start(f32[384,128]{1,0:T(8,128)S(1)} %pad_maximum_fusion.5), channel_id=1, source_target_pairs={{0,1},{1,2},{2,3},{4,5},{5,6},{6,7},{8,9},{9,10},{10,11},{12,13},{... | collective-permute-start | bytes 589832 | tf_op jit(solution)/shard_map/ppermute | solution.py:22
  79.7 4.7 %collective-permute-start.28 = (f32[192,128]{1,0:T(8,128)S(1)}, f32[192,128]{1,0:T(8,128)S(1)}, u32[]{:S(2)}, u32[]{:S(2)}) collective-permute-start(f32[192,128]{1,0:T(8,128)S(1)} %fusion.9), channel_id=1, source_target_pairs={{0,8},{4,12},{8,0},{12,4},{16,24},{20,28},{24,16},{28,20},{1,9},{5... | collective-permute-start | bytes 294920 | tf_op jit(solution)/shard_map/ppermute | solution.py:26
  84.3 6.6 %collective-permute-start.29 = (f32[192,128]{1,0:T(8,128)S(1)}, f32[192,128]{1,0:T(8,128)S(1)}, u32[]{:S(2)}, u32[]{:S(2)}) collective-permute-start(f32[192,128]{1,0:T(8,128)S(1)} %add.152), channel_id=1, source_target_pairs={{0,16},{4,20},{8,24},{12,28},{16,0},{20,4},{24,8},{28,12},{1,17},{... | collective-permute-start | bytes 294920 | tf_op jit(solution)/shard_map/ppermute | solution.py:26
  85.2 6.6 %collective-permute-start.23 = (f32[128,256]{1,0:T(8,128)S(1)}, f32[128,256]{1,0:T(8,128)S(1)}, u32[]{:S(2)}, u32[]{:S(2)}) collective-permute-start(f32[128,256]{1,0:T(8,128)S(1)} %pad_maximum_fusion.6), channel_id=1, source_target_pairs={{0,4},{4,0},{8,12},{12,8},{16,20},{20,16},{24,28},{28,24},{1,5},{5... | collective-permute-start | bytes 393224 | tf_op jit(solution)/shard_map/ppermute | solution.py:26
  91.0 4.3 %collective-permute-start.30 = (f32[2,64,128]{2,1,0:T(8,128)S(1)}, f32[2,64,128]{2,1,0:T(8,128)S(1)}, u32[]{:S(2)}, u32[]{:S(2)}) collective-permute-start(f32[2,64,128]{2,1,0:T(8,128)S(1)} %bitcast_add_fusion.1), channel_id=1, source_target_pairs={{0,4},{1,5},{2,6},{3,7},{4,0},{5,1},{6,2},{7,3},{8,12},{9,13},{10,... | collective-permute-start | bytes 196616 | tf_op jit(solution)/shard_map/ppermute | solution.py:37
  91.8 4.9 %collective-permute-start.24 = (f32[128,256]{1,0:T(8,128)S(1)}, f32[128,256]{1,0:T(8,128)S(1)}, u32[]{:S(2)}, u32[]{:S(2)}) collective-permute-start(f32[128,256]{1,0:T(8,128)S(1)} %maximum_add_fusion.1), channel_id=1, source_target_pairs={{0,8},{4,12},{8,16},{12,20},{16,24},{20,28},{1,9},{5,13},{9,17},{1... | collective-permute-start | bytes 393224 | tf_op jit(solution)/shard_map/ppermute | solution.py:22
  (3 other events, 2.7 us)
